TPU v7x, 256 devices: a whole 4x4x8 slice. The times are simulated.
256 devices in a mesh: blk: 32 (over y_lo, z, core), rep: 8 (over y_hi, x).
Axes of the slice: x: 4, y: 4 (y_hi: 2, y_lo: 2; y = y_hi * 2 + y_lo), z: 8, core: 2. Of those that a mesh axis runs over, the one named last changes fastest.
Arguments:
- tokens: bfloat16 [32768, 4096], P(('blk', 'rep')), may hold values from -24 to 24
- cotangent: bfloat16 [32768, 4096], P(('blk', 'rep')), may hold values from -1.5 to 1.5
- gate_weight: bfloat16 [4096, 11008], P(None, 'blk'), may hold values from -0.25 to 0.25
- up_weight: bfloat16 [4096, 11008], P(None, 'blk'), may hold values from -0.25 to 0.25
- down_weight: bfloat16 [11008, 4096], P('blk'), may hold values from -0.0546875 to 0.0546875
Outputs:
- input_grad: bfloat16 [32768, 4096], P(('blk', 'rep'))
- gate_grad: bfloat16 [4096, 11008], P('rep', 'blk')
- up_grad: bfloat16 [4096, 11008], P('rep', 'blk')
- down_grad: bfloat16 [11008, 4096], P('blk', 'rep')
All inputs are finite; a program needn't handle non-finite values.
Results may differ from a plain program's by a relative error of at most 0.019.
Values may be sent and summed in bfloat16 or wider, within the bound.
No kernel may reach another device: no remote copies, remote signals or barrier semaphores. Data moves between devices by JAX's collectives and lax.ppermute only.
A program may use at most 128 MiB of HBM per device.

v0:
```python
import jax
import jax.numpy as jnp
from jax import lax
from jax.sharding import PartitionSpec as P


def shifted(value, axis, by):
    size = lax.axis_size(axis)
    return lax.ppermute(value, axis, [(i, (i + by) % size) for i in range(size)])


def contract_rows(left, right):
    return lax.dot_general(
        left, right, (((0,), (0,)), ((), ())), preferred_element_type=jnp.float32
    )


def contract_cols(left, right):
    return lax.dot_general(
        left, right, (((1,), (1,)), ((), ())), preferred_element_type=jnp.float32
    )


def shard_terms(rows, cotan, w_gate, w_up, w_down):
    gate = jnp.dot(rows, w_gate, preferred_element_type=jnp.float32)
    upval = jnp.dot(rows, w_up, preferred_element_type=jnp.float32)
    sigma = jax.nn.sigmoid(gate)
    active = gate * sigma
    slope = sigma * (1.0 + gate * (1.0 - sigma))
    hidden = (active * upval).astype(jnp.bfloat16)
    d_hidden = contract_cols(cotan, w_down)
    d_up = (d_hidden * active).astype(jnp.bfloat16)
    d_gate = (d_hidden * upval * slope).astype(jnp.bfloat16)
    term_x = contract_cols(d_gate, w_gate) + contract_cols(d_up, w_up)
    grad_gate = contract_rows(rows, d_gate).astype(jnp.bfloat16)
    grad_up = contract_rows(rows, d_up).astype(jnp.bfloat16)
    grad_down = contract_rows(cotan, hidden).astype(jnp.bfloat16)
    return (term_x, jnp.stack([grad_gate, grad_up, grad_down]))


def local(tokens, cotangent, gate_weight, up_weight, down_weight):
    own_x, own_terms = shard_terms(tokens, cotangent, gate_weight, up_weight, down_weight)
    near_gate, near_up, near_down = shifted((gate_weight, up_weight, down_weight), "blk", 1)
    near_x, near_terms = shard_terms(tokens, cotangent, near_gate, near_up, near_down)
    input_grad = (own_x + near_x).astype(jnp.bfloat16)
    returned = shifted(near_terms, "blk", -1)
    own_terms, returned = lax.optimization_barrier((own_terms, returned))
    paired = (own_terms.astype(jnp.float32) + returned.astype(jnp.float32)).astype(jnp.bfloat16)
    paired = lax.optimization_barrier(paired)
    summed = lax.psum_scatter(
        paired.astype(jnp.float32).astype(jnp.bfloat16), "rep", scatter_dimension=1, tiled=True
    )
    return (input_grad, summed[0], summed[1], summed[2].T)


def solution(mesh):
    in_specs = (
        P(("blk", "rep"), None),
        P(("blk", "rep"), None),
        P(None, "blk"),
        P(None, "blk"),
        P("blk", None),
    )
    out_specs = (P(("blk", "rep"), None), P("rep", "blk"), P("rep", "blk"), P("blk", "rep"))
    return jax.shard_map(local, mesh=mesh, in_specs=in_specs, out_specs=out_specs, check_vma=False)
```

profile of v0, /device:TPU:2, one launch (start us, length us, event | category | flops | bytes accessed | tf_op | source)
XLA Modules:
  0.0 336.2 jit_solution(17717688819293089705)
XLA Ops:
  7.3 2.0 collective-permute-start.1
  9.4 35.8 %collective-permute-done.2 = bf16[4096,344]{0,1:T(8,128)(2,1)S(1)} collective-permute-done((bf16[4096,344]{0,1:T(8,128)(2,1)}, bf16[4096,344]{0,1:T(8,128)(2,1)S(1)}, u32[]{:S(2)}, u32[]{:S(2)}) %collective-permute-start.2) | collective-permute-done | bytes 2818080 | tf_op jit(solution)/shard_map/ppermute | solution.py:9
  45.3 1.6 copy-done.5
  46.9 1.0 fusion.18
  48.0 27.5 %collective-permute-done.1 = bf16[4096,344]{0,1:T(8,128)(2,1)S(1)} collective-permute-done((bf16[4096,344]{0,1:T(8,128)(2,1)}, bf16[4096,344]{0,1:T(8,128)(2,1)S(1)}, u32[]{:S(2)}, u32[]{:S(2)}) %collective-permute-start.1) | collective-permute-done | bytes 2818080 | tf_op jit(solution)/shard_map/ppermute | solution.py:9
  75.5 1.6 copy-done.7
  77.1 0.9 fusion.17
  78.0 0.9 fusion.5
  78.9 26.7 %collective-permute-done = bf16[344,4096]{1,0:T(8,128)(2,1)S(1)} collective-permute-done((bf16[344,4096]{1,0:T(8,128)(2,1)}, bf16[344,4096]{1,0:T(8,128)(2,1)S(1)}, u32[]{:S(2)}, u32[]{:S(2)}) %collective-permute-start) | collective-permute-done | bytes 2818080 | tf_op jit(solution)/shard_map/ppermute | solution.py:9
  105.7 1.0 multiply_convert_fusion.3
  106.7 0.9 fusion.3
  107.6 0.9 fusion.4
  108.5 1.0 pad_maximum_fusion.1
  109.8 0.5 copy-done.4
  110.3 1.0 fusion.15
  111.5 0.9 fusion.14
  112.4 0.9 copy-done.10
  113.3 1.0 multiply_convert_fusion.4
  114.3 0.9 fusion.1
  115.2 0.9 fusion
  116.1 0.9 fusion.2
  117.0 1.0 pad_maximum_fusion
  118.0 83.4 %collective-permute-done.3 = bf16[3,4096,344]{1,2,0:T(8,128)(2,1)S(1)} collective-permute-done((bf16[3,4096,344]{1,2,0:T(8,128)(2,1)S(1)}, bf16[3,4096,344]{1,2,0:T(8,128)(2,1)S(1)}, u32[]{:S(2)}, u32[]{:S(2)}) %collective-permute-start.3) | collective-permute-done | bytes 8454176 | tf_op jit(solution)/shard_map/ppermute | solution.py:9
  201.4 6.0 %add_convert_fusion = bf16[3,4096,344]{1,2,0:T(8,128)(2,1)} fusion(bf16[3,4096,344]{1,2,0:T(8,128)(2,1)S(1)} %collective-permute-done.3, bf16[3,4096,344]{1,2,0:T(8,128)(2,1)S(1)} %pad_maximum_fusion), kind=kLoop, calls=%fused_computation | loop fusion | flops 16908288 | bytes 25362432 | tf_op jit(solution)/shard_map/convert_element_type | solution.py:48
  207.4 2.7 fusion.16
  210.2 0.9 convolution_add_fusion.1
  211.1 0.9 copy-done.8
  212.0 0.9 fusion.19
  212.9 0.9 copy-done.6
  213.8 1.9 fusion.7
  215.7 111.5 %reduce-scatter.2.cloned.1.call-done = bf16[3,512,344]{1,2,0:T(8,128)(2,1)} async-done(((bf16[3,4096,344]{1,2,0:T(8,128)(2,1)}), bf16[3,512,344]{1,2,0:T(8,128)(2,1)}) %reduce-scatter.2.cloned.1.call-update) | async-done | bytes 1056784 | tf_op jit(solution)/shard_map/reduce_scatter | solution.py:50
  327.2 2.2 slice_bitcast_fusion
  (21 shorter events, 0.8 us)
Async XLA Ops:
  7.2 39.8 %copy-start = (bf16[128,4096]{1,0:T(8,128)(2,1)S(1)}, bf16[128,4096]{1,0:T(8,128)(2,1)}, u32[]{:S(2)}) copy-start(bf16[128,4096]{1,0:T(8,128)(2,1)} %param.5) | copy-start | bytes 3145732
  7.2 320.0 %reduce-scatter.2.cloned.1.call-start = ((), (), s32[]{:S(2)}) async-start(), calls=%async_computation.1 | async-start | bytes 9510912 | tf_op jit(solution)/shard_map/reduce_scatter | solution.py:50
  7.2 38.0 %collective-permute-start.2 = (bf16[4096,344]{0,1:T(8,128)(2,1)}, bf16[4096,344]{0,1:T(8,128)(2,1)S(1)}, u32[]{:S(2)}, u32[]{:S(2)}) collective-permute-start(bf16[4096,344]{0,1:T(8,128)(2,1)} %param.7), channel_id=1, source_target_pairs={{0,8},{8,16},{16,24},{24,32},{32,40},{40,48},{48,56},{56,64},{64,7... | collective-permute-start | bytes 8454152 | tf_op jit(solution)/shard_map/ppermute | solution.py:9
  7.3 68.1 %collective-permute-start.1 = (bf16[4096,344]{0,1:T(8,128)(2,1)}, bf16[4096,344]{0,1:T(8,128)(2,1)S(1)}, u32[]{:S(2)}, u32[]{:S(2)}) collective-permute-start(bf16[4096,344]{0,1:T(8,128)(2,1)} %param.8), channel_id=1, source_target_pairs={{0,8},{8,16},{16,24},{24,32},{32,40},{40,48},{48,56},{56,64},{64,7... | collective-permute-start | bytes 8454152 | tf_op jit(solution)/shard_map/ppermute | solution.py:9
  9.3 96.3 %collective-permute-start = (bf16[344,4096]{1,0:T(8,128)(2,1)}, bf16[344,4096]{1,0:T(8,128)(2,1)S(1)}, u32[]{:S(2)}, u32[]{:S(2)}) collective-permute-start(bf16[344,4096]{1,0:T(8,128)(2,1)} %param.9), channel_id=1, source_target_pairs={{0,8},{8,16},{16,24},{24,32},{32,40},{40,48},{48,56},{56,64},{64,7... | collective-permute-start | bytes 8454152 | tf_op jit(solution)/shard_map/ppermute | solution.py:9
  45.3 1.6 copy-start.5
  48.0 30.1 %copy-start.9 = (bf16[128,4096]{1,0:T(8,128)(2,1)S(1)}, bf16[128,4096]{1,0:T(8,128)(2,1)}, u32[]{:S(2)}) copy-start(bf16[128,4096]{1,0:T(8,128)(2,1)} %param.6) | copy-start | bytes 3145732
  75.5 1.6 copy-start.7
  108.5 1.8 copy-start.4
  109.5 2.0 copy-start.2
  109.5 91.9 %collective-permute-start.3 = (bf16[3,4096,344]{1,2,0:T(8,128)(2,1)S(1)}, bf16[3,4096,344]{1,2,0:T(8,128)(2,1)S(1)}, u32[]{:S(2)}, u32[]{:S(2)}) collective-permute-start(bf16[3,4096,344]{1,2,0:T(8,128)(2,1)S(1)} %pad_maximum_fusion.1), channel_id=1, source_target_pairs={{0,248},{8,0},{16,8},{24,16},{32,24},{40,32},{48,40},{56,48},{64,5... | collective-permute-start | bytes 25362440 | tf_op jit(solution)/shard_map/ppermute | solution.py:9
  111.5 1.8 copy-start.10
  207.4 2.8 copy-start.3
  210.2 1.8 copy-start.8
  212.0 1.8 copy-start.6
  213.8 115.6 %copy-start.1 = (bf16[128,4096]{1,0:T(8,128)(2,1)S(1)}, bf16[128,4096]{1,0:T(8,128)(2,1)}, u32[]{:S(2)}) copy-start(bf16[128,4096]{1,0:T(8,128)(2,1)} %param.5) | copy-start | bytes 3145732
Sparse Core Ops, SparseCore 0:
  207.5 119.6 reduce-scatter.1
where the time goes:
time: 338 us; the launch traced here: 336 us
  waiting for transfers between devices  285 us (84%)
  matrix products  17.6 us (5%)
  between operations  14.2 us (4%)
  local copies, waits for them, and re-layouts  8.86 us (3%)
  other arithmetic  7.96 us (2%)
    ppermute x4, waiting for transfers between devices, shifted(): lax.ppermute(value, axis, [(i, (i + by) % size) for i in range(size)])  174 us
    reduce_scatter x1, waiting for transfers between devices, local(): lax.psum_scatter(paired.astype(jnp.float32).astype(jnp.bfloat16), 'rep',...  112 us
    dot_general x6, matrix products, contract_cols(): lax.dot_general(left, right, (((1,), (1,)), ((), ())), preferred_element_...  8.48 us
  transfers between devices with their start and end apart: 5, of which 5 were waited for; matrix products, arithmetic and copies ran while one was open for 5% of the time, Pallas kernels for 0%

commit v1 on v0

v1 whole, which is shorter than its diff:
```python
import jax
import jax.numpy as jnp
from jax import lax
from jax.sharding import PartitionSpec as P

ROW = 4


def along_blk(value, by):
    size = lax.axis_size("blk")
    return lax.ppermute(value, "blk", [(i, (i + by) % size) for i in range(size)])


def partner(r, j, i):
    return (r // ROW ^ j) * ROW + (r % ROW + i) % ROW


def along_rep(value, j, i):
    return lax.ppermute(value, "rep", [(r, partner(r, j, i)) for r in range(2 * ROW)])


def nt(left, right):
    return lax.dot_general(
        left, right, (((1,), (1,)), ((), ())), preferred_element_type=jnp.float32
    )


def tn(left, right):
    return lax.dot_general(
        left, right, (((0,), (0,)), ((), ())), preferred_element_type=jnp.float32
    )


def unit_grads(rows, cotan, w_gate, w_up, w_down):
    gate = nt(w_gate, rows)
    upval = nt(w_up, rows)
    sigma = jax.nn.sigmoid(gate)
    active = gate * sigma
    slope = sigma * (1.0 + gate * (1.0 - sigma))
    hidden = (active * upval).astype(jnp.bfloat16)
    d_hidden = nt(w_down, cotan)
    d_up = (d_hidden * active).astype(jnp.bfloat16)
    d_gate = (d_hidden * upval * slope).astype(jnp.bfloat16)
    return jnp.concatenate([d_gate, d_up, hidden])


def row_term(grads, w_gate, w_up):
    s = w_gate.shape[0]
    return tn(grads[:s], w_gate) + tn(grads[s : 2 * s], w_up)


def local(tokens, cotangent, gate_weight, up_weight, down_weight):
    w_gate, w_up, w_down = gate_weight.T, up_weight.T, down_weight
    s = w_gate.shape[0]
    far_rows = along_blk(tokens, -1)
    far_cotan = along_blk(cotangent, -1)
    me = lax.axis_index("rep")
    wide = tokens.shape[1] // (2 * ROW)

    def columns(i):
        out = []
        for j in range(2):
            to = (me // ROW ^ j) * ROW + (me % ROW + i) % ROW
            out += [lax.dynamic_slice_in_dim(a, to * wide, wide, 1) for a in (tokens, cotangent)]
        return jnp.concatenate(out, 1)

    near_cols = jnp.concatenate([columns(0)] + [along_rep(columns(i), 0, i) for i in range(1, ROW)])
    far_cols = along_blk(near_cols, -1)

    own = unit_grads(tokens, cotangent, w_gate, w_up, w_down)
    own_all = [own] + [along_rep(own, 0, i) for i in range(1, ROW)]
    own_x = row_term(own, w_gate, w_up)

    far = unit_grads(far_rows, far_cotan, w_gate, w_up, w_down)
    far_all = [far] + [along_rep(far, 0, i) for i in range(1, ROW)]
    far_x = row_term(far, w_gate, w_up).astype(jnp.bfloat16)

    grads = jnp.concatenate(own_all + far_all, 1)
    cols = jnp.concatenate([near_cols, far_cols])

    def weight_terms(first):
        pair = jnp.dot(grads[: 2 * s], cols[:, first : first + wide], preferred_element_type=jnp.float32)
        down = jnp.dot(grads[2 * s :], cols[:, first + wide : first + 2 * wide], preferred_element_type=jnp.float32)
        return pair, down

    other = jnp.concatenate([a.astype(jnp.bfloat16) for a in weight_terms(2 * wide)])
    other = along_rep(other, 1, 0).astype(jnp.float32)
    pair, down = weight_terms(0)
    pair = (pair + other[: 2 * s]).astype(jnp.bfloat16)
    down = (down + other[2 * s :]).astype(jnp.bfloat16)
    input_grad = (own_x + along_blk(far_x, 1).astype(jnp.float32)).astype(jnp.bfloat16)
    return input_grad, pair[:s].T, pair[s:].T, down


def solution(mesh):
    in_specs = (
        P(("blk", "rep"), None),
        P(("blk", "rep"), None),
        P(None, "blk"),
        P(None, "blk"),
        P("blk", None),
    )
    out_specs = (P(("blk", "rep"), None), P("rep", "blk"), P("rep", "blk"), P("blk", "rep"))
    return jax.shard_map(local, mesh=mesh, in_specs=in_specs, out_specs=out_specs, check_vma=False)
```

time: 338 us -> 110 us (0.33)
  waiting for transfers between devices: 285 us -> 55.9 us
  starting transfers between devices: 2.5 us -> 25.3 us
  between operations: 14.2 us -> 1.01 us
  other arithmetic: 7.96 us -> 4.41 us
    ppermute x4 -> x14, waiting for transfers between devices: 174 us -> 55.9 us  [the longest x10 48 us: along_rep(): lax.ppermute(value, 'rep', [(r, partner(r, j, i)) for r in range(2 * ROW)])]
    reduce_scatter x1 -> x0, waiting for transfers between devices: 112 us -> none  [local(): lax.psum_scatter(paired.astype(jnp.float32).astype(jnp.bfloat16), 'rep',...]
    ppermute x4 -> x14, starting transfers between devices: 2.46 us -> 25.3 us  [the longest x10 16.7 us: along_rep(): lax.ppermute(value, 'rep', [(r, partner(r, j, i)) for r in range(2 * ROW)])]
    convert_element_type x1, other arithmetic: 5.98 us -> 0.28 us  [local(): other = along_rep(other, 1, 0).astype(jnp.float32)]
    concatenate x0 -> x7, other arithmetic: none -> 4.09 us  [the longest x1 3.01 us: local(): jnp.concatenate([columns(0)] + [along_rep(columns(i), 0, i) for i in rang...]
    dot_general x16 -> x14, matrix products: 17.6 us -> 16.2 us  [the longest x6 8.14 us: nt(): lax.dot_general(left, right, (((1,), (1,)), ((), ())), preferred_element_...]
  transfers between devices with their start and end apart: 5 -> 14, of which waited for: 5 -> 8; matrix products, arithmetic and copies ran while one was open for 5% -> 15% of each run, Pallas kernels for 0% -> 0%
where the time goes in v1:
time: 110 us
  waiting for transfers between devices  55.9 us (51%)
  starting transfers between devices  25.3 us (23%)
  matrix products  16.2 us (15%)
  local copies, waits for them, and re-layouts  6.8 us (6%)
  other arithmetic  4.41 us (4%)
    ppermute x10, waiting for transfers between devices, along_rep(): lax.ppermute(value, 'rep', [(r, partner(r, j, i)) for r in range(2 * ROW)])  48 us
    ppermute x10, starting transfers between devices, along_rep(): lax.ppermute(value, 'rep', [(r, partner(r, j, i)) for r in range(2 * ROW)])  16.7 us
    ppermute x4, starting transfers between devices, along_blk(): lax.ppermute(value, 'blk', [(i, (i + by) % size) for i in range(size)])  8.67 us
    dot_general x6, matrix products, nt(): lax.dot_general(left, right, (((1,), (1,)), ((), ())), preferred_element_...  8.14 us
    ppermute x4, waiting for transfers between devices, along_blk(): lax.ppermute(value, 'blk', [(i, (i + by) % size) for i in range(size)])  7.87 us
    dot_general x4, matrix products, tn(): lax.dot_general(left, right, (((0,), (0,)), ((), ())), preferred_element_...  4.44 us
    unnamed x26, local copies, waits for them, and re-layouts  4.02 us
    concatenate x1, other arithmetic, local(): jnp.concatenate([columns(0)] + [along_rep(columns(i), 0, i) for i in rang...  3.01 us
  transfers between devices with their start and end apart: 14, of which 8 were waited for; matrix products, arithmetic and copies ran while one was open for 15% of the time, Pallas kernels for 0%

profile of v1, /device:TPU:2, one launch (start us, length us, event | category | flops | bytes accessed | tf_op | source)
XLA Modules:
  0.0 109.6 jit_solution(1531942143968765878)
XLA Ops:
  0.7 3.1 %fusion.14 = f32[344,128]{1,0:T(8,128)S(1)} fusion(bf16[4096,344]{0,1:T(8,128)(2,1)} %param.7, bf16[128,4096]{1,0:T(8,128)(2,1)} %param.5), kind=kOutput, calls=%fused_computation.67 | convolution fusion | flops 360710144 | bytes 4042752 | tf_op jit(solution)/shard_map/dot_general | solution.py:23
  4.0 1.0 fusion.13
  5.4 1.0 multiply_convert_fusion.1
  7.2 1.5 %collective-permute-start.3 = (bf16[1032,128]{1,0:T(8,128)(2,1)S(1)}, bf16[1032,128]{1,0:T(8,128)(2,1)}, u32[]{:S(2)}, u32[]{:S(2)}) collective-permute-start(bf16[1032,128]{1,0:T(8,128)(2,1)S(1)} %get-tuple-element.30), channel_id=1, source_target_pairs={{0,1},{1,2},{2,3},{3,0},{4,5},{5,6},{6,7},{7,4},{8,9},{9,10},{10,1... | collective-permute-start | bytes 792584 | tf_op jit(solution)/shard_map/ppermute | solution.py:19
  8.7 2.8 %collective-permute-start.4 = (bf16[1032,128]{1,0:T(8,128)(2,1)S(1)}, bf16[1032,128]{1,0:T(8,128)(2,1)}, u32[]{:S(2)}, u32[]{:S(2)}) collective-permute-start(bf16[1032,128]{1,0:T(8,128)(2,1)S(1)} %get-tuple-element.30), channel_id=1, source_target_pairs={{0,2},{1,3},{2,0},{3,1},{4,6},{5,7},{6,4},{7,5},{8,10},{9,11},{10,... | collective-permute-start | bytes 792584 | tf_op jit(solution)/shard_map/ppermute | solution.py:19
  12.0 1.5 %constant_dynamic-slice_fusion.2 = (bf16[128,512]{1,0:T(8,128)(2,1)S(1)}, bf16[128,512]{1,0:T(8,128)(2,1)S(1)}, bf16[128,512]{1,0:T(8,128)(2,1)S(1)}, bf16[128,5...) fusion(bf16[128,4096]{1,0:T(8,128)(2,1)} %param.6, ...), kind=kLoop, calls=%fused_computation.52 | loop fusion | bytes 2097184 | tf_op jit(solution)/shard_map/dynamic_slice | solution.py:64
  13.8 1.7 %collective-permute-start.9 = (bf16[128,2048]{1,0:T(8,128)(2,1)S(1)}, bf16[128,2048]{1,0:T(8,128)(2,1)S(1)}, u32[]{:S(2)}, u32[]{:S(2)}) collective-permute-start(bf16[128,2048]{1,0:T(8,128)(2,1)S(1)} %pad_maximum_fusion.2), channel_id=1, source_target_pairs={{0,1},{1,2},{2,3},{3,0},{4,5},{5,6},{6,7},{7,4},{8,9},{9,10},{10,1... | collective-permute-start | bytes 1572872 | tf_op jit(solution)/shard_map/ppermute | solution.py:19
  15.6 2.0 %collective-permute-start.10 = (bf16[128,2048]{1,0:T(8,128)(2,1)S(1)}, bf16[128,2048]{1,0:T(8,128)(2,1)S(1)}, u32[]{:S(2)}, u32[]{:S(2)}) collective-permute-start(bf16[128,2048]{1,0:T(8,128)(2,1)S(1)} %pad_maximum_fusion.3), channel_id=1, source_target_pairs={{0,2},{1,3},{2,0},{3,1},{4,6},{5,7},{6,4},{7,5},{8,10},{9,11},{10,... | collective-permute-start | bytes 1572872 | tf_op jit(solution)/shard_map/ppermute | solution.py:19
  17.6 2.7 %collective-permute-done.3 = bf16[1032,128]{1,0:T(8,128)(2,1)} collective-permute-done((bf16[1032,128]{1,0:T(8,128)(2,1)S(1)}, bf16[1032,128]{1,0:T(8,128)(2,1)}, u32[]{:S(2)}, u32[]{:S(2)}) %collective-permute-start.3) | collective-permute-done | bytes 264224 | tf_op jit(solution)/shard_map/ppermute | solution.py:19
  20.4 1.0 constant_dynamic-update-slice_fusion.6
  21.4 2.4 %collective-permute-start.1 = (bf16[128,4096]{1,0:T(8,128)(2,1)S(1)}, bf16[128,4096]{1,0:T(8,128)(2,1)S(1)}, u32[]{:S(2)}, u32[]{:S(2)}) collective-permute-start(bf16[128,4096]{1,0:T(8,128)(2,1)S(1)} %copy-done.5), channel_id=1, source_target_pairs={{0,248},{8,0},{16,8},{24,16},{32,24},{40,32},{48,40},{56,48},{64,5... | collective-permute-start | bytes 3145736 | tf_op jit(solution)/shard_map/ppermute | solution.py:11
  23.8 1.0 constant_dynamic-update-slice_fusion.5
  24.8 8.9 %collective-permute-done.5 = bf16[1032,128]{1,0:T(8,128)(2,1)S(1)} collective-permute-done((bf16[1032,128]{1,0:T(8,128)(2,1)S(1)}, bf16[1032,128]{1,0:T(8,128)(2,1)S(1)}, u32[]{:S(2)}, u32[]{:S(2)}) %collective-permute-start.5) | collective-permute-done | bytes 264224 | tf_op jit(solution)/shard_map/ppermute | solution.py:19
  33.8 2.6 %collective-permute-done.10 = bf16[128,2048]{1,0:T(8,128)(2,1)S(1)} collective-permute-done((bf16[128,2048]{1,0:T(8,128)(2,1)S(1)}, bf16[128,2048]{1,0:T(8,128)(2,1)S(1)}, u32[]{:S(2)}, u32[]{:S(2)}) %collective-permute-start.10) | collective-permute-done | bytes 524320 | tf_op jit(solution)/shard_map/ppermute | solution.py:19
  36.5 8.9 %collective-permute-done.11 = bf16[128,2048]{1,0:T(8,128)(2,1)S(1)} collective-permute-done((bf16[128,2048]{1,0:T(8,128)(2,1)S(1)}, bf16[128,2048]{1,0:T(8,128)(2,1)S(1)}, u32[]{:S(2)}, u32[]{:S(2)}) %collective-permute-start.11) | collective-permute-done | bytes 524320 | tf_op jit(solution)/shard_map/ppermute | solution.py:19
  45.3 3.0 %pad_maximum_fusion = bf16[512,2048]{1,0:T(8,128)(2,1)S(1)} fusion(bf16[128,2048]{1,0:T(8,128)(2,1)S(1)} %collective-permute-done.11, bf16[128,2048]{1,0:T(8,128)(2,1)S(1)} %collective-permute-done.10, bf16[128,2048]{1,0:T(8,128)(2,1)S(1)} %collective-permute-done.9, bf16[128,512]{1,0:T(8,128)(2,1)S(1)} %get-tuple-element.17, ...), kind=kLoop, calls=%fused_computation.3 | loop fusion | flops 14680064 | bytes 4194304 | tf_op jit(solution)/shard_map/concatenate | solution.py:67
  48.4 6.2 %collective-permute-start.12 = (bf16[512,2048]{1,0:T(8,128)(2,1)S(1)}, bf16[512,2048]{1,0:T(8,128)(2,1)S(1)}, u32[]{:S(2)}, u32[]{:S(2)}) collective-permute-start(bf16[512,2048]{1,0:T(8,128)(2,1)S(1)} %pad_maximum_fusion), channel_id=1, source_target_pairs={{0,248},{8,0},{16,8},{24,16},{32,24},{40,32},{48,40},{56,48},{64,5... | collective-permute-start | bytes 6291464 | tf_op jit(solution)/shard_map/ppermute | solution.py:11
  54.7 1.0 fusion.17
  56.5 1.0 fusion.16
  57.5 1.0 multiply_convert_fusion
  59.4 1.9 %collective-permute-start.7 = (bf16[1032,128]{1,0:T(8,128)(2,1)S(1)}, bf16[1032,128]{1,0:T(8,128)(2,1)S(1)}, u32[]{:S(2)}, u32[]{:S(2)}) collective-permute-start(bf16[1032,128]{1,0:T(8,128)(2,1)S(1)} %get-tuple-element.28), channel_id=1, source_target_pairs={{0,2},{1,3},{2,0},{3,1},{4,6},{5,7},{6,4},{7,5},{8,10},{9,11},{10,... | collective-permute-start | bytes 792584 | tf_op jit(solution)/shard_map/ppermute | solution.py:19
  61.3 2.5 %collective-permute-start.8 = (bf16[1032,128]{1,0:T(8,128)(2,1)S(1)}, bf16[1032,128]{1,0:T(8,128)(2,1)S(1)}, u32[]{:S(2)}, u32[]{:S(2)}) collective-permute-start(bf16[1032,128]{1,0:T(8,128)(2,1)S(1)} %get-tuple-element.28), channel_id=1, source_target_pairs={{0,3},{1,0},{2,1},{3,2},{4,7},{5,4},{6,5},{7,6},{8,11},{9,8},{10,9... | collective-permute-start | bytes 792584 | tf_op jit(solution)/shard_map/ppermute | solution.py:19
  63.8 0.9 fusion.18
  65.8 1.6 %collective-permute-done.7 = bf16[1032,128]{1,0:T(8,128)(2,1)S(1)} collective-permute-done((bf16[1032,128]{1,0:T(8,128)(2,1)S(1)}, bf16[1032,128]{1,0:T(8,128)(2,1)S(1)}, u32[]{:S(2)}, u32[]{:S(2)}) %collective-permute-start.7) | collective-permute-done | bytes 264224 | tf_op jit(solution)/shard_map/ppermute | solution.py:19
  67.5 2.6 %collective-permute-done.8 = bf16[1032,128]{1,0:T(8,128)(2,1)S(1)} collective-permute-done((bf16[1032,128]{1,0:T(8,128)(2,1)S(1)}, bf16[1032,128]{1,0:T(8,128)(2,1)S(1)}, u32[]{:S(2)}, u32[]{:S(2)}) %collective-permute-start.8) | collective-permute-done | bytes 264224 | tf_op jit(solution)/shard_map/ppermute | solution.py:19
  70.2 7.9 %collective-permute-done.12 = bf16[512,2048]{1,0:T(8,128)(2,1)S(1)} collective-permute-done((bf16[512,2048]{1,0:T(8,128)(2,1)S(1)}, bf16[512,2048]{1,0:T(8,128)(2,1)S(1)}, u32[]{:S(2)}, u32[]{:S(2)}) %collective-permute-start.12) | collective-permute-done | bytes 2097184 | tf_op jit(solution)/shard_map/ppermute | solution.py:11
  79.9 3.0 %collective-permute-start.13 = (bf16[1032,512]{1,0:T(8,128)(2,1)S(1)}, bf16[1032,512]{1,0:T(8,128)(2,1)S(1)}, u32[]{:S(2)}, u32[]{:S(2)}) collective-permute-start(bf16[1032,512]{1,0:T(8,128)(2,1)S(1)} %pad_maximum_fusion.1), channel_id=1, source_target_pairs={{0,4},{1,5},{2,6},{3,7},{4,0},{5,1},{6,2},{7,3},{8,12},{9,13},{10,... | collective-permute-start | bytes 3170312 | tf_op jit(solution)/shard_map/ppermute | solution.py:19
  82.9 0.9 fusion.15
  83.8 1.8 %add_convert_fusion = bf16[128,4096]{1,0:T(8,128)(2,1)} fusion(bf16[128,4096]{1,0:T(8,128)(2,1)S(1)} %collective-permute-done.2, f32[128,4096]{1,0:T(8,128)S(1)} %fusion.15, bf16[344,128]{1,0:T(8,128)(2,1)S(1)} %get-tuple-element.27, bf16[4096,344]{0,1:T(8,128)(2,1)S(1)} %copy-done), kind=kOutput, calls=%fused_computation.4 | convolution fusion | flops 362807296 | bytes 7100416 | tf_op jit(solution)/shard_map/dot_general | solution.py:29
  85.6 20.7 %collective-permute-done.13 = bf16[1032,512]{1,0:T(8,128)(2,1)S(1)} collective-permute-done((bf16[1032,512]{1,0:T(8,128)(2,1)S(1)}, bf16[1032,512]{1,0:T(8,128)(2,1)S(1)}, u32[]{:S(2)}, u32[]{:S(2)}) %collective-permute-start.13) | collective-permute-done | bytes 1056800 | tf_op jit(solution)/shard_map/ppermute | solution.py:19
  106.5 0.9 fusion.1
  107.5 1.3 %fusion.4 = bf16[344,512]{1,0:T(8,128)(2,1)} fusion(bf16[1024,2048]{1,0:T(8,128)(2,1)S(1)} %constant_dynamic-update-slice_fusion.8, f32[1032,512]{1,0:T(8,128)S(1)} %convert_element_type.53, bf16[1032,1024]{1,0:T(8,128)(2,1)S(1)} %constant_dynamic-update-slice_fusion), kind=kOutput, calls=%fused_computation.12 | convolution fusion | flops 361062400 | bytes 2809856 | tf_op jit(solution)/shard_map/dot_general | solution.py:83
  (50 shorter events, 8.3 us)
Async XLA Ops:
  0.6 4.4 %copy-start = (bf16[4096,344]{0,1:T(8,128)(2,1)S(1)}, bf16[4096,344]{0,1:T(8,128)(2,1)}, u32[]{:S(2)}) copy-start(bf16[4096,344]{0,1:T(8,128)(2,1)} %param.8) | copy-start | bytes 8454148
  0.6 3.2 %copy-start.2 = (bf16[344,4096]{1,0:T(8,128)(2,1)S(1)}, bf16[344,4096]{1,0:T(8,128)(2,1)}, u32[]{:S(2)}) copy-start(bf16[344,4096]{1,0:T(8,128)(2,1)} %param.9) | copy-start | bytes 8454148
  0.7 3.4 %copy-start.6 = (bf16[128,4096]{1,0:T(8,128)(2,1)S(1)}, bf16[128,4096]{1,0:T(8,128)(2,1)}, u32[]{:S(2)}) copy-start(bf16[128,4096]{1,0:T(8,128)(2,1)} %param.6) | copy-start | bytes 3145732
  4.0 1.4 %copy-start.4 = (bf16[128,4096]{1,0:T(8,128)(2,1)S(1)}, bf16[128,4096]{1,0:T(8,128)(2,1)}, u32[]{:S(2)}) copy-start(bf16[128,4096]{1,0:T(8,128)(2,1)} %param.5) | copy-start | bytes 3145732
  7.2 13.1 %collective-permute-start.3 = (bf16[1032,128]{1,0:T(8,128)(2,1)S(1)}, bf16[1032,128]{1,0:T(8,128)(2,1)}, u32[]{:S(2)}, u32[]{:S(2)}) collective-permute-start(bf16[1032,128]{1,0:T(8,128)(2,1)S(1)} %get-tuple-element.30), channel_id=1, source_target_pairs={{0,1},{1,2},{2,3},{3,0},{4,5},{5,6},{6,7},{7,4},{8,9},{9,10},{10,1... | collective-permute-start | bytes 792584 | tf_op jit(solution)/shard_map/ppermute | solution.py:19
  8.7 12.7 %collective-permute-start.4 = (bf16[1032,128]{1,0:T(8,128)(2,1)S(1)}, bf16[1032,128]{1,0:T(8,128)(2,1)}, u32[]{:S(2)}, u32[]{:S(2)}) collective-permute-start(bf16[1032,128]{1,0:T(8,128)(2,1)S(1)} %get-tuple-element.30), channel_id=1, source_target_pairs={{0,2},{1,3},{2,0},{3,1},{4,6},{5,7},{6,4},{7,5},{8,10},{9,11},{10,... | collective-permute-start | bytes 792584 | tf_op jit(solution)/shard_map/ppermute | solution.py:19
  11.6 22.2 %collective-permute-start.5 = (bf16[1032,128]{1,0:T(8,128)(2,1)S(1)}, bf16[1032,128]{1,0:T(8,128)(2,1)S(1)}, u32[]{:S(2)}, u32[]{:S(2)}) collective-permute-start(bf16[1032,128]{1,0:T(8,128)(2,1)S(1)} %get-tuple-element.30), channel_id=1, source_target_pairs={{0,3},{1,0},{2,1},{3,2},{4,7},{5,4},{6,5},{7,6},{8,11},{9,8},{10,9... | collective-permute-start | bytes 792584 | tf_op jit(solution)/shard_map/ppermute | solution.py:19
  12.0 1.6 %copy-start.5 = (bf16[128,4096]{1,0:T(8,128)(2,1)S(1)}, bf16[128,4096]{1,0:T(8,128)(2,1)}, u32[]{:S(2)}) copy-start(bf16[128,4096]{1,0:T(8,128)(2,1)} %param.5) | copy-start | bytes 3145732
  13.7 6.6 %copy-start.8 = (bf16[1032,1024]{1,0:T(8,128)(2,1)S(1)}, bf16[1032,1024]{1,0:T(8,128)(2,1)}, u32[]{:S(2)}) copy-start(bf16[1032,1024]{1,0:T(8,128)(2,1)} %get-tuple-element.31) | copy-start | bytes 6340612
  13.8 19.9 %copy-start.7 = (bf16[128,4096]{1,0:T(8,128)(2,1)S(1)}, bf16[128,4096]{1,0:T(8,128)(2,1)}, u32[]{:S(2)}) copy-start(bf16[128,4096]{1,0:T(8,128)(2,1)} %param.6) | copy-start | bytes 3145732
  13.8 20.0 %collective-permute-start.9 = (bf16[128,2048]{1,0:T(8,128)(2,1)S(1)}, bf16[128,2048]{1,0:T(8,128)(2,1)S(1)}, u32[]{:S(2)}, u32[]{:S(2)}) collective-permute-start(bf16[128,2048]{1,0:T(8,128)(2,1)S(1)} %pad_maximum_fusion.2), channel_id=1, source_target_pairs={{0,1},{1,2},{2,3},{3,0},{4,5},{5,6},{6,7},{7,4},{8,9},{9,10},{10,1... | collective-permute-start | bytes 1572872 | tf_op jit(solution)/shard_map/ppermute | solution.py:19
  15.6 20.9 %collective-permute-start.10 = (bf16[128,2048]{1,0:T(8,128)(2,1)S(1)}, bf16[128,2048]{1,0:T(8,128)(2,1)S(1)}, u32[]{:S(2)}, u32[]{:S(2)}) collective-permute-start(bf16[128,2048]{1,0:T(8,128)(2,1)S(1)} %pad_maximum_fusion.3), channel_id=1, source_target_pairs={{0,2},{1,3},{2,0},{3,1},{4,6},{5,7},{6,4},{7,5},{8,10},{9,11},{10,... | collective-permute-start | bytes 1572872 | tf_op jit(solution)/shard_map/ppermute | solution.py:19
  20.4 25.0 %collective-permute-start.11 = (bf16[128,2048]{1,0:T(8,128)(2,1)S(1)}, bf16[128,2048]{1,0:T(8,128)(2,1)S(1)}, u32[]{:S(2)}, u32[]{:S(2)}) collective-permute-start(bf16[128,2048]{1,0:T(8,128)(2,1)S(1)} %pad_maximum_fusion.4), channel_id=1, source_target_pairs={{0,3},{1,0},{2,1},{3,2},{4,7},{5,4},{6,5},{7,6},{8,11},{9,8},{10,9... | collective-permute-start | bytes 1572872 | tf_op jit(solution)/shard_map/ppermute | solution.py:19
  21.4 33.3 %collective-permute-start.1 = (bf16[128,4096]{1,0:T(8,128)(2,1)S(1)}, bf16[128,4096]{1,0:T(8,128)(2,1)S(1)}, u32[]{:S(2)}, u32[]{:S(2)}) collective-permute-start(bf16[128,4096]{1,0:T(8,128)(2,1)S(1)} %copy-done.5), channel_id=1, source_target_pairs={{0,248},{8,0},{16,8},{24,16},{32,24},{40,32},{48,40},{56,48},{64,5... | collective-permute-start | bytes 3145736 | tf_op jit(solution)/shard_map/ppermute | solution.py:11
  33.7 22.0 %collective-permute-start = (bf16[128,4096]{1,0:T(8,128)(2,1)S(1)}, bf16[128,4096]{1,0:T(8,128)(2,1)S(1)}, u32[]{:S(2)}, u32[]{:S(2)}) collective-permute-start(bf16[128,4096]{1,0:T(8,128)(2,1)S(1)} %copy-done.7), channel_id=1, source_target_pairs={{0,248},{8,0},{16,8},{24,16},{32,24},{40,32},{48,40},{56,48},{64,5... | collective-permute-start | bytes 3145736 | tf_op jit(solution)/shard_map/ppermute | solution.py:11
  48.3 6.4 %copy-start.1 = (bf16[4096,344]{0,1:T(8,128)(2,1)S(1)}, bf16[4096,344]{0,1:T(8,128)(2,1)}, u32[]{:S(2)}) copy-start(bf16[4096,344]{0,1:T(8,128)(2,1)} %param.7) | copy-start | bytes 8454148
  48.4 29.8 %collective-permute-start.12 = (bf16[512,2048]{1,0:T(8,128)(2,1)S(1)}, bf16[512,2048]{1,0:T(8,128)(2,1)S(1)}, u32[]{:S(2)}, u32[]{:S(2)}) collective-permute-start(bf16[512,2048]{1,0:T(8,128)(2,1)S(1)} %pad_maximum_fusion), channel_id=1, source_target_pairs={{0,248},{8,0},{16,8},{24,16},{32,24},{40,32},{48,40},{56,48},{64,5... | collective-permute-start | bytes 6291464 | tf_op jit(solution)/shard_map/ppermute | solution.py:11
  54.7 1.8 %copy-start.3 = (bf16[344,4096]{1,0:T(8,128)(2,1)S(1)}, bf16[344,4096]{1,0:T(8,128)(2,1)}, u32[]{:S(2)}) copy-start(bf16[344,4096]{1,0:T(8,128)(2,1)} %param.9) | copy-start | bytes 8454148
  58.6 7.1 %collective-permute-start.6 = (bf16[1032,128]{1,0:T(8,128)(2,1)S(1)}, bf16[1032,128]{1,0:T(8,128)(2,1)S(1)}, u32[]{:S(2)}, u32[]{:S(2)}) collective-permute-start(bf16[1032,128]{1,0:T(8,128)(2,1)S(1)} %get-tuple-element.28), channel_id=1, source_target_pairs={{0,1},{1,2},{2,3},{3,0},{4,5},{5,6},{6,7},{7,4},{8,9},{9,10},{10,1... | collective-permute-start | bytes 792584 | tf_op jit(solution)/shard_map/ppermute | solution.py:19
  59.4 8.0 %collective-permute-start.7 = (bf16[1032,128]{1,0:T(8,128)(2,1)S(1)}, bf16[1032,128]{1,0:T(8,128)(2,1)S(1)}, u32[]{:S(2)}, u32[]{:S(2)}) collective-permute-start(bf16[1032,128]{1,0:T(8,128)(2,1)S(1)} %get-tuple-element.28), channel_id=1, source_target_pairs={{0,2},{1,3},{2,0},{3,1},{4,6},{5,7},{6,4},{7,5},{8,10},{9,11},{10,... | collective-permute-start | bytes 792584 | tf_op jit(solution)/shard_map/ppermute | solution.py:19
  61.3 8.8 %collective-permute-start.8 = (bf16[1032,128]{1,0:T(8,128)(2,1)S(1)}, bf16[1032,128]{1,0:T(8,128)(2,1)S(1)}, u32[]{:S(2)}, u32[]{:S(2)}) collective-permute-start(bf16[1032,128]{1,0:T(8,128)(2,1)S(1)} %get-tuple-element.28), channel_id=1, source_target_pairs={{0,3},{1,0},{2,1},{3,2},{4,7},{5,4},{6,5},{7,6},{8,11},{9,8},{10,9... | collective-permute-start | bytes 792584 | tf_op jit(solution)/shard_map/ppermute | solution.py:19
  65.6 18.2 %collective-permute-start.2 = (bf16[128,4096]{1,0:T(8,128)(2,1)S(1)}, bf16[128,4096]{1,0:T(8,128)(2,1)S(1)}, u32[]{:S(2)}, u32[]{:S(2)}) collective-permute-start(bf16[128,4096]{1,0:T(8,128)(2,1)S(1)} %fusion), channel_id=1, source_target_pairs={{0,8},{8,16},{16,24},{24,32},{32,40},{40,48},{48,56},{56,64},{64,7... | collective-permute-start | bytes 3145736 | tf_op jit(solution)/shard_map/ppermute | solution.py:11
  79.9 26.4 %collective-permute-start.13 = (bf16[1032,512]{1,0:T(8,128)(2,1)S(1)}, bf16[1032,512]{1,0:T(8,128)(2,1)S(1)}, u32[]{:S(2)}, u32[]{:S(2)}) collective-permute-start(bf16[1032,512]{1,0:T(8,128)(2,1)S(1)} %pad_maximum_fusion.1), channel_id=1, source_target_pairs={{0,4},{1,5},{2,6},{3,7},{4,0},{5,1},{6,2},{7,3},{8,12},{9,13},{10,... | collective-permute-start | bytes 3170312 | tf_op jit(solution)/shard_map/ppermute | solution.py:19

commit v2 on v1

v2 whole, which is shorter than its diff:
```python
import functools

import jax
import jax.numpy as jnp
from jax import lax
from jax.experimental import pallas as pl
from jax.experimental.pallas import tpu as pltpu
from jax.sharding import PartitionSpec as P

ROW = 4
HALF = 176
STEPS = 4
MIB = 1 << 20


def along_blk(value, by):
    size = lax.axis_size("blk")
    return lax.ppermute(value, "blk", [(i, (i + by) % size) for i in range(size)])


def partner(r, j, i):
    return (r // ROW ^ j) * ROW + (r % ROW + i) % ROW


def along_rep(value, j, i):
    return lax.ppermute(value, "rep", [(r, partner(r, j, i)) for r in range(2 * ROW)])


def nt(left, right):
    return lax.dot_general(
        left, right, (((1,), (1,)), ((), ())), preferred_element_type=jnp.float32
    )


def tn(left, right):
    return lax.dot_general(
        left, right, (((0,), (0,)), ((), ())), preferred_element_type=jnp.float32
    )


def cost(us):
    return pl.CostEstimate(flops=int(us * 1e9), bytes_accessed=int(us * 3.5e6), transcendentals=0)


def params():
    return pltpu.CompilerParams(vmem_limit_bytes=40 * MIB)


def halves(d_gate, d_up, hidden):
    pad = jnp.zeros((2 * HALF - d_gate.shape[0], d_gate.shape[1]), jnp.float32)
    parts = (d_gate, d_up, hidden)
    first = jnp.concatenate([p[:HALF] for p in parts])
    second = jnp.concatenate([q for p in parts for q in (p[HALF:], pad)])
    return first.astype(jnp.bfloat16), second.astype(jnp.bfloat16)


def unit_grads(gate, upval, d_hidden):
    sigma = jax.nn.sigmoid(gate)
    active = gate * sigma
    slope = sigma * (1.0 + gate * (1.0 - sigma))
    return halves(d_hidden * upval * slope, d_hidden * active, active * upval)


VMEM = pl.BlockSpec(memory_space=pltpu.VMEM)


def deep(weight, rows):
    wide = weight.shape[1] // STEPS
    return sum(nt(weight[:, k * wide : (k + 1) * wide], rows[:, k * wide : (k + 1) * wide]) for k in range(STEPS))


def own_kernel(x, c, wg, wu, wd, first, second):
    first[...], second[...] = unit_grads(deep(wg, x), deep(wu, x), deep(wd, c))


def own_units(x, c, wg, wu, wd, us):
    t = x.shape[0]
    return pl.pallas_call(
        own_kernel,
        in_specs=[VMEM] * 5,
        out_specs=[VMEM] * 2,
        out_shape=[jax.ShapeDtypeStruct((3 * HALF, t), jnp.bfloat16)] * 2,
        compiler_params=params(),
        cost_estimate=cost(us),
        name="own_units",
    )(x, c, wg, wu, wd)


def gate_up_kernel(x, wg, wu, gate, upval):
    gate[...] = deep(wg, x)
    upval[...] = deep(wu, x)


def gate_up(x, wg, wu, us):
    return pl.pallas_call(
        gate_up_kernel,
        in_specs=[VMEM] * 3,
        out_specs=[VMEM] * 2,
        out_shape=[jax.ShapeDtypeStruct((wg.shape[0], x.shape[0]), jnp.float32)] * 2,
        compiler_params=params(),
        cost_estimate=cost(us),
        name="gate_up",
    )(x, wg, wu)


def far_kernel(c, wd, gate, upval, own_first, own_second, first, second):
    t = c.shape[0]
    first[:, :t] = own_first[...]
    second[:, :t] = own_second[...]
    first[:, t:], second[:, t:] = unit_grads(gate[...], upval[...], deep(wd, c))


def far_units(c, wd, gate, upval, own_first, own_second, us):
    return pl.pallas_call(
        far_kernel,
        in_specs=[VMEM] * 6,
        out_specs=[VMEM] * 2,
        out_shape=[jax.ShapeDtypeStruct((3 * HALF, 2 * c.shape[0]), jnp.bfloat16)] * 2,
        compiler_params=params(),
        cost_estimate=cost(us),
        name="far_units",
    )(c, wd, gate, upval, own_first, own_second)


def term_kernel(at, first, second, wg, wu, out):
    s, d = wg.shape
    cols = slice(at, at + out.shape[0])
    grads = []
    for n in range(2):
        rows = slice(n * HALF, (n + 1) * HALF)
        grads.append(jnp.concatenate([first[rows, cols], second[rows, cols]])[:s])
    for k in range(STEPS):
        cut = slice(k * d // STEPS, (k + 1) * d // STEPS)
        out[:, cut] = (tn(grads[0], wg[:, cut]) + tn(grads[1], wu[:, cut])).astype(out.dtype)


def row_term(first, second, wg, wu, at, t, dtype, us):
    return pl.pallas_call(
        functools.partial(term_kernel, at),
        in_specs=[VMEM] * 4,
        out_specs=VMEM,
        out_shape=jax.ShapeDtypeStruct((t, wg.shape[1]), dtype),
        compiler_params=params(),
        cost_estimate=cost(us),
        name="row_term",
    )(first, second, wg, wu)


def pack_kernel(x, c, *refs):
    outs, sem = refs[:-1], refs[-1]
    me = lax.axis_index("rep")
    wide = x.shape[1] // (2 * ROW)
    copies = []
    for i, out in enumerate(outs):
        for j in range(2):
            row = lax.rem(me // ROW + j, 2)
            to = row * ROW + lax.rem(me + i, ROW)
            source = pl.ds(pl.multiple_of(to * wide, wide), wide)
            for n, a in enumerate((x, c)):
                target = pl.ds((2 * j + n) * wide, wide)
                copies.append(pltpu.make_async_copy(a.at[:, source], out.at[:, target], sem.at[len(copies)]))
    for copy in copies:
        copy.start()
    for copy in copies:
        copy.wait()


def pack(x, c, pieces, us):
    t, d = x.shape
    return pl.pallas_call(
        pack_kernel,
        out_shape=[jax.ShapeDtypeStruct((t, d // 2), jnp.bfloat16)] * pieces,
        in_specs=[pl.BlockSpec(memory_space=pl.ANY)] * 2,
        out_specs=[pl.BlockSpec(memory_space=pl.ANY)] * pieces,
        scratch_shapes=[pltpu.SemaphoreType.DMA((4 * pieces,))],
        compiler_params=params(),
        cost_estimate=cost(us),
        name="pack",
    )(x, c)


def weight_kernel(at, *refs):
    near, far, grads, out = refs[:ROW], refs[ROW : ROW + 2], refs[ROW + 2 : -1], refs[-1]
    t = near[0].shape[0]
    wide = out.shape[1]
    left = jnp.concatenate([g[...] for g in grads], 1)

    def columns(first):
        cut = slice(first, first + wide)
        tall = [a for i in range(ROW) for a in (
            near[i][:, cut],
            far[0][:, cut] if i == 0 else far[1][(i - 1) * t : i * t, cut],
        )]
        return jnp.concatenate(tall)

    dot = functools.partial(jnp.dot, preferred_element_type=jnp.float32)
    out[: 2 * HALF] = dot(left[: 2 * HALF], columns(at)).astype(out.dtype)
    out[2 * HALF :] = dot(left[2 * HALF :], columns(at + wide)).astype(out.dtype)


def weight_terms(near, far, grads, at, dtype, us):
    wide = near[0].shape[1] // 4
    return pl.pallas_call(
        functools.partial(weight_kernel, at * wide),
        out_shape=jax.ShapeDtypeStruct((3 * HALF, wide), dtype),
        in_specs=[VMEM] * (2 * ROW + 2),
        out_specs=VMEM,
        compiler_params=params(),
        cost_estimate=cost(us),
        name="weight_terms",
    )(*near, *far, *grads)


def sum_kernel(a, b, a_other, b_other, gate, up, down):
    s = gate.shape[0]
    for n, out in enumerate((gate, up, down)):
        rows = slice(n * HALF, (n + 1) * HALF)
        total = a[rows] + a_other[rows].astype(jnp.float32)
        out[:HALF] = total.astype(out.dtype)
        total = b[rows] + b_other[rows].astype(jnp.float32)
        out[HALF:] = total[: s - HALF].astype(out.dtype)


def sums(a, b, a_other, b_other, s):
    return pl.pallas_call(
        sum_kernel,
        out_shape=[jax.ShapeDtypeStruct((s, a.shape[1]), jnp.bfloat16)] * 3,
        in_specs=[VMEM] * 4,
        out_specs=[VMEM] * 3,
        compiler_params=params(),
        cost_estimate=cost(1),
        name="sums",
    )(a, b, a_other, b_other)


def local(tokens, cotangent, gate_weight, up_weight, down_weight):
    w_gate, w_up, w_down = gate_weight.T, up_weight.T, down_weight
    s = w_gate.shape[0]
    t = tokens.shape[0]
    far_rows = along_blk(tokens, -1)
    far_cotan = along_blk(cotangent, -1)
    in_hbm = [pltpu.with_memory_space_constraint(a, pltpu.HBM) for a in (tokens, cotangent)]
    near = pack(*in_hbm, ROW, 1)
    near = [near[0]] + [along_rep(near[i], 0, i) for i in range(1, ROW)]

    own = own_units(tokens, cotangent, w_gate, w_up, w_down, 20)
    own_x = row_term(*own, w_gate, w_up, 0, t, jnp.float32, 3)

    far_rows, own_x = lax.optimization_barrier((far_rows, own_x))
    gate, upval = gate_up(far_rows, w_gate, w_up, 2)
    both = far_units(far_cotan, w_down, gate, upval, *own, 1.5)
    far_x = row_term(*both, w_gate, w_up, t, t, jnp.bfloat16, 1)
    near, far_x = lax.optimization_barrier((near, far_x))
    far_x = along_blk(far_x, 1)
    first, second = both
    second, far_x = lax.optimization_barrier((second, far_x))
    gathered = [[g] + [along_rep(g, 0, i) for i in range(1, ROW)] for g in (first, second)]
    far_cols = along_blk(jnp.concatenate(near[1:]), -1)
    far = [pack(far_rows, far_cotan, 1, 0.5)[0], far_cols]

    other = [along_rep(weight_terms(near, far, g, 2, jnp.bfloat16, 1), 1, 0) for g in gathered]
    mine = [weight_terms(near, far, g, 0, jnp.float32, 1) for g in gathered]
    gate_grad, up_grad, down_grad = sums(*mine, *other, s)
    input_grad = (own_x + far_x.astype(jnp.float32)).astype(jnp.bfloat16)
    return input_grad, gate_grad.T, up_grad.T, down_grad


def solution(mesh):
    in_specs = (
        P(("blk", "rep"), None),
        P(("blk", "rep"), None),
        P(None, "blk"),
        P(None, "blk"),
        P("blk", None),
    )
    out_specs = (P(("blk", "rep"), None), P("rep", "blk"), P("rep", "blk"), P("blk", "rep"))
    return jax.shard_map(local, mesh=mesh, in_specs=in_specs, out_specs=out_specs, check_vma=False)
```

time: 110 us -> 85.7 us (0.78)
  waiting for transfers between devices: 55.9 us -> 33.6 us
  matrix products: 16.2 us -> 0 us
  Pallas kernels: 0 us -> 13.4 us
  starting transfers between devices: 25.3 us -> 28.9 us
  other arithmetic: 4.41 us -> 1.28 us
    ppermute x10 -> x11, waiting for transfers between devices: 48 us -> 16.9 us  [along_rep(): lax.ppermute(value, 'rep', [(r, partner(r, j, i)) for r in range(2 * ROW)])]
    dot_general x14 -> x0, matrix products: 16.2 us -> none  [the longest x6 8.14 us: nt(): lax.dot_general(left, right, (((1,), (1,)), ((), ())), preferred_element_...]
    pallas_call x0 -> x12, Pallas kernels: none -> 13.4 us  [the longest x4 2.92 us: weight_terms(): pl.pallas_call(functools.partial(weight_kernel, at * wide), out_shape=jax...]
    ppermute x4, waiting for transfers between devices: 7.87 us -> 16.8 us  [along_blk(): lax.ppermute(value, 'blk', [(i, (i + by) % size) for i in range(size)])]
    concatenate x7 -> x1, other arithmetic: 4.09 us -> 0.1 us  [local(): far_cols = along_blk(jnp.concatenate(near[1:]), -1)]
    ppermute x10 -> x11, starting transfers between devices: 16.7 us -> 20.4 us  [along_rep(): lax.ppermute(value, 'rep', [(r, partner(r, j, i)) for r in range(2 * ROW)])]
    unnamed x26 -> x14, local copies, waits for them, and re-layouts: 4.02 us -> 6.91 us
    dynamic_slice x2 -> x0, local copies, waits for them, and re-layouts: 1.57 us -> none  [columns(): lax.dynamic_slice_in_dim(a, to * wide, wide, 1)]
  transfers between devices with their start and end apart: 14 -> 15, of which waited for: 8 -> 7; matrix products, arithmetic and copies ran while one was open for 15% -> 1% of each run, Pallas kernels for 0% -> 14%
where the time goes in v2:
time: 85.7 us; the launch traced here: 85 us
  waiting for transfers between devices  33.6 us (39%)
  starting transfers between devices  28.9 us (34%)
  Pallas kernels  13.4 us (16%)
  local copies, waits for them, and re-layouts  6.91 us (8%)
  other arithmetic  1.28 us (1%)
    ppermute x11, starting transfers between devices, along_rep(): lax.ppermute(value, 'rep', [(r, partner(r, j, i)) for r in range(2 * ROW)])  20.4 us
    ppermute x11, waiting for transfers between devices, along_rep(): lax.ppermute(value, 'rep', [(r, partner(r, j, i)) for r in range(2 * ROW)])  16.9 us
    ppermute x4, waiting for transfers between devices, along_blk(): lax.ppermute(value, 'blk', [(i, (i + by) % size) for i in range(size)])  16.8 us
    ppermute x4, starting transfers between devices, along_blk(): lax.ppermute(value, 'blk', [(i, (i + by) % size) for i in range(size)])  8.59 us
    unnamed x14, local copies, waits for them, and re-layouts  6.91 us
    pallas_call x4, Pallas kernels, weight_terms(): pl.pallas_call(functools.partial(weight_kernel, at * wide), out_shape=jax...  2.92 us
    pallas_call x2, Pallas kernels, row_term(): pl.pallas_call(functools.partial(term_kernel, at), in_specs=[VMEM] * 4, o...  2.57 us
    pallas_call x1, Pallas kernels, own_units(): pl.pallas_call(own_kernel, in_specs=[VMEM] * 5, out_specs=[VMEM] * 2, out...  2.4 us
  transfers between devices with their start and end apart: 15, of which 7 were waited for; matrix products, arithmetic and copies ran while one was open for 1% of the time, Pallas kernels for 14%

profile of v2, /device:TPU:2, one launch (start us, length us, event | category | flops | bytes accessed | tf_op | source)
XLA Modules:
  0.0 85.0 jit_solution(18149672745429725096)
XLA Ops:
  0.6 6.4 %collective-permute-start = (bf16[128,4096]{1,0:T(8,128)(2,1)}, bf16[128,4096]{1,0:T(8,128)(2,1)S(1)}, u32[]{:S(2)}, u32[]{:S(2)}) collective-permute-start(bf16[128,4096]{1,0:T(8,128)(2,1)} %x.3), channel_id=1, source_target_pairs={{0,248},{8,0},{16,8},{24,16},{32,24},{40,32},{48,40},{56,48},{64,5... | collective-permute-start | bytes 3145736 | tf_op jit(solution)/shard_map/ppermute | solution.py:18
  7.7 1.7 %pack.2 = (bf16[128,2048]{1,0:T(8,128)(2,1)S(1)}, bf16[128,2048]{1,0:T(8,128)(2,1)S(1)}, bf16[128,2048]{1,0:T(8,128)(2,1)S(1)}, bf16[128,2048]{1,0:T(8,128)(2,1)S(1)}) custom-call(bf16[128,4096]{1,0:T(8,128)(2,1)} %x.3, bf16[128,4096]{1,0:T(8,128)(2,1)} %c.3), custom_call_target="tpu_custom_call" | custom-call | flops 1000000000 | bytes 3500000 | tf_op jit(solution)/shard_map/pack/pallas_call | solution.py:170
  9.5 1.6 %collective-permute-start.2 = (bf16[128,2048]{1,0:T(8,128)(2,1)S(1)}, bf16[128,2048]{1,0:T(8,128)(2,1)S(1)}, u32[]{:S(2)}, u32[]{:S(2)}) collective-permute-start(bf16[128,2048]{1,0:T(8,128)(2,1)S(1)} %get-tuple-element.34), channel_id=1, source_target_pairs={{0,1},{1,2},{2,3},{3,0},{4,5},{5,6},{6,7},{7,4},{8,9},{9,10},{10,1... | collective-permute-start | bytes 1572872 | tf_op jit(solution)/shard_map/ppermute | solution.py:26
  11.0 1.1 %collective-permute-start.3 = (bf16[128,2048]{1,0:T(8,128)(2,1)S(1)}, bf16[128,2048]{1,0:T(8,128)(2,1)S(1)}, u32[]{:S(2)}, u32[]{:S(2)}) collective-permute-start(bf16[128,2048]{1,0:T(8,128)(2,1)S(1)} %get-tuple-element.35), channel_id=1, source_target_pairs={{0,2},{1,3},{2,0},{3,1},{4,6},{5,7},{6,4},{7,5},{8,10},{9,11},{10,... | collective-permute-start | bytes 1572872 | tf_op jit(solution)/shard_map/ppermute | solution.py:26
  12.1 2.2 %collective-permute-start.4 = (bf16[128,2048]{1,0:T(8,128)(2,1)S(1)}, bf16[128,2048]{1,0:T(8,128)(2,1)S(1)}, u32[]{:S(2)}, u32[]{:S(2)}) collective-permute-start(bf16[128,2048]{1,0:T(8,128)(2,1)S(1)} %get-tuple-element.36), channel_id=1, source_target_pairs={{0,3},{1,0},{2,1},{3,2},{4,7},{5,4},{6,5},{7,6},{8,11},{9,8},{10,9... | collective-permute-start | bytes 1572872 | tf_op jit(solution)/shard_map/ppermute | solution.py:26
  14.3 1.8 %copy-done.1 = bf16[4096,344]{0,1:T(8,128)(2,1)S(1)} copy-done((bf16[4096,344]{0,1:T(8,128)(2,1)S(1)}, bf16[4096,344]{0,1:T(8,128)(2,1)}, u32[]{:S(2)}) %copy-start.1) | copy-done | bytes 2818072
  16.1 1.8 %copy-done.3 = bf16[344,4096]{1,0:T(8,128)(2,1)S(1)} copy-done((bf16[344,4096]{1,0:T(8,128)(2,1)S(1)}, bf16[344,4096]{1,0:T(8,128)(2,1)}, u32[]{:S(2)}) %copy-start.3) | copy-done | bytes 2818072
  17.9 1.2 %copy-done.5 = bf16[128,4096]{1,0:T(8,128)(2,1)S(1)} copy-done((bf16[128,4096]{1,0:T(8,128)(2,1)S(1)}, bf16[128,4096]{1,0:T(8,128)(2,1)}, u32[]{:S(2)}) %copy-start.5) | copy-done | bytes 1048600
  19.1 1.2 %copy-done.6 = bf16[128,4096]{1,0:T(8,128)(2,1)S(1)} copy-done((bf16[128,4096]{1,0:T(8,128)(2,1)S(1)}, bf16[128,4096]{1,0:T(8,128)(2,1)}, u32[]{:S(2)}) %copy-start.6) | copy-done | bytes 1048600
  20.3 2.4 %own_units.1 = (bf16[528,128]{1,0:T(8,128)(2,1)S(1)}, bf16[528,128]{1,0:T(8,128)(2,1)S(1)}) custom-call(bf16[128,4096]{1,0:T(8,128)(2,1)S(1)} %copy-done.5, bf16[128,4096]{1,0:T(8,128)(2,1)S(1)} %copy-done.6, bf16[344,4096]{1,0:T(8,128)(2,1)S(1)} %bitcast.4, bf16[344,4096]{1,0:T(8,128)(2,1)S(1)} %bitcast.8, bf16[344,4096]{1,0:T(8,128)(2,1)S(1)} %copy-done.3), custom_call_target="tpu_custom_call" | custom-call | flops 20000000000 | bytes 70000000 | tf_op jit(solution)/shard_map/own_units/pallas_call | solution.py:78
  22.7 1.3 %row_term.2 = f32[128,4096]{1,0:T(8,128)S(1)} custom-call(bf16[528,128]{1,0:T(8,128)(2,1)S(1)} %get-tuple-element.26.first.own_first, bf16[528,128]{1,0:T(8,128)(2,1)S(1)} %get-tuple-element.27.second.own_second, bf16[344,4096]{1,0:T(8,128)(2,1)S(1)} %bitcast.5, bf16[344,4096]{1,0:T(8,128)(2,1)S(1)} %bitcast.9), custom_call_target="tpu_custom_call" | custom-call | flops 3000000000 | bytes 10500000 | tf_op jit(solution)/shard_map/row_term/pallas_call | solution.py:138
  24.1 1.6 %gate_up.1 = (f32[344,128]{1,0:T(8,128)S(1)}, f32[344,128]{1,0:T(8,128)S(1)}) custom-call(bf16[128,4096]{1,0:T(8,128)(2,1)S(1)} %collective-permute-done.x, bf16[344,4096]{1,0:T(8,128)(2,1)S(1)} %bitcast.6, bf16[344,4096]{1,0:T(8,128)(2,1)S(1)} %bitcast.10), custom_call_target="tpu_custom_call" | custom-call | flops 2000000000 | bytes 7000000 | tf_op jit(solution)/shard_map/gate_up/pallas_call | solution.py:95
  25.7 5.2 %collective-permute-done.1.c = bf16[128,4096]{1,0:T(8,128)(2,1)S(1)} collective-permute-done((bf16[128,4096]{1,0:T(8,128)(2,1)}, bf16[128,4096]{1,0:T(8,128)(2,1)S(1)}, u32[]{:S(2)}, u32[]{:S(2)}) %collective-permute-start.1) | collective-permute-done | bytes 1048608 | tf_op jit(solution)/shard_map/ppermute | solution.py:18
  30.9 0.9 %far_units.1 = (bf16[528,256]{1,0:T(8,128)(2,1)S(1)}, bf16[528,256]{1,0:T(8,128)(2,1)S(1)}) custom-call(bf16[128,4096]{1,0:T(8,128)(2,1)S(1)} %collective-permute-done.1.c, bf16[344,4096]{1,0:T(8,128)(2,1)S(1)} %copy-done.4, f32[344,128]{1,0:T(8,128)S(1)} %get-tuple-element.30.gate, f32[344,128]{1,0:T(8,128)S(1)} %get-tuple-element.31.upval, ...), custom_call_target="tpu_custom_call" | custom-call | flops 1500000000 | bytes 5250000 | tf_op jit(solution)/shard_map/far_units/pallas_call | solution.py:114
  31.8 0.9 %copy-done.2 = bf16[4096,344]{0,1:T(8,128)(2,1)S(1)} copy-done((bf16[4096,344]{0,1:T(8,128)(2,1)S(1)}, bf16[4096,344]{0,1:T(8,128)(2,1)}, u32[]{:S(2)}) %copy-start.2) | copy-done | bytes 2818072
  32.7 1.3 %row_term.3 = bf16[128,4096]{1,0:T(8,128)(2,1)S(1)} custom-call(bf16[528,256]{1,0:T(8,128)(2,1)S(1)} %get-tuple-element.37.first.refs_6_, bf16[528,256]{1,0:T(8,128)(2,1)S(1)} %get-tuple-element.44.second.refs_6_, bf16[344,4096]{1,0:T(8,128)(2,1)S(1)} %bitcast.7, bf16[344,4096]{1,0:T(8,128)(2,1)S(1)} %bitcast.11), custom_call_target="tpu_custom_call" | custom-call | flops 1000000000 | bytes 3500000 | tf_op jit(solution)/shard_map/row_term/pallas_call | solution.py:138
  34.0 2.5 %collective-permute-done.4.refs_3_ = bf16[128,2048]{1,0:T(8,128)(2,1)S(1)} collective-permute-done((bf16[128,2048]{1,0:T(8,128)(2,1)S(1)}, bf16[128,2048]{1,0:T(8,128)(2,1)S(1)}, u32[]{:S(2)}, u32[]{:S(2)}) %collective-permute-start.4) | collective-permute-done | bytes 524320 | tf_op jit(solution)/shard_map/ppermute | solution.py:26
  36.6 1.5 %collective-permute-start.6 = (bf16[384,2048]{1,0:T(8,128)(2,1)S(1)}, bf16[384,2048]{1,0:T(8,128)(2,1)S(1)}, u32[]{:S(2)}, u32[]{:S(2)}) collective-permute-start(bf16[384,2048]{1,0:T(8,128)(2,1)S(1)} %pad_maximum_fusion), channel_id=1, source_target_pairs={{0,248},{8,0},{16,8},{24,16},{32,24},{40,32},{48,40},{56,48},{64,5... | collective-permute-start | bytes 4718600 | tf_op jit(solution)/shard_map/ppermute | solution.py:18
  38.1 0.8 collective-permute-start.9
  38.9 2.1 %collective-permute-start.8 = (bf16[528,256]{1,0:T(8,128)(2,1)S(1)}, bf16[528,256]{1,0:T(8,128)(2,1)S(1)}, u32[]{:S(2)}, u32[]{:S(2)}) collective-permute-start(bf16[528,256]{1,0:T(8,128)(2,1)S(1)} %get-tuple-element.37.first.refs_6_), channel_id=1, source_target_pairs={{0,2},{1,3},{2,0},{3,1},{4,6},{5,7},{6,4},{7,5},{8,10},{9,11},{10,... | collective-permute-start | bytes 811016 | tf_op jit(solution)/shard_map/ppermute | solution.py:26
  41.1 1.8 %collective-permute-start.7 = (bf16[528,256]{1,0:T(8,128)(2,1)S(1)}, bf16[528,256]{1,0:T(8,128)(2,1)S(1)}, u32[]{:S(2)}, u32[]{:S(2)}) collective-permute-start(bf16[528,256]{1,0:T(8,128)(2,1)S(1)} %get-tuple-element.37.first.refs_6_), channel_id=1, source_target_pairs={{0,1},{1,2},{2,3},{3,0},{4,5},{5,6},{6,7},{7,4},{8,9},{9,10},{10,1... | collective-permute-start | bytes 811016 | tf_op jit(solution)/shard_map/ppermute | solution.py:26
  42.9 11.6 %collective-permute-done.5 = bf16[128,4096]{1,0:T(8,128)(2,1)S(1)} collective-permute-done((bf16[128,4096]{1,0:T(8,128)(2,1)S(1)}, bf16[128,4096]{1,0:T(8,128)(2,1)S(1)}, u32[]{:S(2)}, u32[]{:S(2)}) %collective-permute-start.5) | collective-permute-done | bytes 1048608 | tf_op jit(solution)/shard_map/ppermute | solution.py:18
  55.3 2.1 %collective-permute-start.11 = (bf16[528,256]{1,0:T(8,128)(2,1)S(1)}, bf16[528,256]{1,0:T(8,128)(2,1)S(1)}, u32[]{:S(2)}, u32[]{:S(2)}) collective-permute-start(bf16[528,256]{1,0:T(8,128)(2,1)S(1)} %get-tuple-element.44.second.refs_6_), channel_id=1, source_target_pairs={{0,2},{1,3},{2,0},{3,1},{4,6},{5,7},{6,4},{7,5},{8,10},{9,11},{10,... | collective-permute-start | bytes 811016 | tf_op jit(solution)/shard_map/ppermute | solution.py:26
  57.4 1.8 %collective-permute-start.10 = (bf16[528,256]{1,0:T(8,128)(2,1)S(1)}, bf16[528,256]{1,0:T(8,128)(2,1)S(1)}, u32[]{:S(2)}, u32[]{:S(2)}) collective-permute-start(bf16[528,256]{1,0:T(8,128)(2,1)S(1)} %get-tuple-element.44.second.refs_6_), channel_id=1, source_target_pairs={{0,1},{1,2},{2,3},{3,0},{4,5},{5,6},{6,7},{7,4},{8,9},{9,10},{10,1... | collective-permute-start | bytes 811016 | tf_op jit(solution)/shard_map/ppermute | solution.py:26
  60.1 3.0 %collective-permute-start.13 = (bf16[528,512]{1,0:T(8,128)(2,1)S(1)}, bf16[528,512]{1,0:T(8,128)(2,1)S(1)}, u32[]{:S(2)}, u32[]{:S(2)}) collective-permute-start(bf16[528,512]{1,0:T(8,128)(2,1)S(1)} %weight_terms.6), channel_id=1, source_target_pairs={{0,4},{1,5},{2,6},{3,7},{4,0},{5,1},{6,2},{7,3},{8,12},{9,13},{10,... | collective-permute-start | bytes 1622024 | tf_op jit(solution)/shard_map/ppermute | solution.py:26
  63.1 1.6 %collective-permute-done.11.refs_8_ = bf16[528,256]{1,0:T(8,128)(2,1)S(1)} collective-permute-done((bf16[528,256]{1,0:T(8,128)(2,1)S(1)}, bf16[528,256]{1,0:T(8,128)(2,1)S(1)}, u32[]{:S(2)}, u32[]{:S(2)}) %collective-permute-start.11) | collective-permute-done | bytes 270368 | tf_op jit(solution)/shard_map/ppermute | solution.py:26
  64.7 1.2 %collective-permute-done.10.refs_7_ = bf16[528,256]{1,0:T(8,128)(2,1)S(1)} collective-permute-done((bf16[528,256]{1,0:T(8,128)(2,1)S(1)}, bf16[528,256]{1,0:T(8,128)(2,1)S(1)}, u32[]{:S(2)}, u32[]{:S(2)}) %collective-permute-start.10) | collective-permute-done | bytes 270368 | tf_op jit(solution)/shard_map/ppermute | solution.py:26
  66.6 3.0 %collective-permute-start.14 = (bf16[528,512]{1,0:T(8,128)(2,1)S(1)}, bf16[528,512]{1,0:T(8,128)(2,1)S(1)}, u32[]{:S(2)}, u32[]{:S(2)}) collective-permute-start(bf16[528,512]{1,0:T(8,128)(2,1)S(1)} %weight_terms.7), channel_id=1, source_target_pairs={{0,4},{1,5},{2,6},{3,7},{4,0},{5,1},{6,2},{7,3},{8,12},{9,13},{10,... | collective-permute-start | bytes 1622024 | tf_op jit(solution)/shard_map/ppermute | solution.py:26
  69.6 1.2 %add_convert_fusion = bf16[128,4096]{1,0:T(8,128)(2,1)} fusion(f32[128,4096]{1,0:T(8,128)S(1)} %row_term.2, bf16[128,4096]{1,0:T(8,128)(2,1)S(1)} %collective-permute-done.5), kind=kLoop, calls=%fused_computation | loop fusion | flops 1572864 | bytes 4194304 | tf_op jit(solution)/shard_map/convert_element_type | solution.py:264
  72.3 4.7 %collective-permute-done.13.a_other = bf16[528,512]{1,0:T(8,128)(2,1)S(1)} collective-permute-done((bf16[528,512]{1,0:T(8,128)(2,1)S(1)}, bf16[528,512]{1,0:T(8,128)(2,1)S(1)}, u32[]{:S(2)}, u32[]{:S(2)}) %collective-permute-start.13) | collective-permute-done | bytes 540704 | tf_op jit(solution)/shard_map/ppermute | solution.py:26
  76.9 7.0 %collective-permute-done.14.b_other = bf16[528,512]{1,0:T(8,128)(2,1)S(1)} collective-permute-done((bf16[528,512]{1,0:T(8,128)(2,1)S(1)}, bf16[528,512]{1,0:T(8,128)(2,1)S(1)}, u32[]{:S(2)}, u32[]{:S(2)}) %collective-permute-start.14) | collective-permute-done | bytes 540704 | tf_op jit(solution)/shard_map/ppermute | solution.py:26
  83.9 1.1 %sums.1 = (bf16[344,512]{1,0:T(8,128)(2,1)}, bf16[344,512]{1,0:T(8,128)(2,1)}, bf16[344,512]{1,0:T(8,128)(2,1)}) custom-call(f32[528,512]{1,0:T(8,128)S(1)} %weight_terms.4.a, f32[528,512]{1,0:T(8,128)S(1)} %weight_terms.5.b, bf16[528,512]{1,0:T(8,128)(2,1)S(1)} %collective-permute-done.13.a_other, bf16[528,512]{1,0:T(8,128)(2,1)S(1)} %collective-permute-done.14.b_other), custom_call_target="tpu_custom_call" | custom-call | flops 1000000000 | bytes 3500000 | tf_op jit(solution)/shard_map/sums/pallas_call | solution.py:225
  (26 shorter events, 4.7 us)
Async XLA Ops:
  0.6 13.7 %copy-start = (bf16[4096,344]{0,1:T(8,128)(2,1)S(1)}, bf16[4096,344]{0,1:T(8,128)(2,1)}, u32[]{:S(2)}) copy-start(bf16[4096,344]{0,1:T(8,128)(2,1)} %param.7) | copy-start | bytes 8454148
  0.6 23.4 %collective-permute-start = (bf16[128,4096]{1,0:T(8,128)(2,1)}, bf16[128,4096]{1,0:T(8,128)(2,1)S(1)}, u32[]{:S(2)}, u32[]{:S(2)}) collective-permute-start(bf16[128,4096]{1,0:T(8,128)(2,1)} %x.3), channel_id=1, source_target_pairs={{0,248},{8,0},{16,8},{24,16},{32,24},{40,32},{48,40},{56,48},{64,5... | collective-permute-start | bytes 3145736 | tf_op jit(solution)/shard_map/ppermute | solution.py:18
  7.0 23.9 %collective-permute-start.1 = (bf16[128,4096]{1,0:T(8,128)(2,1)}, bf16[128,4096]{1,0:T(8,128)(2,1)S(1)}, u32[]{:S(2)}, u32[]{:S(2)}) collective-permute-start(bf16[128,4096]{1,0:T(8,128)(2,1)} %c.3), channel_id=1, source_target_pairs={{0,248},{8,0},{16,8},{24,16},{32,24},{40,32},{48,40},{56,48},{64,5... | collective-permute-start | bytes 3145736 | tf_op jit(solution)/shard_map/ppermute | solution.py:18
  9.5 24.5 %collective-permute-start.2 = (bf16[128,2048]{1,0:T(8,128)(2,1)S(1)}, bf16[128,2048]{1,0:T(8,128)(2,1)S(1)}, u32[]{:S(2)}, u32[]{:S(2)}) collective-permute-start(bf16[128,2048]{1,0:T(8,128)(2,1)S(1)} %get-tuple-element.34), channel_id=1, source_target_pairs={{0,1},{1,2},{2,3},{3,0},{4,5},{5,6},{6,7},{7,4},{8,9},{9,10},{10,1... | collective-permute-start | bytes 1572872 | tf_op jit(solution)/shard_map/ppermute | solution.py:26
  11.0 23.0 %collective-permute-start.3 = (bf16[128,2048]{1,0:T(8,128)(2,1)S(1)}, bf16[128,2048]{1,0:T(8,128)(2,1)S(1)}, u32[]{:S(2)}, u32[]{:S(2)}) collective-permute-start(bf16[128,2048]{1,0:T(8,128)(2,1)S(1)} %get-tuple-element.35), channel_id=1, source_target_pairs={{0,2},{1,3},{2,0},{3,1},{4,6},{5,7},{6,4},{7,5},{8,10},{9,11},{10,... | collective-permute-start | bytes 1572872 | tf_op jit(solution)/shard_map/ppermute | solution.py:26
  12.1 24.3 %collective-permute-start.4 = (bf16[128,2048]{1,0:T(8,128)(2,1)S(1)}, bf16[128,2048]{1,0:T(8,128)(2,1)S(1)}, u32[]{:S(2)}, u32[]{:S(2)}) collective-permute-start(bf16[128,2048]{1,0:T(8,128)(2,1)S(1)} %get-tuple-element.36), channel_id=1, source_target_pairs={{0,3},{1,0},{2,1},{3,2},{4,7},{5,4},{6,5},{7,6},{8,11},{9,8},{10,9... | collective-permute-start | bytes 1572872 | tf_op jit(solution)/shard_map/ppermute | solution.py:26
  14.3 1.8 %copy-start.1 = (bf16[4096,344]{0,1:T(8,128)(2,1)S(1)}, bf16[4096,344]{0,1:T(8,128)(2,1)}, u32[]{:S(2)}) copy-start(bf16[4096,344]{0,1:T(8,128)(2,1)} %param.8) | copy-start | bytes 8454148
  16.1 1.8 %copy-start.3 = (bf16[344,4096]{1,0:T(8,128)(2,1)S(1)}, bf16[344,4096]{1,0:T(8,128)(2,1)}, u32[]{:S(2)}) copy-start(bf16[344,4096]{1,0:T(8,128)(2,1)} %wd.3) | copy-start | bytes 8454148
  17.9 1.2 %copy-start.5 = (bf16[128,4096]{1,0:T(8,128)(2,1)S(1)}, bf16[128,4096]{1,0:T(8,128)(2,1)}, u32[]{:S(2)}) copy-start(bf16[128,4096]{1,0:T(8,128)(2,1)} %x.3) | copy-start | bytes 3145732
  19.1 1.2 %copy-start.6 = (bf16[128,4096]{1,0:T(8,128)(2,1)S(1)}, bf16[128,4096]{1,0:T(8,128)(2,1)}, u32[]{:S(2)}) copy-start(bf16[128,4096]{1,0:T(8,128)(2,1)} %c.3) | copy-start | bytes 3145732
  24.0 6.9 %copy-start.4 = (bf16[344,4096]{1,0:T(8,128)(2,1)S(1)}, bf16[344,4096]{1,0:T(8,128)(2,1)}, u32[]{:S(2)}) copy-start(bf16[344,4096]{1,0:T(8,128)(2,1)} %wd.3) | copy-start | bytes 8454148
  30.9 1.8 %copy-start.2 = (bf16[4096,344]{0,1:T(8,128)(2,1)S(1)}, bf16[4096,344]{0,1:T(8,128)(2,1)}, u32[]{:S(2)}) copy-start(bf16[4096,344]{0,1:T(8,128)(2,1)} %param.8) | copy-start | bytes 8454148
  36.6 22.8 %collective-permute-start.6 = (bf16[384,2048]{1,0:T(8,128)(2,1)S(1)}, bf16[384,2048]{1,0:T(8,128)(2,1)S(1)}, u32[]{:S(2)}, u32[]{:S(2)}) collective-permute-start(bf16[384,2048]{1,0:T(8,128)(2,1)S(1)} %pad_maximum_fusion), channel_id=1, source_target_pairs={{0,248},{8,0},{16,8},{24,16},{32,24},{40,32},{48,40},{56,48},{64,5... | collective-permute-start | bytes 4718600 | tf_op jit(solution)/shard_map/ppermute | solution.py:18
  38.1 16.3 %collective-permute-start.5 = (bf16[128,4096]{1,0:T(8,128)(2,1)S(1)}, bf16[128,4096]{1,0:T(8,128)(2,1)S(1)}, u32[]{:S(2)}, u32[]{:S(2)}) collective-permute-start(bf16[128,4096]{1,0:T(8,128)(2,1)S(1)} %row_term.3), channel_id=1, source_target_pairs={{0,8},{8,16},{16,24},{24,32},{32,40},{40,48},{48,56},{56,64},{64,7... | collective-permute-start | bytes 3145736 | tf_op jit(solution)/shard_map/ppermute | solution.py:18
  38.1 17.2 %collective-permute-start.9 = (bf16[528,256]{1,0:T(8,128)(2,1)S(1)}, bf16[528,256]{1,0:T(8,128)(2,1)S(1)}, u32[]{:S(2)}, u32[]{:S(2)}) collective-permute-start(bf16[528,256]{1,0:T(8,128)(2,1)S(1)} %get-tuple-element.37.first.refs_6_), channel_id=1, source_target_pairs={{0,3},{1,0},{2,1},{3,2},{4,7},{5,4},{6,5},{7,6},{8,11},{9,8},{10,9... | collective-permute-start | bytes 811016 | tf_op jit(solution)/shard_map/ppermute | solution.py:26
  38.9 18.5 %collective-permute-start.8 = (bf16[528,256]{1,0:T(8,128)(2,1)S(1)}, bf16[528,256]{1,0:T(8,128)(2,1)S(1)}, u32[]{:S(2)}, u32[]{:S(2)}) collective-permute-start(bf16[528,256]{1,0:T(8,128)(2,1)S(1)} %get-tuple-element.37.first.refs_6_), channel_id=1, source_target_pairs={{0,2},{1,3},{2,0},{3,1},{4,6},{5,7},{6,4},{7,5},{8,10},{9,11},{10,... | collective-permute-start | bytes 811016 | tf_op jit(solution)/shard_map/ppermute | solution.py:26
  41.1 18.3 %collective-permute-start.7 = (bf16[528,256]{1,0:T(8,128)(2,1)S(1)}, bf16[528,256]{1,0:T(8,128)(2,1)S(1)}, u32[]{:S(2)}, u32[]{:S(2)}) collective-permute-start(bf16[528,256]{1,0:T(8,128)(2,1)S(1)} %get-tuple-element.37.first.refs_6_), channel_id=1, source_target_pairs={{0,1},{1,2},{2,3},{3,0},{4,5},{5,6},{6,7},{7,4},{8,9},{9,10},{10,1... | collective-permute-start | bytes 811016 | tf_op jit(solution)/shard_map/ppermute | solution.py:26
  54.4 8.7 %collective-permute-start.12 = (bf16[528,256]{1,0:T(8,128)(2,1)S(1)}, bf16[528,256]{1,0:T(8,128)(2,1)S(1)}, u32[]{:S(2)}, u32[]{:S(2)}) collective-permute-start(bf16[528,256]{1,0:T(8,128)(2,1)S(1)} %get-tuple-element.44.second.refs_6_), channel_id=1, source_target_pairs={{0,3},{1,0},{2,1},{3,2},{4,7},{5,4},{6,5},{7,6},{8,11},{9,8},{10,9... | collective-permute-start | bytes 811016 | tf_op jit(solution)/shard_map/ppermute | solution.py:26
  55.3 9.5 %collective-permute-start.11 = (bf16[528,256]{1,0:T(8,128)(2,1)S(1)}, bf16[528,256]{1,0:T(8,128)(2,1)S(1)}, u32[]{:S(2)}, u32[]{:S(2)}) collective-permute-start(bf16[528,256]{1,0:T(8,128)(2,1)S(1)} %get-tuple-element.44.second.refs_6_), channel_id=1, source_target_pairs={{0,2},{1,3},{2,0},{3,1},{4,6},{5,7},{6,4},{7,5},{8,10},{9,11},{10,... | collective-permute-start | bytes 811016 | tf_op jit(solution)/shard_map/ppermute | solution.py:26
  57.4 8.5 %collective-permute-start.10 = (bf16[528,256]{1,0:T(8,128)(2,1)S(1)}, bf16[528,256]{1,0:T(8,128)(2,1)S(1)}, u32[]{:S(2)}, u32[]{:S(2)}) collective-permute-start(bf16[528,256]{1,0:T(8,128)(2,1)S(1)} %get-tuple-element.44.second.refs_6_), channel_id=1, source_target_pairs={{0,1},{1,2},{2,3},{3,0},{4,5},{5,6},{6,7},{7,4},{8,9},{9,10},{10,1... | collective-permute-start | bytes 811016 | tf_op jit(solution)/shard_map/ppermute | solution.py:26
  60.1 16.8 %collective-permute-start.13 = (bf16[528,512]{1,0:T(8,128)(2,1)S(1)}, bf16[528,512]{1,0:T(8,128)(2,1)S(1)}, u32[]{:S(2)}, u32[]{:S(2)}) collective-permute-start(bf16[528,512]{1,0:T(8,128)(2,1)S(1)} %weight_terms.6), channel_id=1, source_target_pairs={{0,4},{1,5},{2,6},{3,7},{4,0},{5,1},{6,2},{7,3},{8,12},{9,13},{10,... | collective-permute-start | bytes 1622024 | tf_op jit(solution)/shard_map/ppermute | solution.py:26
  66.6 17.2 %collective-permute-start.14 = (bf16[528,512]{1,0:T(8,128)(2,1)S(1)}, bf16[528,512]{1,0:T(8,128)(2,1)S(1)}, u32[]{:S(2)}, u32[]{:S(2)}) collective-permute-start(bf16[528,512]{1,0:T(8,128)(2,1)S(1)} %weight_terms.7), channel_id=1, source_target_pairs={{0,4},{1,5},{2,6},{3,7},{4,0},{5,1},{6,2},{7,3},{8,12},{9,13},{10,... | collective-permute-start | bytes 1622024 | tf_op jit(solution)/shard_map/ppermute | solution.py:26

commit v3 on v2

--- a/solution.py
+++ b/solution.py
@@ -8,7 +8,8 @@
 from jax.sharding import PartitionSpec as P
 
 ROW = 4
-HALF = 176
+CUT = 176
+PADDED = 352
 STEPS = 4
 MIB = 1 << 20
 
@@ -47,10 +48,10 @@
 
 
 def halves(d_gate, d_up, hidden):
-    pad = jnp.zeros((2 * HALF - d_gate.shape[0], d_gate.shape[1]), jnp.float32)
+    pad = jnp.zeros((PADDED - d_gate.shape[0], d_gate.shape[1]), jnp.float32)
     parts = (d_gate, d_up, hidden)
-    first = jnp.concatenate([p[:HALF] for p in parts])
-    second = jnp.concatenate([q for p in parts for q in (p[HALF:], pad)])
+    first = jnp.concatenate([p[:CUT] for p in parts])
+    second = jnp.concatenate([q for p in parts for q in (p[CUT:], pad)])
     return first.astype(jnp.bfloat16), second.astype(jnp.bfloat16)
 
 
@@ -79,7 +80,7 @@
         own_kernel,
         in_specs=[VMEM] * 5,
         out_specs=[VMEM] * 2,
-        out_shape=[jax.ShapeDtypeStruct((3 * HALF, t), jnp.bfloat16)] * 2,
+        out_shape=[jax.ShapeDtypeStruct((3 * n, t), jnp.bfloat16) for n in (CUT, PADDED - CUT)],
         compiler_params=params(),
         cost_estimate=cost(us),
         name="own_units",
@@ -115,7 +116,7 @@
         far_kernel,
         in_specs=[VMEM] * 6,
         out_specs=[VMEM] * 2,
-        out_shape=[jax.ShapeDtypeStruct((3 * HALF, 2 * c.shape[0]), jnp.bfloat16)] * 2,
+        out_shape=[jax.ShapeDtypeStruct((3 * n, 2 * c.shape[0]), jnp.bfloat16) for n in (CUT, PADDED - CUT)],
         compiler_params=params(),
         cost_estimate=cost(us),
         name="far_units",
@@ -127,8 +128,8 @@
     cols = slice(at, at + out.shape[0])
     grads = []
     for n in range(2):
-        rows = slice(n * HALF, (n + 1) * HALF)
-        grads.append(jnp.concatenate([first[rows, cols], second[rows, cols]])[:s])
+        parts = [a[n * a.shape[0] // 3 : (n + 1) * a.shape[0] // 3, cols] for a in (first, second)]
+        grads.append(jnp.concatenate(parts)[:s])
     for k in range(STEPS):
         cut = slice(k * d // STEPS, (k + 1) * d // STEPS)
         out[:, cut] = (tn(grads[0], wg[:, cut]) + tn(grads[1], wu[:, cut])).astype(out.dtype)
@@ -153,7 +154,7 @@
     copies = []
     for i, out in enumerate(outs):
         for j in range(2):
-            row = lax.rem(me // ROW + j, 2)
+            row = lax.rem(me // ROW + 1 + j, 2)
             to = row * ROW + lax.rem(me + i, ROW)
             source = pl.ds(pl.multiple_of(to * wide, wide), wide)
             for n, a in enumerate((x, c)):
@@ -180,57 +181,56 @@
 
 
 def weight_kernel(at, *refs):
-    near, far, grads, out = refs[:ROW], refs[ROW : ROW + 2], refs[ROW + 2 : -1], refs[-1]
+    near, head, tail, grads, out = refs[:ROW], refs[ROW], refs[ROW + 1], refs[ROW + 2 : -1], refs[-1]
     t = near[0].shape[0]
-    wide = out.shape[1]
+    n, wide = out.shape[0] // 3, out.shape[1]
     left = jnp.concatenate([g[...] for g in grads], 1)
 
     def columns(first):
-        cut = slice(first, first + wide)
-        tall = [a for i in range(ROW) for a in (
-            near[i][:, cut],
-            far[0][:, cut] if i == 0 else far[1][(i - 1) * t : i * t, cut],
-        )]
-        return jnp.concatenate(tall)
+        parts = [near[0][:, at + first : at + first + wide], head[:, at + first : at + first + wide]]
+        for i in range(1, ROW):
+            parts.append(near[i][:, at + first : at + first + wide])
+            parts.append(tail[(i - 1) * t : i * t, first : first + wide])
+        return jnp.concatenate(parts)
 
     dot = functools.partial(jnp.dot, preferred_element_type=jnp.float32)
-    out[: 2 * HALF] = dot(left[: 2 * HALF], columns(at)).astype(out.dtype)
-    out[2 * HALF :] = dot(left[2 * HALF :], columns(at + wide)).astype(out.dtype)
-
-
-def weight_terms(near, far, grads, at, dtype, us):
+    out[: 2 * n] = dot(left[: 2 * n], columns(0)).astype(out.dtype)
+    out[2 * n :] = dot(left[2 * n :], columns(wide)).astype(out.dtype)
+
+
+def weight_terms(near, head, tail, grads, at, dtype, us):
     wide = near[0].shape[1] // 4
     return pl.pallas_call(
         functools.partial(weight_kernel, at * wide),
-        out_shape=jax.ShapeDtypeStruct((3 * HALF, wide), dtype),
+        out_shape=jax.ShapeDtypeStruct((grads[0].shape[0], wide), dtype),
         in_specs=[VMEM] * (2 * ROW + 2),
         out_specs=VMEM,
         compiler_params=params(),
         cost_estimate=cost(us),
         name="weight_terms",
-    )(*near, *far, *grads)
-
-
-def sum_kernel(a, b, a_other, b_other, gate, up, down):
+    )(*near, head, tail, *grads)
+
+
+def sum_kernel(first, second, first_other, second_other, gate, up, down):
     s = gate.shape[0]
     for n, out in enumerate((gate, up, down)):
-        rows = slice(n * HALF, (n + 1) * HALF)
-        total = a[rows] + a_other[rows].astype(jnp.float32)
-        out[:HALF] = total.astype(out.dtype)
-        total = b[rows] + b_other[rows].astype(jnp.float32)
-        out[HALF:] = total[: s - HALF].astype(out.dtype)
-
-
-def sums(a, b, a_other, b_other, s):
+        for a, b, at in ((first, first_other, 0), (second, second_other, CUT)):
+            part = a.shape[0] // 3
+            rows = slice(n * part, (n + 1) * part)
+            total = a[rows] + b[rows].astype(jnp.float32)
+            out[at : min(at + part, s)] = total[: s - at].astype(out.dtype)
+
+
+def sums(first, second, first_other, second_other, s):
     return pl.pallas_call(
         sum_kernel,
-        out_shape=[jax.ShapeDtypeStruct((s, a.shape[1]), jnp.bfloat16)] * 3,
+        out_shape=[jax.ShapeDtypeStruct((s, first.shape[1]), jnp.bfloat16)] * 3,
         in_specs=[VMEM] * 4,
         out_specs=[VMEM] * 3,
         compiler_params=params(),
         cost_estimate=cost(1),
         name="sums",
-    )(a, b, a_other, b_other)
+    )(first, second, first_other, second_other)
 
 
 def local(tokens, cotangent, gate_weight, up_weight, down_weight):
@@ -238,9 +238,10 @@
     s = w_gate.shape[0]
     t = tokens.shape[0]
     far_rows = along_blk(tokens, -1)
-    far_cotan = along_blk(cotangent, -1)
     in_hbm = [pltpu.with_memory_space_constraint(a, pltpu.HBM) for a in (tokens, cotangent)]
-    near = pack(*in_hbm, ROW, 1)
+    near = list(pack(*in_hbm, ROW, 1))
+    late, near[0] = lax.optimization_barrier((cotangent, near[0]))
+    far_cotan = along_blk(late, -1)
     near = [near[0]] + [along_rep(near[i], 0, i) for i in range(1, ROW)]
 
     own = own_units(tokens, cotangent, w_gate, w_up, w_down, 20)
@@ -251,15 +252,18 @@
     both = far_units(far_cotan, w_down, gate, upval, *own, 1.5)
     far_x = row_term(*both, w_gate, w_up, t, t, jnp.bfloat16, 1)
     near, far_x = lax.optimization_barrier((near, far_x))
+    half = near[0].shape[1] // 2
+    far_other = along_blk(jnp.concatenate([a[:, :half] for a in near[1:]]), -1)
     far_x = along_blk(far_x, 1)
-    first, second = both
-    second, far_x = lax.optimization_barrier((second, far_x))
-    gathered = [[g] + [along_rep(g, 0, i) for i in range(1, ROW)] for g in (first, second)]
-    far_cols = along_blk(jnp.concatenate(near[1:]), -1)
-    far = [pack(far_rows, far_cotan, 1, 0.5)[0], far_cols]
-
-    other = [along_rep(weight_terms(near, far, g, 2, jnp.bfloat16, 1), 1, 0) for g in gathered]
-    mine = [weight_terms(near, far, g, 0, jnp.float32, 1) for g in gathered]
+    first, second = ([g] + [along_rep(g, 0, i) for i in (1, 3)] for g in both)
+    first.insert(2, along_rep(first[1], 0, 1))
+    second.insert(2, along_rep(second[2], 0, 3))
+    own_cols = near[1:]
+    far_mine = along_blk(jnp.concatenate([a[:, half:] for a in own_cols]), -1)
+    far = pack(far_rows, far_cotan, 1, 0.5)[0]
+
+    other = [along_rep(weight_terms(near, far, far_other, g, 0, jnp.bfloat16, 1), 1, 0) for g in (first, second)]
+    mine = [weight_terms(near, far, far_mine, g, 2, jnp.float32, 1) for g in (first, second)]
     gate_grad, up_grad, down_grad = sums(*mine, *other, s)
     input_grad = (own_x + far_x.astype(jnp.float32)).astype(jnp.bfloat16)
     return input_grad, gate_grad.T, up_grad.T, down_grad

time: 85.7 us -> 83.4 us (0.973)
  waiting for transfers between devices: 33.6 us -> 27.3 us
  starting transfers between devices: 28.9 us -> 32.6 us
    ppermute x4 -> x5, waiting for transfers between devices: 16.8 us -> 5.88 us  [along_blk(): lax.ppermute(value, 'blk', [(i, (i + by) % size) for i in range(size)])]
    ppermute x4 -> x5, starting transfers between devices: 8.59 us -> 14.3 us  [along_blk(): lax.ppermute(value, 'blk', [(i, (i + by) % size) for i in range(size)])]
    ppermute x11, waiting for transfers between devices: 16.9 us -> 21.4 us  [along_rep(): lax.ppermute(value, 'rep', [(r, partner(r, j, i)) for r in range(2 * ROW)])]
    ppermute x11, starting transfers between devices: 20.4 us -> 18.3 us  [along_rep(): lax.ppermute(value, 'rep', [(r, partner(r, j, i)) for r in range(2 * ROW)])]
  transfers between devices with their start and end apart: 15 -> 16, of which waited for: 7 -> 8; matrix products, arithmetic and copies ran while one was open for 1% -> 1% of each run, Pallas kernels for 14% -> 15%
where the time goes in v3:
time: 83.4 us; the launch traced here: 82.5 us
  starting transfers between devices  32.6 us (39%)
  waiting for transfers between devices  27.3 us (33%)
  Pallas kernels  13.5 us (16%)
  local copies, waits for them, and re-layouts  7.02 us (8%)
  other arithmetic  1.29 us (2%)
    ppermute x11, waiting for transfers between devices, along_rep(): lax.ppermute(value, 'rep', [(r, partner(r, j, i)) for r in range(2 * ROW)])  21.4 us
    ppermute x11, starting transfers between devices, along_rep(): lax.ppermute(value, 'rep', [(r, partner(r, j, i)) for r in range(2 * ROW)])  18.3 us
    ppermute x5, starting transfers between devices, along_blk(): lax.ppermute(value, 'blk', [(i, (i + by) % size) for i in range(size)])  14.3 us
    unnamed x14, local copies, waits for them, and re-layouts  6.92 us
    ppermute x5, waiting for transfers between devices, along_blk(): lax.ppermute(value, 'blk', [(i, (i + by) % size) for i in range(size)])  5.88 us
    pallas_call x4, Pallas kernels, weight_terms(): pl.pallas_call(functools.partial(weight_kernel, at * wide), out_shape=jax...  2.92 us
    pallas_call x2, Pallas kernels, row_term(): pl.pallas_call(functools.partial(term_kernel, at), in_specs=[VMEM] * 4, o...  2.58 us
    pallas_call x1, Pallas kernels, own_units(): pl.pallas_call(own_kernel, in_specs=[VMEM] * 5, out_specs=[VMEM] * 2, out...  2.41 us
  transfers between devices with their start and end apart: 16, of which 8 were waited for; matrix products, arithmetic and copies ran while one was open for 1% of the time, Pallas kernels for 15%

profile of v3, /device:TPU:2, one launch (start us, length us, event | category | flops | bytes accessed | tf_op | source)
XLA Modules:
  0.0 82.5 jit_solution(6592659533808109945)
XLA Ops:
  0.6 6.4 %collective-permute-start = (bf16[128,4096]{1,0:T(8,128)(2,1)}, bf16[128,4096]{1,0:T(8,128)(2,1)S(1)}, u32[]{:S(2)}, u32[]{:S(2)}) collective-permute-start(bf16[128,4096]{1,0:T(8,128)(2,1)} %x.3), channel_id=1, source_target_pairs={{0,248},{8,0},{16,8},{24,16},{32,24},{40,32},{48,40},{56,48},{64,5... | collective-permute-start | bytes 3145736 | tf_op jit(solution)/shard_map/ppermute | solution.py:19
  7.0 1.7 %pack.2 = (bf16[128,2048]{1,0:T(8,128)(2,1)S(1)}, bf16[128,2048]{1,0:T(8,128)(2,1)S(1)}, bf16[128,2048]{1,0:T(8,128)(2,1)S(1)}, bf16[128,2048]{1,0:T(8,128)(2,1)S(1)}) custom-call(bf16[128,4096]{1,0:T(8,128)(2,1)} %x.3, bf16[128,4096]{1,0:T(8,128)(2,1)} %c.3), custom_call_target="tpu_custom_call" | custom-call | flops 1000000000 | bytes 3500000 | tf_op jit(solution)/shard_map/pack/pallas_call | solution.py:171
  8.8 1.6 %collective-permute-start.1 = (bf16[128,2048]{1,0:T(8,128)(2,1)S(1)}, bf16[128,2048]{1,0:T(8,128)(2,1)S(1)}, u32[]{:S(2)}, u32[]{:S(2)}) collective-permute-start(bf16[128,2048]{1,0:T(8,128)(2,1)S(1)} %get-tuple-element.31), channel_id=1, source_target_pairs={{0,1},{1,2},{2,3},{3,0},{4,5},{5,6},{6,7},{7,4},{8,9},{9,10},{10,1... | collective-permute-start | bytes 1572872 | tf_op jit(solution)/shard_map/ppermute | solution.py:27
  10.3 1.1 %collective-permute-start.2 = (bf16[128,2048]{1,0:T(8,128)(2,1)S(1)}, bf16[128,2048]{1,0:T(8,128)(2,1)S(1)}, u32[]{:S(2)}, u32[]{:S(2)}) collective-permute-start(bf16[128,2048]{1,0:T(8,128)(2,1)S(1)} %get-tuple-element.32), channel_id=1, source_target_pairs={{0,2},{1,3},{2,0},{3,1},{4,6},{5,7},{6,4},{7,5},{8,10},{9,11},{10,... | collective-permute-start | bytes 1572872 | tf_op jit(solution)/shard_map/ppermute | solution.py:27
  11.5 2.2 %collective-permute-start.3 = (bf16[128,2048]{1,0:T(8,128)(2,1)S(1)}, bf16[128,2048]{1,0:T(8,128)(2,1)S(1)}, u32[]{:S(2)}, u32[]{:S(2)}) collective-permute-start(bf16[128,2048]{1,0:T(8,128)(2,1)S(1)} %get-tuple-element.33), channel_id=1, source_target_pairs={{0,3},{1,0},{2,1},{3,2},{4,7},{5,4},{6,5},{7,6},{8,11},{9,8},{10,9... | collective-permute-start | bytes 1572872 | tf_op jit(solution)/shard_map/ppermute | solution.py:27
  13.6 1.8 %copy-done.1 = bf16[4096,344]{0,1:T(8,128)(2,1)S(1)} copy-done((bf16[4096,344]{0,1:T(8,128)(2,1)S(1)}, bf16[4096,344]{0,1:T(8,128)(2,1)}, u32[]{:S(2)}) %copy-start.1) | copy-done | bytes 2818072
  15.4 1.8 %copy-done.3 = bf16[344,4096]{1,0:T(8,128)(2,1)S(1)} copy-done((bf16[344,4096]{1,0:T(8,128)(2,1)S(1)}, bf16[344,4096]{1,0:T(8,128)(2,1)}, u32[]{:S(2)}) %copy-start.3) | copy-done | bytes 2818072
  17.2 1.2 %copy-done.5 = bf16[128,4096]{1,0:T(8,128)(2,1)S(1)} copy-done((bf16[128,4096]{1,0:T(8,128)(2,1)S(1)}, bf16[128,4096]{1,0:T(8,128)(2,1)}, u32[]{:S(2)}) %copy-start.5) | copy-done | bytes 1048600
  18.4 1.2 %copy-done.6 = bf16[128,4096]{1,0:T(8,128)(2,1)S(1)} copy-done((bf16[128,4096]{1,0:T(8,128)(2,1)S(1)}, bf16[128,4096]{1,0:T(8,128)(2,1)}, u32[]{:S(2)}) %copy-start.6) | copy-done | bytes 1048600
  19.7 2.4 %own_units.1 = (bf16[528,128]{1,0:T(8,128)(2,1)S(1)}, bf16[528,128]{1,0:T(8,128)(2,1)S(1)}) custom-call(bf16[128,4096]{1,0:T(8,128)(2,1)S(1)} %copy-done.5, bf16[128,4096]{1,0:T(8,128)(2,1)S(1)} %copy-done.6, bf16[344,4096]{1,0:T(8,128)(2,1)S(1)} %bitcast.4, bf16[344,4096]{1,0:T(8,128)(2,1)S(1)} %bitcast.8, bf16[344,4096]{1,0:T(8,128)(2,1)S(1)} %copy-done.3), custom_call_target="tpu_custom_call" | custom-call | flops 20000000000 | bytes 70000000 | tf_op jit(solution)/shard_map/own_units/pallas_call | solution.py:79
  22.1 1.3 %row_term.2 = f32[128,4096]{1,0:T(8,128)S(1)} custom-call(bf16[528,128]{1,0:T(8,128)(2,1)S(1)} %get-tuple-element.26.first.own_first, bf16[528,128]{1,0:T(8,128)(2,1)S(1)} %get-tuple-element.27.second.own_second, bf16[344,4096]{1,0:T(8,128)(2,1)S(1)} %bitcast.5, bf16[344,4096]{1,0:T(8,128)(2,1)S(1)} %bitcast.9), custom_call_target="tpu_custom_call" | custom-call | flops 3000000000 | bytes 10500000 | tf_op jit(solution)/shard_map/row_term/pallas_call | solution.py:139
  23.4 1.6 %gate_up.1 = (f32[344,128]{1,0:T(8,128)S(1)}, f32[344,128]{1,0:T(8,128)S(1)}) custom-call(bf16[128,4096]{1,0:T(8,128)(2,1)S(1)} %collective-permute-done.x, bf16[344,4096]{1,0:T(8,128)(2,1)S(1)} %bitcast.6, bf16[344,4096]{1,0:T(8,128)(2,1)S(1)} %bitcast.10), custom_call_target="tpu_custom_call" | custom-call | flops 2000000000 | bytes 7000000 | tf_op jit(solution)/shard_map/gate_up/pallas_call | solution.py:96
  25.0 5.9 %collective-permute-done.4.c = bf16[128,4096]{1,0:T(8,128)(2,1)S(1)} collective-permute-done((bf16[128,4096]{1,0:T(8,128)(2,1)}, bf16[128,4096]{1,0:T(8,128)(2,1)S(1)}, u32[]{:S(2)}, u32[]{:S(2)}) %collective-permute-start.4) | collective-permute-done | bytes 1048608 | tf_op jit(solution)/shard_map/ppermute | solution.py:19
  30.9 0.9 %far_units.1 = (bf16[528,256]{1,0:T(8,128)(2,1)S(1)}, bf16[528,256]{1,0:T(8,128)(2,1)S(1)}) custom-call(bf16[128,4096]{1,0:T(8,128)(2,1)S(1)} %collective-permute-done.4.c, bf16[344,4096]{1,0:T(8,128)(2,1)S(1)} %copy-done.4, f32[344,128]{1,0:T(8,128)S(1)} %get-tuple-element.36.gate, f32[344,128]{1,0:T(8,128)S(1)} %get-tuple-element.37.upval, ...), custom_call_target="tpu_custom_call" | custom-call | flops 1500000000 | bytes 5250000 | tf_op jit(solution)/shard_map/far_units/pallas_call | solution.py:115
  32.7 1.3 %row_term.3 = bf16[128,4096]{1,0:T(8,128)(2,1)S(1)} custom-call(bf16[528,256]{1,0:T(8,128)(2,1)S(1)} %get-tuple-element.38.first.refs_6_, bf16[528,256]{1,0:T(8,128)(2,1)S(1)} %get-tuple-element.39.second.refs_6_, bf16[344,4096]{1,0:T(8,128)(2,1)S(1)} %bitcast.7, bf16[344,4096]{1,0:T(8,128)(2,1)S(1)} %bitcast.11), custom_call_target="tpu_custom_call" | custom-call | flops 1000000000 | bytes 3500000 | tf_op jit(solution)/shard_map/row_term/pallas_call | solution.py:139
  34.2 4.0 %collective-permute-start.13 = (bf16[384,1024]{1,0:T(8,128)(2,1)S(1)}, bf16[384,1024]{1,0:T(8,128)(2,1)S(1)}, u32[]{:S(2)}, u32[]{:S(2)}) collective-permute-start(bf16[384,1024]{1,0:T(8,128)(2,1)S(1)} %pad_maximum_fusion.1), channel_id=1, source_target_pairs={{0,248},{8,0},{16,8},{24,16},{32,24},{40,32},{48,40},{56,48},{64,5... | collective-permute-start | bytes 2359304 | tf_op jit(solution)/shard_map/ppermute | solution.py:19
  38.2 1.5 %collective-permute-start.7 = (bf16[528,256]{1,0:T(8,128)(2,1)S(1)}, bf16[528,256]{1,0:T(8,128)(2,1)S(1)}, u32[]{:S(2)}, u32[]{:S(2)}) collective-permute-start(bf16[528,256]{1,0:T(8,128)(2,1)S(1)} %get-tuple-element.38.first.refs_6_), channel_id=1, source_target_pairs={{0,1},{1,2},{2,3},{3,0},{4,5},{5,6},{6,7},{7,4},{8,9},{9,10},{10,1... | collective-permute-start | bytes 811016 | tf_op jit(solution)/shard_map/ppermute | solution.py:27
  40.3 3.9 %collective-permute-start.6 = (bf16[384,1024]{1,0:T(8,128)(2,1)S(1)}, bf16[384,1024]{1,0:T(8,128)(2,1)S(1)}, u32[]{:S(2)}, u32[]{:S(2)}) collective-permute-start(bf16[384,1024]{1,0:T(8,128)(2,1)S(1)} %pad_maximum_fusion), channel_id=1, source_target_pairs={{0,248},{8,0},{16,8},{24,16},{32,24},{40,32},{48,40},{56,48},{64,5... | collective-permute-start | bytes 2359304 | tf_op jit(solution)/shard_map/ppermute | solution.py:19
  44.6 2.1 %collective-permute-start.11 = (bf16[528,256]{1,0:T(8,128)(2,1)S(1)}, bf16[528,256]{1,0:T(8,128)(2,1)S(1)}, u32[]{:S(2)}, u32[]{:S(2)}) collective-permute-start(bf16[528,256]{1,0:T(8,128)(2,1)S(1)} %get-tuple-element.39.second.refs_6_), channel_id=1, source_target_pairs={{0,3},{1,0},{2,1},{3,2},{4,7},{5,4},{6,5},{7,6},{8,11},{9,8},{10,9... | collective-permute-start | bytes 811016 | tf_op jit(solution)/shard_map/ppermute | solution.py:27
  46.7 2.1 %collective-permute-done.9.refs_9_ = bf16[528,256]{1,0:T(8,128)(2,1)S(1)} collective-permute-done((bf16[528,256]{1,0:T(8,128)(2,1)S(1)}, bf16[528,256]{1,0:T(8,128)(2,1)S(1)}, u32[]{:S(2)}, u32[]{:S(2)}) %collective-permute-start.9) | collective-permute-done | bytes 270368 | tf_op jit(solution)/shard_map/ppermute | solution.py:27
  48.8 1.0 %collective-permute-start.8 = (bf16[528,256]{1,0:T(8,128)(2,1)S(1)}, bf16[528,256]{1,0:T(8,128)(2,1)S(1)}, u32[]{:S(2)}, u32[]{:S(2)}) collective-permute-start(bf16[528,256]{1,0:T(8,128)(2,1)S(1)} %collective-permute-done.7.refs_7_), channel_id=1, source_target_pairs={{0,1},{1,2},{2,3},{3,0},{4,5},{5,6},{6,7},{7,4},{8,9},{9,10},{10,1... | collective-permute-start | bytes 811016 | tf_op jit(solution)/shard_map/ppermute | solution.py:27
  49.8 2.1 %collective-permute-done.11.refs_9_ = bf16[528,256]{1,0:T(8,128)(2,1)S(1)} collective-permute-done((bf16[528,256]{1,0:T(8,128)(2,1)S(1)}, bf16[528,256]{1,0:T(8,128)(2,1)S(1)}, u32[]{:S(2)}, u32[]{:S(2)}) %collective-permute-start.11) | collective-permute-done | bytes 270368 | tf_op jit(solution)/shard_map/ppermute | solution.py:27
  51.9 1.2 %collective-permute-start.10 = (bf16[528,256]{1,0:T(8,128)(2,1)S(1)}, bf16[528,256]{1,0:T(8,128)(2,1)S(1)}, u32[]{:S(2)}, u32[]{:S(2)}) collective-permute-start(bf16[528,256]{1,0:T(8,128)(2,1)S(1)} %get-tuple-element.39.second.refs_6_), channel_id=1, source_target_pairs={{0,1},{1,2},{2,3},{3,0},{4,5},{5,6},{6,7},{7,4},{8,9},{9,10},{10,1... | collective-permute-start | bytes 811016 | tf_op jit(solution)/shard_map/ppermute | solution.py:27
  53.1 4.6 %collective-permute-done.8.refs_8_ = bf16[528,256]{1,0:T(8,128)(2,1)S(1)} collective-permute-done((bf16[528,256]{1,0:T(8,128)(2,1)S(1)}, bf16[528,256]{1,0:T(8,128)(2,1)S(1)}, u32[]{:S(2)}, u32[]{:S(2)}) %collective-permute-start.8) | collective-permute-done | bytes 270368 | tf_op jit(solution)/shard_map/ppermute | solution.py:27
  57.7 1.2 %collective-permute-start.12 = (bf16[528,256]{1,0:T(8,128)(2,1)S(1)}, bf16[528,256]{1,0:T(8,128)(2,1)S(1)}, u32[]{:S(2)}, u32[]{:S(2)}) collective-permute-start(bf16[528,256]{1,0:T(8,128)(2,1)S(1)} %collective-permute-done.11.refs_9_), channel_id=1, source_target_pairs={{0,3},{1,0},{2,1},{3,2},{4,7},{5,4},{6,5},{7,6},{8,11},{9,8},{10,9... | collective-permute-start | bytes 811016 | tf_op jit(solution)/shard_map/ppermute | solution.py:27
  59.9 2.9 %collective-permute-start.14 = (bf16[528,512]{1,0:T(8,128)(2,1)S(1)}, bf16[528,512]{1,0:T(8,128)(2,1)S(1)}, u32[]{:S(2)}, u32[]{:S(2)}) collective-permute-start(bf16[528,512]{1,0:T(8,128)(2,1)S(1)} %weight_terms.6), channel_id=1, source_target_pairs={{0,4},{1,5},{2,6},{3,7},{4,0},{5,1},{6,2},{7,3},{8,12},{9,13},{10,... | collective-permute-start | bytes 1622024 | tf_op jit(solution)/shard_map/ppermute | solution.py:27
  62.8 1.4 %collective-permute-done.12.refs_8_ = bf16[528,256]{1,0:T(8,128)(2,1)S(1)} collective-permute-done((bf16[528,256]{1,0:T(8,128)(2,1)S(1)}, bf16[528,256]{1,0:T(8,128)(2,1)S(1)}, u32[]{:S(2)}, u32[]{:S(2)}) %collective-permute-start.12) | collective-permute-done | bytes 270368 | tf_op jit(solution)/shard_map/ppermute | solution.py:27
  64.9 3.0 %collective-permute-start.15 = (bf16[528,512]{1,0:T(8,128)(2,1)S(1)}, bf16[528,512]{1,0:T(8,128)(2,1)S(1)}, u32[]{:S(2)}, u32[]{:S(2)}) collective-permute-start(bf16[528,512]{1,0:T(8,128)(2,1)S(1)} %weight_terms.7), channel_id=1, source_target_pairs={{0,4},{1,5},{2,6},{3,7},{4,0},{5,1},{6,2},{7,3},{8,12},{9,13},{10,... | collective-permute-start | bytes 1622024 | tf_op jit(solution)/shard_map/ppermute | solution.py:27
  69.4 1.2 %add_convert_fusion = bf16[128,4096]{1,0:T(8,128)(2,1)} fusion(f32[128,4096]{1,0:T(8,128)S(1)} %row_term.2, bf16[128,4096]{1,0:T(8,128)(2,1)S(1)} %collective-permute-done.5), kind=kLoop, calls=%fused_computation | loop fusion | flops 1572864 | bytes 4194304 | tf_op jit(solution)/shard_map/convert_element_type | solution.py:268
  70.6 4.9 %collective-permute-done.14.first_other = bf16[528,512]{1,0:T(8,128)(2,1)S(1)} collective-permute-done((bf16[528,512]{1,0:T(8,128)(2,1)S(1)}, bf16[528,512]{1,0:T(8,128)(2,1)S(1)}, u32[]{:S(2)}, u32[]{:S(2)}) %collective-permute-start.14) | collective-permute-done | bytes 540704 | tf_op jit(solution)/shard_map/ppermute | solution.py:27
  75.5 5.8 %collective-permute-done.15.second_other = bf16[528,512]{1,0:T(8,128)(2,1)S(1)} collective-permute-done((bf16[528,512]{1,0:T(8,128)(2,1)S(1)}, bf16[528,512]{1,0:T(8,128)(2,1)S(1)}, u32[]{:S(2)}, u32[]{:S(2)}) %collective-permute-start.15) | collective-permute-done | bytes 540704 | tf_op jit(solution)/shard_map/ppermute | solution.py:27
  81.3 1.1 %sums.1 = (bf16[344,512]{1,0:T(8,128)(2,1)}, bf16[344,512]{1,0:T(8,128)(2,1)}, bf16[344,512]{1,0:T(8,128)(2,1)}) custom-call(f32[528,512]{1,0:T(8,128)S(1)} %weight_terms.4.first, f32[528,512]{1,0:T(8,128)S(1)} %weight_terms.5.second, bf16[528,512]{1,0:T(8,128)(2,1)S(1)} %collective-permute-done.14.first_other, ...), custom_call_target="tpu_custom_call" | custom-call | flops 1000000000 | bytes 3500000 | tf_op jit(solution)/shard_map/sums/pallas_call | solution.py:225
  (31 shorter events, 5.1 us)
Async XLA Ops:
  0.6 13.0 %copy-start = (bf16[4096,344]{0,1:T(8,128)(2,1)S(1)}, bf16[4096,344]{0,1:T(8,128)(2,1)}, u32[]{:S(2)}) copy-start(bf16[4096,344]{0,1:T(8,128)(2,1)} %param.7) | copy-start | bytes 8454148
  0.6 22.7 %collective-permute-start = (bf16[128,4096]{1,0:T(8,128)(2,1)}, bf16[128,4096]{1,0:T(8,128)(2,1)S(1)}, u32[]{:S(2)}, u32[]{:S(2)}) collective-permute-start(bf16[128,4096]{1,0:T(8,128)(2,1)} %x.3), channel_id=1, source_target_pairs={{0,248},{8,0},{16,8},{24,16},{32,24},{40,32},{48,40},{56,48},{64,5... | collective-permute-start | bytes 3145736 | tf_op jit(solution)/shard_map/ppermute | solution.py:19
  8.8 25.2 %collective-permute-start.1 = (bf16[128,2048]{1,0:T(8,128)(2,1)S(1)}, bf16[128,2048]{1,0:T(8,128)(2,1)S(1)}, u32[]{:S(2)}, u32[]{:S(2)}) collective-permute-start(bf16[128,2048]{1,0:T(8,128)(2,1)S(1)} %get-tuple-element.31), channel_id=1, source_target_pairs={{0,1},{1,2},{2,3},{3,0},{4,5},{5,6},{6,7},{7,4},{8,9},{9,10},{10,1... | collective-permute-start | bytes 1572872 | tf_op jit(solution)/shard_map/ppermute | solution.py:27
  10.3 23.7 %collective-permute-start.2 = (bf16[128,2048]{1,0:T(8,128)(2,1)S(1)}, bf16[128,2048]{1,0:T(8,128)(2,1)S(1)}, u32[]{:S(2)}, u32[]{:S(2)}) collective-permute-start(bf16[128,2048]{1,0:T(8,128)(2,1)S(1)} %get-tuple-element.32), channel_id=1, source_target_pairs={{0,2},{1,3},{2,0},{3,1},{4,6},{5,7},{6,4},{7,5},{8,10},{9,11},{10,... | collective-permute-start | bytes 1572872 | tf_op jit(solution)/shard_map/ppermute | solution.py:27
  11.5 22.6 %collective-permute-start.3 = (bf16[128,2048]{1,0:T(8,128)(2,1)S(1)}, bf16[128,2048]{1,0:T(8,128)(2,1)S(1)}, u32[]{:S(2)}, u32[]{:S(2)}) collective-permute-start(bf16[128,2048]{1,0:T(8,128)(2,1)S(1)} %get-tuple-element.33), channel_id=1, source_target_pairs={{0,3},{1,0},{2,1},{3,2},{4,7},{5,4},{6,5},{7,6},{8,11},{9,8},{10,9... | collective-permute-start | bytes 1572872 | tf_op jit(solution)/shard_map/ppermute | solution.py:27
  13.6 17.3 %collective-permute-start.4 = (bf16[128,4096]{1,0:T(8,128)(2,1)}, bf16[128,4096]{1,0:T(8,128)(2,1)S(1)}, u32[]{:S(2)}, u32[]{:S(2)}) collective-permute-start(bf16[128,4096]{1,0:T(8,128)(2,1)} %c.3), channel_id=1, source_target_pairs={{0,248},{8,0},{16,8},{24,16},{32,24},{40,32},{48,40},{56,48},{64,5... | collective-permute-start | bytes 3145736 | tf_op jit(solution)/shard_map/ppermute | solution.py:19
  13.6 1.8 %copy-start.1 = (bf16[4096,344]{0,1:T(8,128)(2,1)S(1)}, bf16[4096,344]{0,1:T(8,128)(2,1)}, u32[]{:S(2)}) copy-start(bf16[4096,344]{0,1:T(8,128)(2,1)} %param.8) | copy-start | bytes 8454148
  15.4 1.8 %copy-start.3 = (bf16[344,4096]{1,0:T(8,128)(2,1)S(1)}, bf16[344,4096]{1,0:T(8,128)(2,1)}, u32[]{:S(2)}) copy-start(bf16[344,4096]{1,0:T(8,128)(2,1)} %wd.3) | copy-start | bytes 8454148
  17.2 1.2 %copy-start.5 = (bf16[128,4096]{1,0:T(8,128)(2,1)S(1)}, bf16[128,4096]{1,0:T(8,128)(2,1)}, u32[]{:S(2)}) copy-start(bf16[128,4096]{1,0:T(8,128)(2,1)} %x.3) | copy-start | bytes 3145732
  18.4 1.2 %copy-start.6 = (bf16[128,4096]{1,0:T(8,128)(2,1)S(1)}, bf16[128,4096]{1,0:T(8,128)(2,1)}, u32[]{:S(2)}) copy-start(bf16[128,4096]{1,0:T(8,128)(2,1)} %c.3) | copy-start | bytes 3145732
  23.4 7.5 %copy-start.4 = (bf16[344,4096]{1,0:T(8,128)(2,1)S(1)}, bf16[344,4096]{1,0:T(8,128)(2,1)}, u32[]{:S(2)}) copy-start(bf16[344,4096]{1,0:T(8,128)(2,1)} %wd.3) | copy-start | bytes 8454148
  30.9 1.8 %copy-start.2 = (bf16[4096,344]{0,1:T(8,128)(2,1)S(1)}, bf16[4096,344]{0,1:T(8,128)(2,1)}, u32[]{:S(2)}) copy-start(bf16[4096,344]{0,1:T(8,128)(2,1)} %param.8) | copy-start | bytes 8454148
  34.2 24.9 %collective-permute-start.13 = (bf16[384,1024]{1,0:T(8,128)(2,1)S(1)}, bf16[384,1024]{1,0:T(8,128)(2,1)S(1)}, u32[]{:S(2)}, u32[]{:S(2)}) collective-permute-start(bf16[384,1024]{1,0:T(8,128)(2,1)S(1)} %pad_maximum_fusion.1), channel_id=1, source_target_pairs={{0,248},{8,0},{16,8},{24,16},{32,24},{40,32},{48,40},{56,48},{64,5... | collective-permute-start | bytes 2359304 | tf_op jit(solution)/shard_map/ppermute | solution.py:19
  38.2 6.5 %collective-permute-start.7 = (bf16[528,256]{1,0:T(8,128)(2,1)S(1)}, bf16[528,256]{1,0:T(8,128)(2,1)S(1)}, u32[]{:S(2)}, u32[]{:S(2)}) collective-permute-start(bf16[528,256]{1,0:T(8,128)(2,1)S(1)} %get-tuple-element.38.first.refs_6_), channel_id=1, source_target_pairs={{0,1},{1,2},{2,3},{3,0},{4,5},{5,6},{6,7},{7,4},{8,9},{9,10},{10,1... | collective-permute-start | bytes 811016 | tf_op jit(solution)/shard_map/ppermute | solution.py:27
  39.7 9.1 %collective-permute-start.9 = (bf16[528,256]{1,0:T(8,128)(2,1)S(1)}, bf16[528,256]{1,0:T(8,128)(2,1)S(1)}, u32[]{:S(2)}, u32[]{:S(2)}) collective-permute-start(bf16[528,256]{1,0:T(8,128)(2,1)S(1)} %get-tuple-element.38.first.refs_6_), channel_id=1, source_target_pairs={{0,3},{1,0},{2,1},{3,2},{4,7},{5,4},{6,5},{7,6},{8,11},{9,8},{10,9... | collective-permute-start | bytes 811016 | tf_op jit(solution)/shard_map/ppermute | solution.py:27
  40.2 29.2 %collective-permute-start.5 = (bf16[128,4096]{1,0:T(8,128)(2,1)S(1)}, bf16[128,4096]{1,0:T(8,128)(2,1)S(1)}, u32[]{:S(2)}, u32[]{:S(2)}) collective-permute-start(bf16[128,4096]{1,0:T(8,128)(2,1)S(1)} %row_term.3), channel_id=1, source_target_pairs={{0,8},{8,16},{16,24},{24,32},{32,40},{40,48},{48,56},{56,64},{64,7... | collective-permute-start | bytes 3145736 | tf_op jit(solution)/shard_map/ppermute | solution.py:19
  40.3 27.7 %collective-permute-start.6 = (bf16[384,1024]{1,0:T(8,128)(2,1)S(1)}, bf16[384,1024]{1,0:T(8,128)(2,1)S(1)}, u32[]{:S(2)}, u32[]{:S(2)}) collective-permute-start(bf16[384,1024]{1,0:T(8,128)(2,1)S(1)} %pad_maximum_fusion), channel_id=1, source_target_pairs={{0,248},{8,0},{16,8},{24,16},{32,24},{40,32},{48,40},{56,48},{64,5... | collective-permute-start | bytes 2359304 | tf_op jit(solution)/shard_map/ppermute | solution.py:19
  44.6 7.3 %collective-permute-start.11 = (bf16[528,256]{1,0:T(8,128)(2,1)S(1)}, bf16[528,256]{1,0:T(8,128)(2,1)S(1)}, u32[]{:S(2)}, u32[]{:S(2)}) collective-permute-start(bf16[528,256]{1,0:T(8,128)(2,1)S(1)} %get-tuple-element.39.second.refs_6_), channel_id=1, source_target_pairs={{0,3},{1,0},{2,1},{3,2},{4,7},{5,4},{6,5},{7,6},{8,11},{9,8},{10,9... | collective-permute-start | bytes 811016 | tf_op jit(solution)/shard_map/ppermute | solution.py:27
  48.8 8.9 %collective-permute-start.8 = (bf16[528,256]{1,0:T(8,128)(2,1)S(1)}, bf16[528,256]{1,0:T(8,128)(2,1)S(1)}, u32[]{:S(2)}, u32[]{:S(2)}) collective-permute-start(bf16[528,256]{1,0:T(8,128)(2,1)S(1)} %collective-permute-done.7.refs_7_), channel_id=1, source_target_pairs={{0,1},{1,2},{2,3},{3,0},{4,5},{5,6},{6,7},{7,4},{8,9},{9,10},{10,1... | collective-permute-start | bytes 811016 | tf_op jit(solution)/shard_map/ppermute | solution.py:27
  51.9 10.9 %collective-permute-start.10 = (bf16[528,256]{1,0:T(8,128)(2,1)S(1)}, bf16[528,256]{1,0:T(8,128)(2,1)S(1)}, u32[]{:S(2)}, u32[]{:S(2)}) collective-permute-start(bf16[528,256]{1,0:T(8,128)(2,1)S(1)} %get-tuple-element.39.second.refs_6_), channel_id=1, source_target_pairs={{0,1},{1,2},{2,3},{3,0},{4,5},{5,6},{6,7},{7,4},{8,9},{9,10},{10,1... | collective-permute-start | bytes 811016 | tf_op jit(solution)/shard_map/ppermute | solution.py:27
  57.7 6.5 %collective-permute-start.12 = (bf16[528,256]{1,0:T(8,128)(2,1)S(1)}, bf16[528,256]{1,0:T(8,128)(2,1)S(1)}, u32[]{:S(2)}, u32[]{:S(2)}) collective-permute-start(bf16[528,256]{1,0:T(8,128)(2,1)S(1)} %collective-permute-done.11.refs_9_), channel_id=1, source_target_pairs={{0,3},{1,0},{2,1},{3,2},{4,7},{5,4},{6,5},{7,6},{8,11},{9,8},{10,9... | collective-permute-start | bytes 811016 | tf_op jit(solution)/shard_map/ppermute | solution.py:27
  59.9 15.7 %collective-permute-start.14 = (bf16[528,512]{1,0:T(8,128)(2,1)S(1)}, bf16[528,512]{1,0:T(8,128)(2,1)S(1)}, u32[]{:S(2)}, u32[]{:S(2)}) collective-permute-start(bf16[528,512]{1,0:T(8,128)(2,1)S(1)} %weight_terms.6), channel_id=1, source_target_pairs={{0,4},{1,5},{2,6},{3,7},{4,0},{5,1},{6,2},{7,3},{8,12},{9,13},{10,... | collective-permute-start | bytes 1622024 | tf_op jit(solution)/shard_map/ppermute | solution.py:27
  64.9 16.4 %collective-permute-start.15 = (bf16[528,512]{1,0:T(8,128)(2,1)S(1)}, bf16[528,512]{1,0:T(8,128)(2,1)S(1)}, u32[]{:S(2)}, u32[]{:S(2)}) collective-permute-start(bf16[528,512]{1,0:T(8,128)(2,1)S(1)} %weight_terms.7), channel_id=1, source_target_pairs={{0,4},{1,5},{2,6},{3,7},{4,0},{5,1},{6,2},{7,3},{8,12},{9,13},{10,... | collective-permute-start | bytes 1622024 | tf_op jit(solution)/shard_map/ppermute | solution.py:27

commit v4 on v3

--- a/solution.py
+++ b/solution.py
@@ -9,7 +9,6 @@
 
 ROW = 4
 CUT = 176
-PADDED = 352
 STEPS = 4
 MIB = 1 << 20
 
@@ -48,10 +47,9 @@
 
 
 def halves(d_gate, d_up, hidden):
-    pad = jnp.zeros((PADDED - d_gate.shape[0], d_gate.shape[1]), jnp.float32)
     parts = (d_gate, d_up, hidden)
     first = jnp.concatenate([p[:CUT] for p in parts])
-    second = jnp.concatenate([q for p in parts for q in (p[CUT:], pad)])
+    second = jnp.concatenate([p[CUT:] for p in parts])
     return first.astype(jnp.bfloat16), second.astype(jnp.bfloat16)
 
 
@@ -80,7 +78,7 @@
         own_kernel,
         in_specs=[VMEM] * 5,
         out_specs=[VMEM] * 2,
-        out_shape=[jax.ShapeDtypeStruct((3 * n, t), jnp.bfloat16) for n in (CUT, PADDED - CUT)],
+        out_shape=[jax.ShapeDtypeStruct((3 * n, t), jnp.bfloat16) for n in (CUT, wg.shape[0] - CUT)],
         compiler_params=params(),
         cost_estimate=cost(us),
         name="own_units",
@@ -104,19 +102,26 @@
     )(x, wg, wu)
 
 
-def far_kernel(c, wd, gate, upval, own_first, own_second, first, second):
+def far_kernel(c, wd, gate, upval, own_first, own_second, first, second, both):
     t = c.shape[0]
+    far = unit_grads(gate[...], upval[...], deep(wd, c))
     first[:, :t] = own_first[...]
+    first[:, t:] = far[0]
     second[:, :t] = own_second[...]
-    first[:, t:], second[:, t:] = unit_grads(gate[...], upval[...], deep(wd, c))
+    second[:, t:] = far[1]
+    both[: 3 * CUT] = first[...]
+    both[3 * CUT :] = second[...]
 
 
 def far_units(c, wd, gate, upval, own_first, own_second, us):
     return pl.pallas_call(
         far_kernel,
         in_specs=[VMEM] * 6,
-        out_specs=[VMEM] * 2,
-        out_shape=[jax.ShapeDtypeStruct((3 * n, 2 * c.shape[0]), jnp.bfloat16) for n in (CUT, PADDED - CUT)],
+        out_specs=[VMEM] * 3,
+        out_shape=[
+            jax.ShapeDtypeStruct((3 * n, 2 * c.shape[0]), jnp.bfloat16)
+            for n in (CUT, wd.shape[0] - CUT, wd.shape[0])
+        ],
         compiler_params=params(),
         cost_estimate=cost(us),
         name="far_units",
@@ -126,10 +131,11 @@
 def term_kernel(at, first, second, wg, wu, out):
     s, d = wg.shape
     cols = slice(at, at + out.shape[0])
+    wide = [a[:, cols].astype(jnp.float32) for a in (first, second)]
     grads = []
     for n in range(2):
-        parts = [a[n * a.shape[0] // 3 : (n + 1) * a.shape[0] // 3, cols] for a in (first, second)]
-        grads.append(jnp.concatenate(parts)[:s])
+        parts = [a[n * a.shape[0] // 3 : (n + 1) * a.shape[0] // 3] for a in wide]
+        grads.append(jnp.concatenate(parts).astype(jnp.bfloat16))
     for k in range(STEPS):
         cut = slice(k * d // STEPS, (k + 1) * d // STEPS)
         out[:, cut] = (tn(grads[0], wg[:, cut]) + tn(grads[1], wu[:, cut])).astype(out.dtype)
@@ -147,12 +153,12 @@
     )(first, second, wg, wu)
 
 
-def pack_kernel(x, c, *refs):
+def pack_kernel(first, x, c, *refs):
     outs, sem = refs[:-1], refs[-1]
     me = lax.axis_index("rep")
     wide = x.shape[1] // (2 * ROW)
     copies = []
-    for i, out in enumerate(outs):
+    for i, out in enumerate(outs, first):
         for j in range(2):
             row = lax.rem(me // ROW + 1 + j, 2)
             to = row * ROW + lax.rem(me + i, ROW)
@@ -166,10 +172,10 @@
         copy.wait()
 
 
-def pack(x, c, pieces, us):
+def pack(x, c, first, pieces, us):
     t, d = x.shape
     return pl.pallas_call(
-        pack_kernel,
+        functools.partial(pack_kernel, first),
         out_shape=[jax.ShapeDtypeStruct((t, d // 2), jnp.bfloat16)] * pieces,
         in_specs=[pl.BlockSpec(memory_space=pl.ANY)] * 2,
         out_specs=[pl.BlockSpec(memory_space=pl.ANY)] * pieces,
@@ -212,13 +218,11 @@
 
 
 def sum_kernel(first, second, first_other, second_other, gate, up, down):
-    s = gate.shape[0]
-    for n, out in enumerate((gate, up, down)):
-        for a, b, at in ((first, first_other, 0), (second, second_other, CUT)):
-            part = a.shape[0] // 3
-            rows = slice(n * part, (n + 1) * part)
-            total = a[rows] + b[rows].astype(jnp.float32)
-            out[at : min(at + part, s)] = total[: s - at].astype(out.dtype)
+    for a, b, at in ((first, first_other, 0), (second, second_other, CUT)):
+        part = a.shape[0] // 3
+        total = a[...] + b[...].astype(jnp.float32)
+        for n, out in enumerate((gate, up, down)):
+            out[at : at + part] = total[n * part : (n + 1) * part].astype(out.dtype)
 
 
 def sums(first, second, first_other, second_other, s):
@@ -239,28 +243,30 @@
     t = tokens.shape[0]
     far_rows = along_blk(tokens, -1)
     in_hbm = [pltpu.with_memory_space_constraint(a, pltpu.HBM) for a in (tokens, cotangent)]
-    near = list(pack(*in_hbm, ROW, 1))
-    late, near[0] = lax.optimization_barrier((cotangent, near[0]))
+    near = [None, *pack(*in_hbm, 1, ROW - 1, 1)]
+    late, near[1] = lax.optimization_barrier((cotangent, near[1]))
     far_cotan = along_blk(late, -1)
-    near = [near[0]] + [along_rep(near[i], 0, i) for i in range(1, ROW)]
+    near = [along_rep(near[i], 0, i) for i in range(1, ROW)]
 
     own = own_units(tokens, cotangent, w_gate, w_up, w_down, 20)
     own_x = row_term(*own, w_gate, w_up, 0, t, jnp.float32, 3)
 
     far_rows, own_x = lax.optimization_barrier((far_rows, own_x))
     gate, upval = gate_up(far_rows, w_gate, w_up, 2)
-    both = far_units(far_cotan, w_down, gate, upval, *own, 1.5)
-    far_x = row_term(*both, w_gate, w_up, t, t, jnp.bfloat16, 1)
+    first, second, both = far_units(far_cotan, w_down, gate, upval, *own, 1.5)
+    far_x = row_term(first, second, w_gate, w_up, t, t, jnp.bfloat16, 1)
     near, far_x = lax.optimization_barrier((near, far_x))
     half = near[0].shape[1] // 2
-    far_other = along_blk(jnp.concatenate([a[:, :half] for a in near[1:]]), -1)
+    late, far_cotan = lax.optimization_barrier((cotangent, far_cotan))
+    far_other = along_blk(jnp.concatenate([a[:, :half] for a in near]), -1)
     far_x = along_blk(far_x, 1)
-    first, second = ([g] + [along_rep(g, 0, i) for i in (1, 3)] for g in both)
-    first.insert(2, along_rep(first[1], 0, 1))
-    second.insert(2, along_rep(second[2], 0, 3))
-    own_cols = near[1:]
-    far_mine = along_blk(jnp.concatenate([a[:, half:] for a in own_cols]), -1)
-    far = pack(far_rows, far_cotan, 1, 0.5)[0]
+    both = along_rep(both, 0, 3)
+    first = [first, along_rep(first, 0, 1)]
+    first += [along_rep(first[1], 0, 1), both[: 3 * CUT]]
+    second = [second, along_rep(second, 0, 1), along_rep(both[3 * CUT :], 0, 3), both[3 * CUT :]]
+    far_mine = along_blk(jnp.concatenate([a[:, half:] for a in near]), -1)
+    far = pack(far_rows, far_cotan, 0, 1, 0.5)[0]
+    near = [pack(tokens, late, 0, 1, 0.5)[0], *near]
 
     other = [along_rep(weight_terms(near, far, far_other, g, 0, jnp.bfloat16, 1), 1, 0) for g in (first, second)]
     mine = [weight_terms(near, far, far_mine, g, 2, jnp.float32, 1) for g in (first, second)]

time: 83.4 us -> 81.7 us (0.980)
  starting transfers between devices: 32.6 us -> 31.5 us
    ppermute x11 -> x10, starting transfers between devices: 18.3 us -> 17.5 us  [along_rep(): lax.ppermute(value, 'rep', [(r, partner(r, j, i)) for r in range(2 * ROW)])]
    ppermute x11 -> x10, waiting for transfers between devices: 21.4 us -> 21.3 us  [along_rep(): lax.ppermute(value, 'rep', [(r, partner(r, j, i)) for r in range(2 * ROW)])]
    unnamed x14 -> x18, local copies, waits for them, and re-layouts: 6.92 us -> 6.88 us
    pallas_call x3 -> x4, Pallas kernels: 2.79 us -> 2.78 us  [the longest x3 1.81 us: pack(): pl.pallas_call(functools.partial(pack_kernel, first), out_shape=[jax.Shap...]
  transfers between devices with their start and end apart: 16 -> 15, of which waited for: 8 -> 6; matrix products, arithmetic and copies ran while one was open for 1% -> 2% of each run, Pallas kernels for 15% -> 15%
where the time goes in v4:
time: 81.7 us; the launch traced here: 81.4 us
  starting transfers between devices  31.5 us (39%)
  waiting for transfers between devices  27.3 us (33%)
  Pallas kernels  13.4 us (16%)
  local copies, waits for them, and re-layouts  7.04 us (9%)
  other arithmetic  1.29 us (2%)
  between operations  0.86 us (1%)
    ppermute x10, waiting for transfers between devices, along_rep(): lax.ppermute(value, 'rep', [(r, partner(r, j, i)) for r in range(2 * ROW)])  21.3 us
    ppermute x10, starting transfers between devices, along_rep(): lax.ppermute(value, 'rep', [(r, partner(r, j, i)) for r in range(2 * ROW)])  17.5 us
    ppermute x5, starting transfers between devices, along_blk(): lax.ppermute(value, 'blk', [(i, (i + by) % size) for i in range(size)])  14 us
    unnamed x18, local copies, waits for them, and re-layouts  6.88 us
    ppermute x5, waiting for transfers between devices, along_blk(): lax.ppermute(value, 'blk', [(i, (i + by) % size) for i in range(size)])  6.04 us
    pallas_call x4, Pallas kernels, weight_terms(): pl.pallas_call(functools.partial(weight_kernel, at * wide), out_shape=jax...  2.9 us
    pallas_call x2, Pallas kernels, row_term(): pl.pallas_call(functools.partial(term_kernel, at), in_specs=[VMEM] * 4, o...  2.54 us
    pallas_call x1, Pallas kernels, own_units(): pl.pallas_call(own_kernel, in_specs=[VMEM] * 5, out_specs=[VMEM] * 2, out...  2.45 us
  transfers between devices with their start and end apart: 15, of which 6 were waited for; matrix products, arithmetic and copies ran while one was open for 2% of the time, Pallas kernels for 15%

profile of v4, /device:TPU:2, one launch (start us, length us, event | category | flops | bytes accessed | tf_op | source)
XLA Modules:
  0.0 81.4 jit_solution(6082058373822501719)
XLA Ops:
  0.6 6.4 %collective-permute-start = (bf16[128,4096]{1,0:T(8,128)(2,1)}, bf16[128,4096]{1,0:T(8,128)(2,1)S(1)}, u32[]{:S(2)}, u32[]{:S(2)}) collective-permute-start(bf16[128,4096]{1,0:T(8,128)(2,1)} %x.5), channel_id=1, source_target_pairs={{0,248},{8,0},{16,8},{24,16},{32,24},{40,32},{48,40},{56,48},{64,5... | collective-permute-start | bytes 3145736 | tf_op jit(solution)/shard_map/ppermute | solution.py:18
  7.0 1.5 %pack.3 = (bf16[128,2048]{1,0:T(8,128)(2,1)S(1)}, bf16[128,2048]{1,0:T(8,128)(2,1)S(1)}, bf16[128,2048]{1,0:T(8,128)(2,1)S(1)}) custom-call(bf16[128,4096]{1,0:T(8,128)(2,1)} %x.5, bf16[128,4096]{1,0:T(8,128)(2,1)} %c.4), custom_call_target="tpu_custom_call" | custom-call | flops 1000000000 | bytes 3500000 | tf_op jit(solution)/shard_map/pack/pallas_call | solution.py:177
  8.6 1.6 %collective-permute-start.1 = (bf16[128,2048]{1,0:T(8,128)(2,1)S(1)}, bf16[128,2048]{1,0:T(8,128)(2,1)S(1)}, u32[]{:S(2)}, u32[]{:S(2)}) collective-permute-start(bf16[128,2048]{1,0:T(8,128)(2,1)S(1)} %get-tuple-element.31), channel_id=1, source_target_pairs={{0,1},{1,2},{2,3},{3,0},{4,5},{5,6},{6,7},{7,4},{8,9},{9,10},{10,1... | collective-permute-start | bytes 1572872 | tf_op jit(solution)/shard_map/ppermute | solution.py:26
  10.1 1.1 %collective-permute-start.2 = (bf16[128,2048]{1,0:T(8,128)(2,1)S(1)}, bf16[128,2048]{1,0:T(8,128)(2,1)S(1)}, u32[]{:S(2)}, u32[]{:S(2)}) collective-permute-start(bf16[128,2048]{1,0:T(8,128)(2,1)S(1)} %get-tuple-element.32), channel_id=1, source_target_pairs={{0,2},{1,3},{2,0},{3,1},{4,6},{5,7},{6,4},{7,5},{8,10},{9,11},{10,... | collective-permute-start | bytes 1572872 | tf_op jit(solution)/shard_map/ppermute | solution.py:26
  11.3 2.2 %collective-permute-start.3 = (bf16[128,2048]{1,0:T(8,128)(2,1)S(1)}, bf16[128,2048]{1,0:T(8,128)(2,1)S(1)}, u32[]{:S(2)}, u32[]{:S(2)}) collective-permute-start(bf16[128,2048]{1,0:T(8,128)(2,1)S(1)} %get-tuple-element.33), channel_id=1, source_target_pairs={{0,3},{1,0},{2,1},{3,2},{4,7},{5,4},{6,5},{7,6},{8,11},{9,8},{10,9... | collective-permute-start | bytes 1572872 | tf_op jit(solution)/shard_map/ppermute | solution.py:26
  13.4 1.8 %copy-done.1 = bf16[4096,344]{0,1:T(8,128)(2,1)S(1)} copy-done((bf16[4096,344]{0,1:T(8,128)(2,1)S(1)}, bf16[4096,344]{0,1:T(8,128)(2,1)}, u32[]{:S(2)}) %copy-start.1) | copy-done | bytes 2818072
  15.2 1.2 %copy-done.3 = bf16[128,4096]{1,0:T(8,128)(2,1)S(1)} copy-done((bf16[128,4096]{1,0:T(8,128)(2,1)S(1)}, bf16[128,4096]{1,0:T(8,128)(2,1)}, u32[]{:S(2)}) %copy-start.3) | copy-done | bytes 1048600
  16.4 1.2 %copy-done.5 = bf16[128,4096]{1,0:T(8,128)(2,1)S(1)} copy-done((bf16[128,4096]{1,0:T(8,128)(2,1)S(1)}, bf16[128,4096]{1,0:T(8,128)(2,1)}, u32[]{:S(2)}) %copy-start.5) | copy-done | bytes 1048600
  17.7 1.8 %copy-done.7 = bf16[344,4096]{1,0:T(8,128)(2,1)S(1)} copy-done((bf16[344,4096]{1,0:T(8,128)(2,1)S(1)}, bf16[344,4096]{1,0:T(8,128)(2,1)}, u32[]{:S(2)}) %copy-start.7) | copy-done | bytes 2818072
  19.5 2.4 %own_units.1 = (bf16[528,128]{1,0:T(8,128)(2,1)S(1)}, bf16[504,128]{1,0:T(8,128)(2,1)S(1)}) custom-call(bf16[128,4096]{1,0:T(8,128)(2,1)S(1)} %copy-done.3, bf16[128,4096]{1,0:T(8,128)(2,1)S(1)} %copy-done.5, bf16[344,4096]{1,0:T(8,128)(2,1)S(1)} %bitcast.4, bf16[344,4096]{1,0:T(8,128)(2,1)S(1)} %bitcast.8, bf16[344,4096]{1,0:T(8,128)(2,1)S(1)} %copy-done.7), custom_call_target="tpu_custom_call" | custom-call | flops 20000000000 | bytes 70000000 | tf_op jit(solution)/shard_map/own_units/pallas_call | solution.py:77
  21.9 1.3 %row_term.2 = f32[128,4096]{1,0:T(8,128)S(1)} custom-call(bf16[528,128]{1,0:T(8,128)(2,1)S(1)} %get-tuple-element.27.first.own_first, bf16[504,128]{1,0:T(8,128)(2,1)S(1)} %get-tuple-element.28.second.own_second, bf16[344,4096]{1,0:T(8,128)(2,1)S(1)} %bitcast.5, bf16[344,4096]{1,0:T(8,128)(2,1)S(1)} %bitcast.9), custom_call_target="tpu_custom_call" | custom-call | flops 3000000000 | bytes 10500000 | tf_op jit(solution)/shard_map/row_term/pallas_call | solution.py:145
  23.2 1.6 %gate_up.1 = (f32[344,128]{1,0:T(8,128)S(1)}, f32[344,128]{1,0:T(8,128)S(1)}) custom-call(bf16[128,4096]{1,0:T(8,128)(2,1)S(1)} %collective-permute-done.x, bf16[344,4096]{1,0:T(8,128)(2,1)S(1)} %bitcast.6, bf16[344,4096]{1,0:T(8,128)(2,1)S(1)} %bitcast.10), custom_call_target="tpu_custom_call" | custom-call | flops 2000000000 | bytes 7000000 | tf_op jit(solution)/shard_map/gate_up/pallas_call | solution.py:94
  24.9 6.0 %collective-permute-done.4.c = bf16[128,4096]{1,0:T(8,128)(2,1)S(1)} collective-permute-done((bf16[128,4096]{1,0:T(8,128)(2,1)}, bf16[128,4096]{1,0:T(8,128)(2,1)S(1)}, u32[]{:S(2)}, u32[]{:S(2)}) %collective-permute-start.4) | collective-permute-done | bytes 1048608 | tf_op jit(solution)/shard_map/ppermute | solution.py:18
  30.9 1.0 %far_units.1 = (bf16[528,256]{1,0:T(8,128)(2,1)S(1)}, bf16[504,256]{1,0:T(8,128)(2,1)S(1)}, bf16[1032,256]{1,0:T(8,128)(2,1)S(1)}) custom-call(bf16[128,4096]{1,0:T(8,128)(2,1)S(1)} %collective-permute-done.4.c, bf16[344,4096]{1,0:T(8,128)(2,1)S(1)} %copy-done.8, f32[344,128]{1,0:T(8,128)S(1)} %get-tuple-element.36.gate, ...), custom_call_target="tpu_custom_call" | custom-call | flops 1500000000 | bytes 5250000 | tf_op jit(solution)/shard_map/far_units/pallas_call | solution.py:117
  31.9 0.8 %copy-done.2 = bf16[4096,344]{0,1:T(8,128)(2,1)S(1)} copy-done((bf16[4096,344]{0,1:T(8,128)(2,1)S(1)}, bf16[4096,344]{0,1:T(8,128)(2,1)}, u32[]{:S(2)}) %copy-start.2) | copy-done | bytes 2818072
  32.7 1.3 %row_term.3 = bf16[128,4096]{1,0:T(8,128)(2,1)S(1)} custom-call(bf16[528,256]{1,0:T(8,128)(2,1)S(1)} %get-tuple-element.38.first.refs_6_, bf16[504,256]{1,0:T(8,128)(2,1)S(1)} %get-tuple-element.39.second.refs_6_, bf16[344,4096]{1,0:T(8,128)(2,1)S(1)} %bitcast.7, bf16[344,4096]{1,0:T(8,128)(2,1)S(1)} %bitcast.11), custom_call_target="tpu_custom_call" | custom-call | flops 1000000000 | bytes 3500000 | tf_op jit(solution)/shard_map/row_term/pallas_call | solution.py:145
  34.2 4.0 %collective-permute-start.12 = (bf16[384,1024]{1,0:T(8,128)(2,1)S(1)}, bf16[384,1024]{1,0:T(8,128)(2,1)S(1)}, u32[]{:S(2)}, u32[]{:S(2)}) collective-permute-start(bf16[384,1024]{1,0:T(8,128)(2,1)S(1)} %pad_maximum_fusion.1), channel_id=1, source_target_pairs={{0,248},{8,0},{16,8},{24,16},{32,24},{40,32},{48,40},{56,48},{64,5... | collective-permute-start | bytes 2359304 | tf_op jit(solution)/shard_map/ppermute | solution.py:18
  38.2 1.5 %collective-permute-start.7 = (bf16[528,256]{1,0:T(8,128)(2,1)S(1)}, bf16[528,256]{1,0:T(8,128)(2,1)S(1)}, u32[]{:S(2)}, u32[]{:S(2)}) collective-permute-start(bf16[528,256]{1,0:T(8,128)(2,1)S(1)} %get-tuple-element.38.first.refs_6_), channel_id=1, source_target_pairs={{0,1},{1,2},{2,3},{3,0},{4,5},{5,6},{6,7},{7,4},{8,9},{9,10},{10,1... | collective-permute-start | bytes 811016 | tf_op jit(solution)/shard_map/ppermute | solution.py:26
  40.3 3.6 %collective-permute-start.6 = (bf16[384,1024]{1,0:T(8,128)(2,1)S(1)}, bf16[384,1024]{1,0:T(8,128)(2,1)S(1)}, u32[]{:S(2)}, u32[]{:S(2)}) collective-permute-start(bf16[384,1024]{1,0:T(8,128)(2,1)S(1)} %pad_maximum_fusion), channel_id=1, source_target_pairs={{0,248},{8,0},{16,8},{24,16},{32,24},{40,32},{48,40},{56,48},{64,5... | collective-permute-start | bytes 2359304 | tf_op jit(solution)/shard_map/ppermute | solution.py:18
  44.0 1.6 %collective-permute-done.7.refs_7_ = bf16[528,256]{1,0:T(8,128)(2,1)S(1)} collective-permute-done((bf16[528,256]{1,0:T(8,128)(2,1)S(1)}, bf16[528,256]{1,0:T(8,128)(2,1)S(1)}, u32[]{:S(2)}, u32[]{:S(2)}) %collective-permute-start.7) | collective-permute-done | bytes 270368 | tf_op jit(solution)/shard_map/ppermute | solution.py:26
  45.5 1.8 %collective-permute-start.8 = (bf16[528,256]{1,0:T(8,128)(2,1)S(1)}, bf16[528,256]{1,0:T(8,128)(2,1)S(1)}, u32[]{:S(2)}, u32[]{:S(2)}) collective-permute-start(bf16[528,256]{1,0:T(8,128)(2,1)S(1)} %collective-permute-done.7.refs_7_), channel_id=1, source_target_pairs={{0,1},{1,2},{2,3},{3,0},{4,5},{5,6},{6,7},{7,4},{8,9},{9,10},{10,1... | collective-permute-start | bytes 811016 | tf_op jit(solution)/shard_map/ppermute | solution.py:26
  47.3 2.7 %collective-permute-done.9 = bf16[1032,256]{1,0:T(8,128)(2,1)S(1)} collective-permute-done((bf16[1032,256]{1,0:T(8,128)(2,1)S(1)}, bf16[1032,256]{1,0:T(8,128)(2,1)S(1)}, u32[]{:S(2)}, u32[]{:S(2)}) %collective-permute-start.9) | collective-permute-done | bytes 528416 | tf_op jit(solution)/shard_map/ppermute | solution.py:26
  50.0 1.2 %collective-permute-start.10 = (bf16[504,256]{1,0:T(8,128)(2,1)S(1)}, bf16[504,256]{1,0:T(8,128)(2,1)S(1)}, u32[]{:S(2)}, u32[]{:S(2)}) collective-permute-start(bf16[504,256]{1,0:T(8,128)(2,1)S(1)} %get-tuple-element.39.second.refs_6_), channel_id=1, source_target_pairs={{0,1},{1,2},{2,3},{3,0},{4,5},{5,6},{6,7},{7,4},{8,9},{9,10},{10,1... | collective-permute-start | bytes 774152 | tf_op jit(solution)/shard_map/ppermute | solution.py:26
  51.2 2.5 %collective-permute-done.8.refs_8_ = bf16[528,256]{1,0:T(8,128)(2,1)S(1)} collective-permute-done((bf16[528,256]{1,0:T(8,128)(2,1)S(1)}, bf16[528,256]{1,0:T(8,128)(2,1)S(1)}, u32[]{:S(2)}, u32[]{:S(2)}) %collective-permute-start.8) | collective-permute-done | bytes 270368 | tf_op jit(solution)/shard_map/ppermute | solution.py:26
  53.6 1.7 %collective-permute-start.11 = (bf16[504,256]{1,0:T(8,128)(2,1)S(1)}, bf16[504,256]{1,0:T(8,128)(2,1)S(1)}, u32[]{:S(2)}, u32[]{:S(2)}) collective-permute-start(bf16[504,256]{1,0:T(8,128)(2,1)S(1)} %slice.34.refs_9_), channel_id=1, source_target_pairs={{0,3},{1,0},{2,1},{3,2},{4,7},{5,4},{6,5},{7,6},{8,11},{9,8},{10,9... | collective-permute-start | bytes 774152 | tf_op jit(solution)/shard_map/ppermute | solution.py:26
  55.7 0.7 weight_terms.6
  56.4 3.0 %collective-permute-start.13 = (bf16[528,512]{1,0:T(8,128)(2,1)S(1)}, bf16[528,512]{1,0:T(8,128)(2,1)S(1)}, u32[]{:S(2)}, u32[]{:S(2)}) collective-permute-start(bf16[528,512]{1,0:T(8,128)(2,1)S(1)} %weight_terms.6), channel_id=1, source_target_pairs={{0,4},{1,5},{2,6},{3,7},{4,0},{5,1},{6,2},{7,3},{8,12},{9,13},{10,... | collective-permute-start | bytes 1622024 | tf_op jit(solution)/shard_map/ppermute | solution.py:26
  60.7 3.0 %collective-permute-start.14 = (bf16[504,512]{1,0:T(8,128)(2,1)S(1)}, bf16[504,512]{1,0:T(8,128)(2,1)S(1)}, u32[]{:S(2)}, u32[]{:S(2)}) collective-permute-start(bf16[504,512]{1,0:T(8,128)(2,1)S(1)} %weight_terms.7), channel_id=1, source_target_pairs={{0,4},{1,5},{2,6},{3,7},{4,0},{5,1},{6,2},{7,3},{8,12},{9,13},{10,... | collective-permute-start | bytes 1548296 | tf_op jit(solution)/shard_map/ppermute | solution.py:26
  63.7 0.7 weight_terms.4.first
  65.1 1.2 %add_convert_fusion = bf16[128,4096]{1,0:T(8,128)(2,1)} fusion(f32[128,4096]{1,0:T(8,128)S(1)} %row_term.2, bf16[128,4096]{1,0:T(8,128)(2,1)S(1)} %collective-permute-done.5), kind=kLoop, calls=%fused_computation | loop fusion | flops 1572864 | bytes 4194304 | tf_op jit(solution)/shard_map/convert_element_type | solution.py:274
  66.3 14.0 %collective-permute-done.14.second_other = bf16[504,512]{1,0:T(8,128)(2,1)S(1)} collective-permute-done((bf16[504,512]{1,0:T(8,128)(2,1)S(1)}, bf16[504,512]{1,0:T(8,128)(2,1)S(1)}, u32[]{:S(2)}, u32[]{:S(2)}) %collective-permute-start.14) | collective-permute-done | bytes 516128 | tf_op jit(solution)/shard_map/ppermute | solution.py:26
  80.3 1.1 %sums.1 = (bf16[344,512]{1,0:T(8,128)(2,1)}, bf16[344,512]{1,0:T(8,128)(2,1)}, bf16[344,512]{1,0:T(8,128)(2,1)}) custom-call(f32[528,512]{1,0:T(8,128)S(1)} %weight_terms.4.first, f32[504,512]{1,0:T(8,128)S(1)} %weight_terms.5.second, bf16[528,512]{1,0:T(8,128)(2,1)S(1)} %collective-permute-done.13.first_other, ...), custom_call_target="tpu_custom_call" | custom-call | flops 1000000000 | bytes 3500000 | tf_op jit(solution)/shard_map/sums/pallas_call | solution.py:229
  (36 shorter events, 3.1 us)
Async XLA Ops:
  0.6 12.8 %copy-start = (bf16[4096,344]{0,1:T(8,128)(2,1)S(1)}, bf16[4096,344]{0,1:T(8,128)(2,1)}, u32[]{:S(2)}) copy-start(bf16[4096,344]{0,1:T(8,128)(2,1)} %param.7) | copy-start | bytes 8454148
  0.6 22.6 %collective-permute-start = (bf16[128,4096]{1,0:T(8,128)(2,1)}, bf16[128,4096]{1,0:T(8,128)(2,1)S(1)}, u32[]{:S(2)}, u32[]{:S(2)}) collective-permute-start(bf16[128,4096]{1,0:T(8,128)(2,1)} %x.5), channel_id=1, source_target_pairs={{0,248},{8,0},{16,8},{24,16},{32,24},{40,32},{48,40},{56,48},{64,5... | collective-permute-start | bytes 3145736 | tf_op jit(solution)/shard_map/ppermute | solution.py:18
  8.6 25.4 %collective-permute-start.1 = (bf16[128,2048]{1,0:T(8,128)(2,1)S(1)}, bf16[128,2048]{1,0:T(8,128)(2,1)S(1)}, u32[]{:S(2)}, u32[]{:S(2)}) collective-permute-start(bf16[128,2048]{1,0:T(8,128)(2,1)S(1)} %get-tuple-element.31), channel_id=1, source_target_pairs={{0,1},{1,2},{2,3},{3,0},{4,5},{5,6},{6,7},{7,4},{8,9},{9,10},{10,1... | collective-permute-start | bytes 1572872 | tf_op jit(solution)/shard_map/ppermute | solution.py:26
  10.1 23.8 %collective-permute-start.2 = (bf16[128,2048]{1,0:T(8,128)(2,1)S(1)}, bf16[128,2048]{1,0:T(8,128)(2,1)S(1)}, u32[]{:S(2)}, u32[]{:S(2)}) collective-permute-start(bf16[128,2048]{1,0:T(8,128)(2,1)S(1)} %get-tuple-element.32), channel_id=1, source_target_pairs={{0,2},{1,3},{2,0},{3,1},{4,6},{5,7},{6,4},{7,5},{8,10},{9,11},{10,... | collective-permute-start | bytes 1572872 | tf_op jit(solution)/shard_map/ppermute | solution.py:26
  11.3 22.7 %collective-permute-start.3 = (bf16[128,2048]{1,0:T(8,128)(2,1)S(1)}, bf16[128,2048]{1,0:T(8,128)(2,1)S(1)}, u32[]{:S(2)}, u32[]{:S(2)}) collective-permute-start(bf16[128,2048]{1,0:T(8,128)(2,1)S(1)} %get-tuple-element.33), channel_id=1, source_target_pairs={{0,3},{1,0},{2,1},{3,2},{4,7},{5,4},{6,5},{7,6},{8,11},{9,8},{10,9... | collective-permute-start | bytes 1572872 | tf_op jit(solution)/shard_map/ppermute | solution.py:26
  13.4 17.5 %collective-permute-start.4 = (bf16[128,4096]{1,0:T(8,128)(2,1)}, bf16[128,4096]{1,0:T(8,128)(2,1)S(1)}, u32[]{:S(2)}, u32[]{:S(2)}) collective-permute-start(bf16[128,4096]{1,0:T(8,128)(2,1)} %c.4), channel_id=1, source_target_pairs={{0,248},{8,0},{16,8},{24,16},{32,24},{40,32},{48,40},{56,48},{64,5... | collective-permute-start | bytes 3145736 | tf_op jit(solution)/shard_map/ppermute | solution.py:18
  13.4 1.8 %copy-start.1 = (bf16[4096,344]{0,1:T(8,128)(2,1)S(1)}, bf16[4096,344]{0,1:T(8,128)(2,1)}, u32[]{:S(2)}) copy-start(bf16[4096,344]{0,1:T(8,128)(2,1)} %param.8) | copy-start | bytes 8454148
  15.2 1.2 %copy-start.3 = (bf16[128,4096]{1,0:T(8,128)(2,1)S(1)}, bf16[128,4096]{1,0:T(8,128)(2,1)}, u32[]{:S(2)}) copy-start(bf16[128,4096]{1,0:T(8,128)(2,1)} %x.5) | copy-start | bytes 3145732
  16.4 1.2 %copy-start.5 = (bf16[128,4096]{1,0:T(8,128)(2,1)S(1)}, bf16[128,4096]{1,0:T(8,128)(2,1)}, u32[]{:S(2)}) copy-start(bf16[128,4096]{1,0:T(8,128)(2,1)} %c.4) | copy-start | bytes 3145732
  17.7 1.8 %copy-start.7 = (bf16[344,4096]{1,0:T(8,128)(2,1)S(1)}, bf16[344,4096]{1,0:T(8,128)(2,1)}, u32[]{:S(2)}) copy-start(bf16[344,4096]{1,0:T(8,128)(2,1)} %wd.3) | copy-start | bytes 8454148
  23.2 7.7 %copy-start.8 = (bf16[344,4096]{1,0:T(8,128)(2,1)S(1)}, bf16[344,4096]{1,0:T(8,128)(2,1)}, u32[]{:S(2)}) copy-start(bf16[344,4096]{1,0:T(8,128)(2,1)} %wd.3) | copy-start | bytes 8454148
  30.9 1.8 %copy-start.2 = (bf16[4096,344]{0,1:T(8,128)(2,1)S(1)}, bf16[4096,344]{0,1:T(8,128)(2,1)}, u32[]{:S(2)}) copy-start(bf16[4096,344]{0,1:T(8,128)(2,1)} %param.8) | copy-start | bytes 8454148
  34.1 21.2 %copy-start.4 = (bf16[128,4096]{1,0:T(8,128)(2,1)S(1)}, bf16[128,4096]{1,0:T(8,128)(2,1)}, u32[]{:S(2)}) copy-start(bf16[128,4096]{1,0:T(8,128)(2,1)} %x.5) | copy-start | bytes 3145732
  34.2 21.2 %copy-start.6 = (bf16[128,4096]{1,0:T(8,128)(2,1)S(1)}, bf16[128,4096]{1,0:T(8,128)(2,1)}, u32[]{:S(2)}) copy-start(bf16[128,4096]{1,0:T(8,128)(2,1)} %c.4) | copy-start | bytes 3145732
  34.2 21.4 %collective-permute-start.12 = (bf16[384,1024]{1,0:T(8,128)(2,1)S(1)}, bf16[384,1024]{1,0:T(8,128)(2,1)S(1)}, u32[]{:S(2)}, u32[]{:S(2)}) collective-permute-start(bf16[384,1024]{1,0:T(8,128)(2,1)S(1)} %pad_maximum_fusion.1), channel_id=1, source_target_pairs={{0,248},{8,0},{16,8},{24,16},{32,24},{40,32},{48,40},{56,48},{64,5... | collective-permute-start | bytes 2359304 | tf_op jit(solution)/shard_map/ppermute | solution.py:18
  38.2 7.3 %collective-permute-start.7 = (bf16[528,256]{1,0:T(8,128)(2,1)S(1)}, bf16[528,256]{1,0:T(8,128)(2,1)S(1)}, u32[]{:S(2)}, u32[]{:S(2)}) collective-permute-start(bf16[528,256]{1,0:T(8,128)(2,1)S(1)} %get-tuple-element.38.first.refs_6_), channel_id=1, source_target_pairs={{0,1},{1,2},{2,3},{3,0},{4,5},{5,6},{6,7},{7,4},{8,9},{9,10},{10,1... | collective-permute-start | bytes 811016 | tf_op jit(solution)/shard_map/ppermute | solution.py:26
  39.7 25.4 %collective-permute-start.5 = (bf16[128,4096]{1,0:T(8,128)(2,1)S(1)}, bf16[128,4096]{1,0:T(8,128)(2,1)S(1)}, u32[]{:S(2)}, u32[]{:S(2)}) collective-permute-start(bf16[128,4096]{1,0:T(8,128)(2,1)S(1)} %row_term.3), channel_id=1, source_target_pairs={{0,8},{8,16},{16,24},{24,32},{32,40},{40,48},{48,56},{56,64},{64,7... | collective-permute-start | bytes 3145736 | tf_op jit(solution)/shard_map/ppermute | solution.py:18
  39.7 10.3 %collective-permute-start.9 = (bf16[1032,256]{1,0:T(8,128)(2,1)S(1)}, bf16[1032,256]{1,0:T(8,128)(2,1)S(1)}, u32[]{:S(2)}, u32[]{:S(2)}) collective-permute-start(bf16[1032,256]{1,0:T(8,128)(2,1)S(1)} %get-tuple-element.46), channel_id=1, source_target_pairs={{0,3},{1,0},{2,1},{3,2},{4,7},{5,4},{6,5},{7,6},{8,11},{9,8},{10,9... | collective-permute-start | bytes 1585160 | tf_op jit(solution)/shard_map/ppermute | solution.py:26
  40.3 23.4 %collective-permute-start.6 = (bf16[384,1024]{1,0:T(8,128)(2,1)S(1)}, bf16[384,1024]{1,0:T(8,128)(2,1)S(1)}, u32[]{:S(2)}, u32[]{:S(2)}) collective-permute-start(bf16[384,1024]{1,0:T(8,128)(2,1)S(1)} %pad_maximum_fusion), channel_id=1, source_target_pairs={{0,248},{8,0},{16,8},{24,16},{32,24},{40,32},{48,40},{56,48},{64,5... | collective-permute-start | bytes 2359304 | tf_op jit(solution)/shard_map/ppermute | solution.py:18
  45.5 8.1 %collective-permute-start.8 = (bf16[528,256]{1,0:T(8,128)(2,1)S(1)}, bf16[528,256]{1,0:T(8,128)(2,1)S(1)}, u32[]{:S(2)}, u32[]{:S(2)}) collective-permute-start(bf16[528,256]{1,0:T(8,128)(2,1)S(1)} %collective-permute-done.7.refs_7_), channel_id=1, source_target_pairs={{0,1},{1,2},{2,3},{3,0},{4,5},{5,6},{6,7},{7,4},{8,9},{9,10},{10,1... | collective-permute-start | bytes 811016 | tf_op jit(solution)/shard_map/ppermute | solution.py:26
  50.0 9.4 %collective-permute-start.10 = (bf16[504,256]{1,0:T(8,128)(2,1)S(1)}, bf16[504,256]{1,0:T(8,128)(2,1)S(1)}, u32[]{:S(2)}, u32[]{:S(2)}) collective-permute-start(bf16[504,256]{1,0:T(8,128)(2,1)S(1)} %get-tuple-element.39.second.refs_6_), channel_id=1, source_target_pairs={{0,1},{1,2},{2,3},{3,0},{4,5},{5,6},{6,7},{7,4},{8,9},{9,10},{10,1... | collective-permute-start | bytes 774152 | tf_op jit(solution)/shard_map/ppermute | solution.py:26
  53.6 6.3 %collective-permute-start.11 = (bf16[504,256]{1,0:T(8,128)(2,1)S(1)}, bf16[504,256]{1,0:T(8,128)(2,1)S(1)}, u32[]{:S(2)}, u32[]{:S(2)}) collective-permute-start(bf16[504,256]{1,0:T(8,128)(2,1)S(1)} %slice.34.refs_9_), channel_id=1, source_target_pairs={{0,3},{1,0},{2,1},{3,2},{4,7},{5,4},{6,5},{7,6},{8,11},{9,8},{10,9... | collective-permute-start | bytes 774152 | tf_op jit(solution)/shard_map/ppermute | solution.py:26
  56.4 23.9 %collective-permute-start.13 = (bf16[528,512]{1,0:T(8,128)(2,1)S(1)}, bf16[528,512]{1,0:T(8,128)(2,1)S(1)}, u32[]{:S(2)}, u32[]{:S(2)}) collective-permute-start(bf16[528,512]{1,0:T(8,128)(2,1)S(1)} %weight_terms.6), channel_id=1, source_target_pairs={{0,4},{1,5},{2,6},{3,7},{4,0},{5,1},{6,2},{7,3},{8,12},{9,13},{10,... | collective-permute-start | bytes 1622024 | tf_op jit(solution)/shard_map/ppermute | solution.py:26
  60.7 19.6 %collective-permute-start.14 = (bf16[504,512]{1,0:T(8,128)(2,1)S(1)}, bf16[504,512]{1,0:T(8,128)(2,1)S(1)}, u32[]{:S(2)}, u32[]{:S(2)}) collective-permute-start(bf16[504,512]{1,0:T(8,128)(2,1)S(1)} %weight_terms.7), channel_id=1, source_target_pairs={{0,4},{1,5},{2,6},{3,7},{4,0},{5,1},{6,2},{7,3},{8,12},{9,13},{10,... | collective-permute-start | bytes 1548296 | tf_op jit(solution)/shard_map/ppermute | solution.py:26

commit v5 on v4

--- a/solution.py
+++ b/solution.py
@@ -217,24 +217,40 @@
     )(*near, head, tail, *grads)
 
 
-def sum_kernel(first, second, first_other, second_other, gate, up, down):
-    for a, b, at in ((first, first_other, 0), (second, second_other, CUT)):
-        part = a.shape[0] // 3
-        total = a[...] + b[...].astype(jnp.float32)
-        for n, out in enumerate((gate, up, down)):
-            out[at : at + part] = total[n * part : (n + 1) * part].astype(out.dtype)
-
-
-def sums(first, second, first_other, second_other, s):
+def early_kernel(first, other, out):
+    out[...] = (first[...] + other[...].astype(jnp.float32)).astype(out.dtype)
+
+
+def early_sums(first, other):
+    return pl.pallas_call(
+        early_kernel,
+        out_shape=jax.ShapeDtypeStruct(other.shape, jnp.bfloat16),
+        in_specs=[VMEM] * 2,
+        out_specs=VMEM,
+        compiler_params=params(),
+        cost_estimate=cost(0.5),
+        name="early_sums",
+    )(first, other)
+
+
+def sum_kernel(first, second, second_other, gate, up, down):
+    part = second.shape[0] // 3
+    total = second[...] + second_other[...].astype(jnp.float32)
+    for n, out in enumerate((gate, up, down)):
+        out[:CUT] = first[n * CUT : (n + 1) * CUT]
+        out[CUT:] = total[n * part : (n + 1) * part].astype(out.dtype)
+
+
+def sums(first, second, second_other, s):
     return pl.pallas_call(
         sum_kernel,
         out_shape=[jax.ShapeDtypeStruct((s, first.shape[1]), jnp.bfloat16)] * 3,
-        in_specs=[VMEM] * 4,
+        in_specs=[VMEM] * 3,
         out_specs=[VMEM] * 3,
         compiler_params=params(),
         cost_estimate=cost(1),
         name="sums",
-    )(first, second, first_other, second_other)
+    )(first, second, second_other)
 
 
 def local(tokens, cotangent, gate_weight, up_weight, down_weight):
@@ -270,7 +286,7 @@
 
     other = [along_rep(weight_terms(near, far, far_other, g, 0, jnp.bfloat16, 1), 1, 0) for g in (first, second)]
     mine = [weight_terms(near, far, far_mine, g, 2, jnp.float32, 1) for g in (first, second)]
-    gate_grad, up_grad, down_grad = sums(*mine, *other, s)
+    gate_grad, up_grad, down_grad = sums(early_sums(mine[0], other[0]), mine[1], other[1], s)
     input_grad = (own_x + far_x.astype(jnp.float32)).astype(jnp.bfloat16)
     return input_grad, gate_grad.T, up_grad.T, down_grad
 

time: 81.7 us -> 81.7 us (level)
  transfers between devices with their start and end apart: 15 -> 15, of which waited for: 6 -> 7; matrix products, arithmetic and copies ran while one was open for 2% -> 2% of each run, Pallas kernels for 15% -> 15%
where the time goes in v5:
time: 81.7 us; the launch traced here: 81.4 us
  starting transfers between devices  31.5 us (39%)
  waiting for transfers between devices  27.2 us (33%)
  Pallas kernels  13.5 us (17%)
  local copies, waits for them, and re-layouts  7.04 us (9%)
  other arithmetic  1.33 us (2%)
  between operations  0.86 us (1%)
    ppermute x10, waiting for transfers between devices, along_rep(): lax.ppermute(value, 'rep', [(r, partner(r, j, i)) for r in range(2 * ROW)])  21.1 us
    ppermute x10, starting transfers between devices, along_rep(): lax.ppermute(value, 'rep', [(r, partner(r, j, i)) for r in range(2 * ROW)])  17.5 us
    ppermute x5, starting transfers between devices, along_blk(): lax.ppermute(value, 'blk', [(i, (i + by) % size) for i in range(size)])  14 us
    unnamed x18, local copies, waits for them, and re-layouts  6.88 us
    ppermute x5, waiting for transfers between devices, along_blk(): lax.ppermute(value, 'blk', [(i, (i + by) % size) for i in range(size)])  6.04 us
    pallas_call x4, Pallas kernels, weight_terms(): pl.pallas_call(functools.partial(weight_kernel, at * wide), out_shape=jax...  2.9 us
    pallas_call x2, Pallas kernels, row_term(): pl.pallas_call(functools.partial(term_kernel, at), in_specs=[VMEM] * 4, o...  2.54 us
    pallas_call x1, Pallas kernels, own_units(): pl.pallas_call(own_kernel, in_specs=[VMEM] * 5, out_specs=[VMEM] * 2, out...  2.45 us
  transfers between devices with their start and end apart: 15, of which 7 were waited for; matrix products, arithmetic and copies ran while one was open for 2% of the time, Pallas kernels for 15%

profile of v5, /device:TPU:2, one launch (start us, length us, event | category | flops | bytes accessed | tf_op | source)
XLA Modules:
  0.0 81.4 jit_solution(11326845358028618584)
XLA Ops:
  0.6 6.4 %collective-permute-start = (bf16[128,4096]{1,0:T(8,128)(2,1)}, bf16[128,4096]{1,0:T(8,128)(2,1)S(1)}, u32[]{:S(2)}, u32[]{:S(2)}) collective-permute-start(bf16[128,4096]{1,0:T(8,128)(2,1)} %x.5), channel_id=1, source_target_pairs={{0,248},{8,0},{16,8},{24,16},{32,24},{40,32},{48,40},{56,48},{64,5... | collective-permute-start | bytes 3145736 | tf_op jit(solution)/shard_map/ppermute | solution.py:18
  7.0 1.5 %pack.3 = (bf16[128,2048]{1,0:T(8,128)(2,1)S(1)}, bf16[128,2048]{1,0:T(8,128)(2,1)S(1)}, bf16[128,2048]{1,0:T(8,128)(2,1)S(1)}) custom-call(bf16[128,4096]{1,0:T(8,128)(2,1)} %x.5, bf16[128,4096]{1,0:T(8,128)(2,1)} %c.4), custom_call_target="tpu_custom_call" | custom-call | flops 1000000000 | bytes 3500000 | tf_op jit(solution)/shard_map/pack/pallas_call | solution.py:177
  8.6 1.6 %collective-permute-start.1 = (bf16[128,2048]{1,0:T(8,128)(2,1)S(1)}, bf16[128,2048]{1,0:T(8,128)(2,1)S(1)}, u32[]{:S(2)}, u32[]{:S(2)}) collective-permute-start(bf16[128,2048]{1,0:T(8,128)(2,1)S(1)} %get-tuple-element.31), channel_id=1, source_target_pairs={{0,1},{1,2},{2,3},{3,0},{4,5},{5,6},{6,7},{7,4},{8,9},{9,10},{10,1... | collective-permute-start | bytes 1572872 | tf_op jit(solution)/shard_map/ppermute | solution.py:26
  10.1 1.1 %collective-permute-start.2 = (bf16[128,2048]{1,0:T(8,128)(2,1)S(1)}, bf16[128,2048]{1,0:T(8,128)(2,1)S(1)}, u32[]{:S(2)}, u32[]{:S(2)}) collective-permute-start(bf16[128,2048]{1,0:T(8,128)(2,1)S(1)} %get-tuple-element.32), channel_id=1, source_target_pairs={{0,2},{1,3},{2,0},{3,1},{4,6},{5,7},{6,4},{7,5},{8,10},{9,11},{10,... | collective-permute-start | bytes 1572872 | tf_op jit(solution)/shard_map/ppermute | solution.py:26
  11.3 2.2 %collective-permute-start.3 = (bf16[128,2048]{1,0:T(8,128)(2,1)S(1)}, bf16[128,2048]{1,0:T(8,128)(2,1)S(1)}, u32[]{:S(2)}, u32[]{:S(2)}) collective-permute-start(bf16[128,2048]{1,0:T(8,128)(2,1)S(1)} %get-tuple-element.33), channel_id=1, source_target_pairs={{0,3},{1,0},{2,1},{3,2},{4,7},{5,4},{6,5},{7,6},{8,11},{9,8},{10,9... | collective-permute-start | bytes 1572872 | tf_op jit(solution)/shard_map/ppermute | solution.py:26
  13.4 1.8 %copy-done.1 = bf16[4096,344]{0,1:T(8,128)(2,1)S(1)} copy-done((bf16[4096,344]{0,1:T(8,128)(2,1)S(1)}, bf16[4096,344]{0,1:T(8,128)(2,1)}, u32[]{:S(2)}) %copy-start.1) | copy-done | bytes 2818072
  15.2 1.2 %copy-done.3 = bf16[128,4096]{1,0:T(8,128)(2,1)S(1)} copy-done((bf16[128,4096]{1,0:T(8,128)(2,1)S(1)}, bf16[128,4096]{1,0:T(8,128)(2,1)}, u32[]{:S(2)}) %copy-start.3) | copy-done | bytes 1048600
  16.4 1.2 %copy-done.5 = bf16[128,4096]{1,0:T(8,128)(2,1)S(1)} copy-done((bf16[128,4096]{1,0:T(8,128)(2,1)S(1)}, bf16[128,4096]{1,0:T(8,128)(2,1)}, u32[]{:S(2)}) %copy-start.5) | copy-done | bytes 1048600
  17.7 1.8 %copy-done.7 = bf16[344,4096]{1,0:T(8,128)(2,1)S(1)} copy-done((bf16[344,4096]{1,0:T(8,128)(2,1)S(1)}, bf16[344,4096]{1,0:T(8,128)(2,1)}, u32[]{:S(2)}) %copy-start.7) | copy-done | bytes 2818072
  19.5 2.4 %own_units.1 = (bf16[528,128]{1,0:T(8,128)(2,1)S(1)}, bf16[504,128]{1,0:T(8,128)(2,1)S(1)}) custom-call(bf16[128,4096]{1,0:T(8,128)(2,1)S(1)} %copy-done.3, bf16[128,4096]{1,0:T(8,128)(2,1)S(1)} %copy-done.5, bf16[344,4096]{1,0:T(8,128)(2,1)S(1)} %bitcast.4, bf16[344,4096]{1,0:T(8,128)(2,1)S(1)} %bitcast.8, bf16[344,4096]{1,0:T(8,128)(2,1)S(1)} %copy-done.7), custom_call_target="tpu_custom_call" | custom-call | flops 20000000000 | bytes 70000000 | tf_op jit(solution)/shard_map/own_units/pallas_call | solution.py:77
  21.9 1.3 %row_term.2 = f32[128,4096]{1,0:T(8,128)S(1)} custom-call(bf16[528,128]{1,0:T(8,128)(2,1)S(1)} %get-tuple-element.27.first.own_first, bf16[504,128]{1,0:T(8,128)(2,1)S(1)} %get-tuple-element.28.second.own_second, bf16[344,4096]{1,0:T(8,128)(2,1)S(1)} %bitcast.5, bf16[344,4096]{1,0:T(8,128)(2,1)S(1)} %bitcast.9), custom_call_target="tpu_custom_call" | custom-call | flops 3000000000 | bytes 10500000 | tf_op jit(solution)/shard_map/row_term/pallas_call | solution.py:145
  23.2 1.6 %gate_up.1 = (f32[344,128]{1,0:T(8,128)S(1)}, f32[344,128]{1,0:T(8,128)S(1)}) custom-call(bf16[128,4096]{1,0:T(8,128)(2,1)S(1)} %collective-permute-done.x, bf16[344,4096]{1,0:T(8,128)(2,1)S(1)} %bitcast.6, bf16[344,4096]{1,0:T(8,128)(2,1)S(1)} %bitcast.10), custom_call_target="tpu_custom_call" | custom-call | flops 2000000000 | bytes 7000000 | tf_op jit(solution)/shard_map/gate_up/pallas_call | solution.py:94
  24.9 6.0 %collective-permute-done.4.c = bf16[128,4096]{1,0:T(8,128)(2,1)S(1)} collective-permute-done((bf16[128,4096]{1,0:T(8,128)(2,1)}, bf16[128,4096]{1,0:T(8,128)(2,1)S(1)}, u32[]{:S(2)}, u32[]{:S(2)}) %collective-permute-start.4) | collective-permute-done | bytes 1048608 | tf_op jit(solution)/shard_map/ppermute | solution.py:18
  30.9 1.0 %far_units.1 = (bf16[528,256]{1,0:T(8,128)(2,1)S(1)}, bf16[504,256]{1,0:T(8,128)(2,1)S(1)}, bf16[1032,256]{1,0:T(8,128)(2,1)S(1)}) custom-call(bf16[128,4096]{1,0:T(8,128)(2,1)S(1)} %collective-permute-done.4.c, bf16[344,4096]{1,0:T(8,128)(2,1)S(1)} %copy-done.8, f32[344,128]{1,0:T(8,128)S(1)} %get-tuple-element.36.gate, ...), custom_call_target="tpu_custom_call" | custom-call | flops 1500000000 | bytes 5250000 | tf_op jit(solution)/shard_map/far_units/pallas_call | solution.py:117
  31.9 0.8 %copy-done.2 = bf16[4096,344]{0,1:T(8,128)(2,1)S(1)} copy-done((bf16[4096,344]{0,1:T(8,128)(2,1)S(1)}, bf16[4096,344]{0,1:T(8,128)(2,1)}, u32[]{:S(2)}) %copy-start.2) | copy-done | bytes 2818072
  32.7 1.3 %row_term.3 = bf16[128,4096]{1,0:T(8,128)(2,1)S(1)} custom-call(bf16[528,256]{1,0:T(8,128)(2,1)S(1)} %get-tuple-element.38.first.refs_6_, bf16[504,256]{1,0:T(8,128)(2,1)S(1)} %get-tuple-element.39.second.refs_6_, bf16[344,4096]{1,0:T(8,128)(2,1)S(1)} %bitcast.7, bf16[344,4096]{1,0:T(8,128)(2,1)S(1)} %bitcast.11), custom_call_target="tpu_custom_call" | custom-call | flops 1000000000 | bytes 3500000 | tf_op jit(solution)/shard_map/row_term/pallas_call | solution.py:145
  34.2 4.0 %collective-permute-start.10 = (bf16[384,1024]{1,0:T(8,128)(2,1)S(1)}, bf16[384,1024]{1,0:T(8,128)(2,1)S(1)}, u32[]{:S(2)}, u32[]{:S(2)}) collective-permute-start(bf16[384,1024]{1,0:T(8,128)(2,1)S(1)} %pad_maximum_fusion.1), channel_id=1, source_target_pairs={{0,248},{8,0},{16,8},{24,16},{32,24},{40,32},{48,40},{56,48},{64,5... | collective-permute-start | bytes 2359304 | tf_op jit(solution)/shard_map/ppermute | solution.py:18
  38.2 1.5 %collective-permute-start.7 = (bf16[528,256]{1,0:T(8,128)(2,1)S(1)}, bf16[528,256]{1,0:T(8,128)(2,1)S(1)}, u32[]{:S(2)}, u32[]{:S(2)}) collective-permute-start(bf16[528,256]{1,0:T(8,128)(2,1)S(1)} %get-tuple-element.38.first.refs_6_), channel_id=1, source_target_pairs={{0,1},{1,2},{2,3},{3,0},{4,5},{5,6},{6,7},{7,4},{8,9},{9,10},{10,1... | collective-permute-start | bytes 811016 | tf_op jit(solution)/shard_map/ppermute | solution.py:26
  40.3 3.6 %collective-permute-start.6 = (bf16[384,1024]{1,0:T(8,128)(2,1)S(1)}, bf16[384,1024]{1,0:T(8,128)(2,1)S(1)}, u32[]{:S(2)}, u32[]{:S(2)}) collective-permute-start(bf16[384,1024]{1,0:T(8,128)(2,1)S(1)} %pad_maximum_fusion), channel_id=1, source_target_pairs={{0,248},{8,0},{16,8},{24,16},{32,24},{40,32},{48,40},{56,48},{64,5... | collective-permute-start | bytes 2359304 | tf_op jit(solution)/shard_map/ppermute | solution.py:18
  44.0 1.6 %collective-permute-done.7.refs_7_ = bf16[528,256]{1,0:T(8,128)(2,1)S(1)} collective-permute-done((bf16[528,256]{1,0:T(8,128)(2,1)S(1)}, bf16[528,256]{1,0:T(8,128)(2,1)S(1)}, u32[]{:S(2)}, u32[]{:S(2)}) %collective-permute-start.7) | collective-permute-done | bytes 270368 | tf_op jit(solution)/shard_map/ppermute | solution.py:26
  45.5 1.8 %collective-permute-start.8 = (bf16[528,256]{1,0:T(8,128)(2,1)S(1)}, bf16[528,256]{1,0:T(8,128)(2,1)S(1)}, u32[]{:S(2)}, u32[]{:S(2)}) collective-permute-start(bf16[528,256]{1,0:T(8,128)(2,1)S(1)} %collective-permute-done.7.refs_7_), channel_id=1, source_target_pairs={{0,1},{1,2},{2,3},{3,0},{4,5},{5,6},{6,7},{7,4},{8,9},{9,10},{10,1... | collective-permute-start | bytes 811016 | tf_op jit(solution)/shard_map/ppermute | solution.py:26
  47.3 2.7 %collective-permute-done.9 = bf16[1032,256]{1,0:T(8,128)(2,1)S(1)} collective-permute-done((bf16[1032,256]{1,0:T(8,128)(2,1)S(1)}, bf16[1032,256]{1,0:T(8,128)(2,1)S(1)}, u32[]{:S(2)}, u32[]{:S(2)}) %collective-permute-start.9) | collective-permute-done | bytes 528416 | tf_op jit(solution)/shard_map/ppermute | solution.py:26
  50.0 1.2 %collective-permute-start.12 = (bf16[504,256]{1,0:T(8,128)(2,1)S(1)}, bf16[504,256]{1,0:T(8,128)(2,1)S(1)}, u32[]{:S(2)}, u32[]{:S(2)}) collective-permute-start(bf16[504,256]{1,0:T(8,128)(2,1)S(1)} %get-tuple-element.39.second.refs_6_), channel_id=1, source_target_pairs={{0,1},{1,2},{2,3},{3,0},{4,5},{5,6},{6,7},{7,4},{8,9},{9,10},{10,1... | collective-permute-start | bytes 774152 | tf_op jit(solution)/shard_map/ppermute | solution.py:26
  51.2 2.5 %collective-permute-done.8.refs_8_ = bf16[528,256]{1,0:T(8,128)(2,1)S(1)} collective-permute-done((bf16[528,256]{1,0:T(8,128)(2,1)S(1)}, bf16[528,256]{1,0:T(8,128)(2,1)S(1)}, u32[]{:S(2)}, u32[]{:S(2)}) %collective-permute-start.8) | collective-permute-done | bytes 270368 | tf_op jit(solution)/shard_map/ppermute | solution.py:26
  53.6 1.7 %collective-permute-start.13 = (bf16[504,256]{1,0:T(8,128)(2,1)S(1)}, bf16[504,256]{1,0:T(8,128)(2,1)S(1)}, u32[]{:S(2)}, u32[]{:S(2)}) collective-permute-start(bf16[504,256]{1,0:T(8,128)(2,1)S(1)} %slice.34.refs_9_), channel_id=1, source_target_pairs={{0,3},{1,0},{2,1},{3,2},{4,7},{5,4},{6,5},{7,6},{8,11},{9,8},{10,9... | collective-permute-start | bytes 774152 | tf_op jit(solution)/shard_map/ppermute | solution.py:26
  56.4 3.0 %collective-permute-start.11 = (bf16[528,512]{1,0:T(8,128)(2,1)S(1)}, bf16[528,512]{1,0:T(8,128)(2,1)S(1)}, u32[]{:S(2)}, u32[]{:S(2)}) collective-permute-start(bf16[528,512]{1,0:T(8,128)(2,1)S(1)} %weight_terms.5), channel_id=1, source_target_pairs={{0,4},{1,5},{2,6},{3,7},{4,0},{5,1},{6,2},{7,3},{8,12},{9,13},{10,... | collective-permute-start | bytes 1622024 | tf_op jit(solution)/shard_map/ppermute | solution.py:26
  60.7 3.0 %collective-permute-start.14 = (bf16[504,512]{1,0:T(8,128)(2,1)S(1)}, bf16[504,512]{1,0:T(8,128)(2,1)S(1)}, u32[]{:S(2)}, u32[]{:S(2)}) collective-permute-start(bf16[504,512]{1,0:T(8,128)(2,1)S(1)} %weight_terms.7), channel_id=1, source_target_pairs={{0,4},{1,5},{2,6},{3,7},{4,0},{5,1},{6,2},{7,3},{8,12},{9,13},{10,... | collective-permute-start | bytes 1548296 | tf_op jit(solution)/shard_map/ppermute | solution.py:26
  63.7 0.7 weight_terms.4.first
  65.2 1.2 %add_convert_fusion = bf16[128,4096]{1,0:T(8,128)(2,1)} fusion(f32[128,4096]{1,0:T(8,128)S(1)} %row_term.2, bf16[128,4096]{1,0:T(8,128)(2,1)S(1)} %collective-permute-done.5), kind=kLoop, calls=%fused_computation | loop fusion | flops 1572864 | bytes 4194304 | tf_op jit(solution)/shard_map/convert_element_type | solution.py:290
  66.4 6.8 %collective-permute-done.11.other = bf16[528,512]{1,0:T(8,128)(2,1)S(1)} collective-permute-done((bf16[528,512]{1,0:T(8,128)(2,1)S(1)}, bf16[528,512]{1,0:T(8,128)(2,1)S(1)}, u32[]{:S(2)}, u32[]{:S(2)}) %collective-permute-start.11) | collective-permute-done | bytes 540704 | tf_op jit(solution)/shard_map/ppermute | solution.py:26
  73.3 7.0 %collective-permute-done.14.second_other = bf16[504,512]{1,0:T(8,128)(2,1)S(1)} collective-permute-done((bf16[504,512]{1,0:T(8,128)(2,1)S(1)}, bf16[504,512]{1,0:T(8,128)(2,1)S(1)}, u32[]{:S(2)}, u32[]{:S(2)}) %collective-permute-start.14) | collective-permute-done | bytes 516128 | tf_op jit(solution)/shard_map/ppermute | solution.py:26
  80.3 1.1 %sums.1 = (bf16[344,512]{1,0:T(8,128)(2,1)}, bf16[344,512]{1,0:T(8,128)(2,1)}, bf16[344,512]{1,0:T(8,128)(2,1)}) custom-call(bf16[528,512]{1,0:T(8,128)(2,1)S(1)} %early_sums.1.first, f32[504,512]{1,0:T(8,128)S(1)} %weight_terms.6.second, bf16[504,512]{1,0:T(8,128)(2,1)S(1)} %collective-permute-done.14.second_other), custom_call_target="tpu_custom_call" | custom-call | flops 1000000000 | bytes 3500000 | tf_op jit(solution)/shard_map/sums/pallas_call | solution.py:245
  (37 shorter events, 4.0 us)
Async XLA Ops:
  0.6 12.8 %copy-start = (bf16[4096,344]{0,1:T(8,128)(2,1)S(1)}, bf16[4096,344]{0,1:T(8,128)(2,1)}, u32[]{:S(2)}) copy-start(bf16[4096,344]{0,1:T(8,128)(2,1)} %param.7) | copy-start | bytes 8454148
  0.6 22.6 %collective-permute-start = (bf16[128,4096]{1,0:T(8,128)(2,1)}, bf16[128,4096]{1,0:T(8,128)(2,1)S(1)}, u32[]{:S(2)}, u32[]{:S(2)}) collective-permute-start(bf16[128,4096]{1,0:T(8,128)(2,1)} %x.5), channel_id=1, source_target_pairs={{0,248},{8,0},{16,8},{24,16},{32,24},{40,32},{48,40},{56,48},{64,5... | collective-permute-start | bytes 3145736 | tf_op jit(solution)/shard_map/ppermute | solution.py:18
  8.6 25.4 %collective-permute-start.1 = (bf16[128,2048]{1,0:T(8,128)(2,1)S(1)}, bf16[128,2048]{1,0:T(8,128)(2,1)S(1)}, u32[]{:S(2)}, u32[]{:S(2)}) collective-permute-start(bf16[128,2048]{1,0:T(8,128)(2,1)S(1)} %get-tuple-element.31), channel_id=1, source_target_pairs={{0,1},{1,2},{2,3},{3,0},{4,5},{5,6},{6,7},{7,4},{8,9},{9,10},{10,1... | collective-permute-start | bytes 1572872 | tf_op jit(solution)/shard_map/ppermute | solution.py:26
  10.1 23.8 %collective-permute-start.2 = (bf16[128,2048]{1,0:T(8,128)(2,1)S(1)}, bf16[128,2048]{1,0:T(8,128)(2,1)S(1)}, u32[]{:S(2)}, u32[]{:S(2)}) collective-permute-start(bf16[128,2048]{1,0:T(8,128)(2,1)S(1)} %get-tuple-element.32), channel_id=1, source_target_pairs={{0,2},{1,3},{2,0},{3,1},{4,6},{5,7},{6,4},{7,5},{8,10},{9,11},{10,... | collective-permute-start | bytes 1572872 | tf_op jit(solution)/shard_map/ppermute | solution.py:26
  11.3 22.7 %collective-permute-start.3 = (bf16[128,2048]{1,0:T(8,128)(2,1)S(1)}, bf16[128,2048]{1,0:T(8,128)(2,1)S(1)}, u32[]{:S(2)}, u32[]{:S(2)}) collective-permute-start(bf16[128,2048]{1,0:T(8,128)(2,1)S(1)} %get-tuple-element.33), channel_id=1, source_target_pairs={{0,3},{1,0},{2,1},{3,2},{4,7},{5,4},{6,5},{7,6},{8,11},{9,8},{10,9... | collective-permute-start | bytes 1572872 | tf_op jit(solution)/shard_map/ppermute | solution.py:26
  13.4 17.5 %collective-permute-start.4 = (bf16[128,4096]{1,0:T(8,128)(2,1)}, bf16[128,4096]{1,0:T(8,128)(2,1)S(1)}, u32[]{:S(2)}, u32[]{:S(2)}) collective-permute-start(bf16[128,4096]{1,0:T(8,128)(2,1)} %c.4), channel_id=1, source_target_pairs={{0,248},{8,0},{16,8},{24,16},{32,24},{40,32},{48,40},{56,48},{64,5... | collective-permute-start | bytes 3145736 | tf_op jit(solution)/shard_map/ppermute | solution.py:18
  13.4 1.8 %copy-start.1 = (bf16[4096,344]{0,1:T(8,128)(2,1)S(1)}, bf16[4096,344]{0,1:T(8,128)(2,1)}, u32[]{:S(2)}) copy-start(bf16[4096,344]{0,1:T(8,128)(2,1)} %param.8) | copy-start | bytes 8454148
  15.2 1.2 %copy-start.3 = (bf16[128,4096]{1,0:T(8,128)(2,1)S(1)}, bf16[128,4096]{1,0:T(8,128)(2,1)}, u32[]{:S(2)}) copy-start(bf16[128,4096]{1,0:T(8,128)(2,1)} %x.5) | copy-start | bytes 3145732
  16.4 1.2 %copy-start.5 = (bf16[128,4096]{1,0:T(8,128)(2,1)S(1)}, bf16[128,4096]{1,0:T(8,128)(2,1)}, u32[]{:S(2)}) copy-start(bf16[128,4096]{1,0:T(8,128)(2,1)} %c.4) | copy-start | bytes 3145732
  17.7 1.8 %copy-start.7 = (bf16[344,4096]{1,0:T(8,128)(2,1)S(1)}, bf16[344,4096]{1,0:T(8,128)(2,1)}, u32[]{:S(2)}) copy-start(bf16[344,4096]{1,0:T(8,128)(2,1)} %wd.3) | copy-start | bytes 8454148
  23.2 7.7 %copy-start.8 = (bf16[344,4096]{1,0:T(8,128)(2,1)S(1)}, bf16[344,4096]{1,0:T(8,128)(2,1)}, u32[]{:S(2)}) copy-start(bf16[344,4096]{1,0:T(8,128)(2,1)} %wd.3) | copy-start | bytes 8454148
  30.9 1.8 %copy-start.2 = (bf16[4096,344]{0,1:T(8,128)(2,1)S(1)}, bf16[4096,344]{0,1:T(8,128)(2,1)}, u32[]{:S(2)}) copy-start(bf16[4096,344]{0,1:T(8,128)(2,1)} %param.8) | copy-start | bytes 8454148
  34.1 21.2 %copy-start.4 = (bf16[128,4096]{1,0:T(8,128)(2,1)S(1)}, bf16[128,4096]{1,0:T(8,128)(2,1)}, u32[]{:S(2)}) copy-start(bf16[128,4096]{1,0:T(8,128)(2,1)} %x.5) | copy-start | bytes 3145732
  34.2 21.2 %copy-start.6 = (bf16[128,4096]{1,0:T(8,128)(2,1)S(1)}, bf16[128,4096]{1,0:T(8,128)(2,1)}, u32[]{:S(2)}) copy-start(bf16[128,4096]{1,0:T(8,128)(2,1)} %c.4) | copy-start | bytes 3145732
  34.2 21.4 %collective-permute-start.10 = (bf16[384,1024]{1,0:T(8,128)(2,1)S(1)}, bf16[384,1024]{1,0:T(8,128)(2,1)S(1)}, u32[]{:S(2)}, u32[]{:S(2)}) collective-permute-start(bf16[384,1024]{1,0:T(8,128)(2,1)S(1)} %pad_maximum_fusion.1), channel_id=1, source_target_pairs={{0,248},{8,0},{16,8},{24,16},{32,24},{40,32},{48,40},{56,48},{64,5... | collective-permute-start | bytes 2359304 | tf_op jit(solution)/shard_map/ppermute | solution.py:18
  38.2 7.3 %collective-permute-start.7 = (bf16[528,256]{1,0:T(8,128)(2,1)S(1)}, bf16[528,256]{1,0:T(8,128)(2,1)S(1)}, u32[]{:S(2)}, u32[]{:S(2)}) collective-permute-start(bf16[528,256]{1,0:T(8,128)(2,1)S(1)} %get-tuple-element.38.first.refs_6_), channel_id=1, source_target_pairs={{0,1},{1,2},{2,3},{3,0},{4,5},{5,6},{6,7},{7,4},{8,9},{9,10},{10,1... | collective-permute-start | bytes 811016 | tf_op jit(solution)/shard_map/ppermute | solution.py:26
  39.7 25.4 %collective-permute-start.5 = (bf16[128,4096]{1,0:T(8,128)(2,1)S(1)}, bf16[128,4096]{1,0:T(8,128)(2,1)S(1)}, u32[]{:S(2)}, u32[]{:S(2)}) collective-permute-start(bf16[128,4096]{1,0:T(8,128)(2,1)S(1)} %row_term.3), channel_id=1, source_target_pairs={{0,8},{8,16},{16,24},{24,32},{32,40},{40,48},{48,56},{56,64},{64,7... | collective-permute-start | bytes 3145736 | tf_op jit(solution)/shard_map/ppermute | solution.py:18
  39.7 10.3 %collective-permute-start.9 = (bf16[1032,256]{1,0:T(8,128)(2,1)S(1)}, bf16[1032,256]{1,0:T(8,128)(2,1)S(1)}, u32[]{:S(2)}, u32[]{:S(2)}) collective-permute-start(bf16[1032,256]{1,0:T(8,128)(2,1)S(1)} %get-tuple-element.46), channel_id=1, source_target_pairs={{0,3},{1,0},{2,1},{3,2},{4,7},{5,4},{6,5},{7,6},{8,11},{9,8},{10,9... | collective-permute-start | bytes 1585160 | tf_op jit(solution)/shard_map/ppermute | solution.py:26
  40.3 23.4 %collective-permute-start.6 = (bf16[384,1024]{1,0:T(8,128)(2,1)S(1)}, bf16[384,1024]{1,0:T(8,128)(2,1)S(1)}, u32[]{:S(2)}, u32[]{:S(2)}) collective-permute-start(bf16[384,1024]{1,0:T(8,128)(2,1)S(1)} %pad_maximum_fusion), channel_id=1, source_target_pairs={{0,248},{8,0},{16,8},{24,16},{32,24},{40,32},{48,40},{56,48},{64,5... | collective-permute-start | bytes 2359304 | tf_op jit(solution)/shard_map/ppermute | solution.py:18
  45.5 8.1 %collective-permute-start.8 = (bf16[528,256]{1,0:T(8,128)(2,1)S(1)}, bf16[528,256]{1,0:T(8,128)(2,1)S(1)}, u32[]{:S(2)}, u32[]{:S(2)}) collective-permute-start(bf16[528,256]{1,0:T(8,128)(2,1)S(1)} %collective-permute-done.7.refs_7_), channel_id=1, source_target_pairs={{0,1},{1,2},{2,3},{3,0},{4,5},{5,6},{6,7},{7,4},{8,9},{9,10},{10,1... | collective-permute-start | bytes 811016 | tf_op jit(solution)/shard_map/ppermute | solution.py:26
  50.0 9.4 %collective-permute-start.12 = (bf16[504,256]{1,0:T(8,128)(2,1)S(1)}, bf16[504,256]{1,0:T(8,128)(2,1)S(1)}, u32[]{:S(2)}, u32[]{:S(2)}) collective-permute-start(bf16[504,256]{1,0:T(8,128)(2,1)S(1)} %get-tuple-element.39.second.refs_6_), channel_id=1, source_target_pairs={{0,1},{1,2},{2,3},{3,0},{4,5},{5,6},{6,7},{7,4},{8,9},{9,10},{10,1... | collective-permute-start | bytes 774152 | tf_op jit(solution)/shard_map/ppermute | solution.py:26
  53.6 6.3 %collective-permute-start.13 = (bf16[504,256]{1,0:T(8,128)(2,1)S(1)}, bf16[504,256]{1,0:T(8,128)(2,1)S(1)}, u32[]{:S(2)}, u32[]{:S(2)}) collective-permute-start(bf16[504,256]{1,0:T(8,128)(2,1)S(1)} %slice.34.refs_9_), channel_id=1, source_target_pairs={{0,3},{1,0},{2,1},{3,2},{4,7},{5,4},{6,5},{7,6},{8,11},{9,8},{10,9... | collective-permute-start | bytes 774152 | tf_op jit(solution)/shard_map/ppermute | solution.py:26
  56.4 16.8 %collective-permute-start.11 = (bf16[528,512]{1,0:T(8,128)(2,1)S(1)}, bf16[528,512]{1,0:T(8,128)(2,1)S(1)}, u32[]{:S(2)}, u32[]{:S(2)}) collective-permute-start(bf16[528,512]{1,0:T(8,128)(2,1)S(1)} %weight_terms.5), channel_id=1, source_target_pairs={{0,4},{1,5},{2,6},{3,7},{4,0},{5,1},{6,2},{7,3},{8,12},{9,13},{10,... | collective-permute-start | bytes 1622024 | tf_op jit(solution)/shard_map/ppermute | solution.py:26
  60.7 19.6 %collective-permute-start.14 = (bf16[504,512]{1,0:T(8,128)(2,1)S(1)}, bf16[504,512]{1,0:T(8,128)(2,1)S(1)}, u32[]{:S(2)}, u32[]{:S(2)}) collective-permute-start(bf16[504,512]{1,0:T(8,128)(2,1)S(1)} %weight_terms.7), channel_id=1, source_target_pairs={{0,4},{1,5},{2,6},{3,7},{4,0},{5,1},{6,2},{7,3},{8,12},{9,13},{10,... | collective-permute-start | bytes 1548296 | tf_op jit(solution)/shard_map/ppermute | solution.py:26
